TPU v7x, 32 devices: a whole 2x2x4 slice. The times are simulated.
32 devices in a mesh: lat: 8 (over y, x, core), lon: 4 (over z).
Axes of the slice: x: 2, y: 2, z: 4, core: 2. Of those that a mesh axis runs over, the one named last changes fastest.
Arguments:
- fields_in: bfloat16 [4, 128, 256, 641], P(None, 'lat', 'lon'), may hold values from -6 to 6
- cotangent: bfloat16 [4, 128, 256, 641], P(None, 'lat', 'lon'), may hold values from -6 to 6
- member_dates: int32 [4], replicated, may hold values from 0 to 15
- date_table: float32 [16, 641], replicated, may hold values from -3 to 3
- norm_gains: float32 [2, 641], replicated, may hold values from 0.25 to 1.75
- spectral_filter: float32 [128, 641], replicated, may hold values from 0.5 to 2
- weight_in: float32 [641, 1282], replicated, may hold values from -0.25 to 0.25
- weight_out: float32 [1282, 641], replicated, may hold values from -0.15625 to 0.15625
- gain_moments: float32 [2, 641], replicated, may hold values from 13107.2 to 262144
- in_row_stats: float32 [641], replicated, may hold values from 9175.04 to 144179.2
- in_column_stats: float32 [1282], replicated, may hold values from 9175.04 to 144179.2
- out_row_stats: float32 [1282], replicated, may hold values from 19660.8 to 314572.8
- out_column_stats: float32 [641], replicated, may hold values from 19660.8 to 314572.8
- filter_row_stats: float32 [128], replicated, may hold values from 131.072 to 6553.6
- filter_column_stats: float32 [641], replicated, may hold values from 131.072 to 6553.6
Outputs:
- block_output: bfloat16 [4, 128, 256, 641], P(None, 'lat', 'lon')
- input_grad: float32 [4, 128, 256, 641], P(None, 'lat', 'lon')
- grad_weight_in: float32 [641, 1282], replicated
- grad_weight_out: float32 [1282, 641], replicated
- grad_filter: float32 [128, 641], replicated
- grad_gains: float32 [2, 641], replicated
- new_weight_in: float32 [641, 1282], replicated
- new_weight_out: float32 [1282, 641], replicated
- new_filter: float32 [128, 641], replicated
- new_gains: float32 [2, 641], replicated
- new_in_row_stats: float32 [641], replicated
- new_in_column_stats: float32 [1282], replicated
- new_out_row_stats: float32 [1282], replicated
- new_out_column_stats: float32 [641], replicated
- new_filter_row_stats: float32 [128], replicated
- new_filter_column_stats: float32 [641], replicated
- new_gain_moments: float32 [2, 641], replicated
Inputs may be any that keep to these rules, and one draw needn't show every extreme that they name: `member_dates`: the date index of each member.
All inputs are finite; a program needn't handle non-finite values.
Results may differ from a plain program's by a relative error of at most 0.014.
Values may be sent and summed in bfloat16 or wider, within the bound.
No kernel may reach another device: no remote copies, remote signals or barrier semaphores. Data moves between devices by JAX's collectives and lax.ppermute only.
A program may use at most 384 MiB of HBM per device.

v0:
```python
import math

import jax
import jax.numpy as jnp
from jax import lax
from jax.sharding import PartitionSpec as P

NLAT = 128
NLON = 256
L = 128
M = 96
STEP = 3


HIGHEST = lax.Precision.HIGHEST
TABLE_PRECISION = lax.Precision.HIGH
NORM_EPS = 1e-06
FIRST_EPS = 1e-30
SECOND_EPS = 0.001
CLIP_LEVEL = 0.5
STEP_RATE = 0.5


def legendre_table():
    angles = (jnp.arange(NLAT, dtype=jnp.float32) + 0.5) * (math.pi / NLAT)
    cosine = jnp.cos(angles)
    sine_lat = jnp.sin(angles)
    orders = jnp.arange(M, dtype=jnp.float32)[:, None]
    factors = jnp.arange(1, M, dtype=jnp.float32)
    growth = jnp.concatenate(
        [
            jnp.zeros((1,), jnp.float32),
            jnp.cumsum(0.5 * jnp.log((2.0 * factors + 1.0) / (2.0 * factors))),
        ]
    )
    diagonal = jnp.exp(0.5 * math.log(0.5) + growth[:, None] + orders * jnp.log(sine_lat)[None, :])

    def advance(state_pair, degree):
        latest, earlier = state_pair
        degree_f = degree.astype(jnp.float32)
        previous = degree_f - 1.0
        first_coef = jnp.sqrt(
            (4.0 * degree_f * degree_f - 1.0)
            / jnp.maximum(degree_f * degree_f - orders * orders, 1.0)
        )
        second_coef = jnp.sqrt(
            jnp.maximum(previous * previous - orders * orders, 0.0)
            / jnp.maximum(4.0 * previous * previous - 1.0, 1.0)
        )
        general = first_coef * (cosine[None, :] * latest - second_coef * earlier)
        values = jnp.where(degree_f < orders, 0.0, jnp.where(degree_f == orders, diagonal, general))
        return ((values, latest), values)

    zeroes = jnp.zeros((M, NLAT), jnp.float32)
    _, stacked = lax.scan(advance, (zeroes, zeroes), jnp.arange(L, dtype=jnp.int32))
    return (jnp.transpose(stacked, (1, 0, 2)), math.pi / NLAT * sine_lat)


def dft_tables():
    points = jnp.arange(NLON, dtype=jnp.int32)[:, None]
    orders = jnp.arange(M, dtype=jnp.int32)[None, :]
    phases = (points * orders % NLON).astype(jnp.float32) * (2.0 * math.pi / NLON)
    cosine = jnp.cos(phases)
    sine_part = jnp.sin(phases)
    forward = jnp.stack([cosine, -sine_part], axis=2).reshape(NLON, 2 * M) / NLON
    doubling = jnp.where(orders == 0, 1.0, 2.0).astype(jnp.float32)
    inverse = jnp.transpose(
        jnp.stack([doubling * cosine, -doubling * sine_part], axis=2).reshape(NLON, 2 * M)
    )
    return (forward, inverse)


def rms_norm(values, scaling):
    return (
        values * lax.rsqrt(jnp.mean(values * values, axis=-1, keepdims=True) + NORM_EPS) * scaling
    )


def exact_gelu(values):
    return jax.nn.gelu(values, approximate=False)


def adafactor_matrix(weight_now, gradient, rows_old, columns_old, decay_rate):
    squares = gradient * gradient + FIRST_EPS
    rows_new = decay_rate * rows_old + (1.0 - decay_rate) * jnp.mean(squares, axis=1)
    columns_new = decay_rate * columns_old + (1.0 - decay_rate) * jnp.mean(squares, axis=0)
    estimate = rows_new[:, None] * columns_new[None, :] / jnp.mean(rows_new)
    update = gradient * lax.rsqrt(estimate)
    update = update / jnp.maximum(1.0, jnp.sqrt(jnp.mean(update * update)) / CLIP_LEVEL)
    scale_now = STEP_RATE * jnp.maximum(SECOND_EPS, jnp.sqrt(jnp.mean(weight_now * weight_now)))
    return (weight_now - scale_now * update, rows_new, columns_new)


def adafactor_vector(weight_now, gradient, moments_old, decay_rate):
    moments_new = decay_rate * moments_old + (1.0 - decay_rate) * (gradient * gradient + FIRST_EPS)
    update = gradient * lax.rsqrt(moments_new)
    update = update / jnp.maximum(
        1.0, jnp.sqrt(jnp.mean(update * update, axis=1, keepdims=True)) / CLIP_LEVEL
    )
    scale_now = STEP_RATE * jnp.maximum(
        SECOND_EPS, jnp.sqrt(jnp.mean(weight_now * weight_now, axis=1, keepdims=True))
    )
    return (weight_now - scale_now * update, moments_new)


def body(
    fields_in,
    cotangent,
    member_dates,
    date_table,
    norm_gains,
    spectral_filter,
    weight_in,
    weight_out,
    gain_moments,
    in_row_stats,
    in_column_stats,
    out_row_stats,
    out_column_stats,
    filter_row_stats,
    filter_column_stats,
):
    legendre, quadrature = legendre_table()
    forward, inverse = dft_tables()
    lat_index = lax.axis_index("lat")
    lat_count = lax.axis_size("lat")
    lat_rows = fields_in.shape[1]
    row_start = lat_index * lat_rows
    date_selector = (
        member_dates[:, None] == jnp.arange(date_table.shape[0], dtype=jnp.int32)[None, :]
    ).astype(jnp.float32)
    offsets = jnp.dot(date_selector, date_table, precision=HIGHEST)[:, None, None, :]
    shifted = fields_in.astype(jnp.float32) + offsets
    normed, first_pull = jax.vjp(rms_norm, shifted, norm_gains[0])
    whole_lon = lax.all_to_all(
        normed.astype(jnp.bfloat16), "lon", split_axis=0, concat_axis=2, tiled=True
    )
    spectra = jnp.einsum(
        "bjkc,kq->bqjc", whole_lon.astype(jnp.float32), forward, precision=TABLE_PRECISION
    ).astype(jnp.bfloat16)
    channels = spectra.shape[3]
    degree_share = L // lat_count
    degree_start = lat_index * degree_share
    paired = lax.dynamic_slice_in_dim(jnp.repeat(legendre, 2, axis=0), row_start, lat_rows, 2)
    weighted = paired * lax.dynamic_slice_in_dim(quadrature, row_start, lat_rows, 0)
    spectra_wide = spectra.astype(jnp.float32)
    portion = weighted
    coefficients = lax.psum_scatter(
        jnp.einsum("qlj,bqjc->lbqc", portion, spectra_wide, precision=TABLE_PRECISION),
        "lat",
        scatter_dimension=0,
        tiled=True,
    )
    response = lax.dynamic_slice_in_dim(spectral_filter, degree_start, degree_share, 0)
    filtered = (response[:, None, None, :] * coefficients).astype(jnp.bfloat16)
    degrees_used = paired
    synthesis = jnp.einsum(
        "qlj,lbqc->bqjc",
        degrees_used,
        lax.all_gather(filtered, "lat", axis=0, tiled=True).astype(jnp.float32),
        precision=TABLE_PRECISION,
    ).astype(jnp.bfloat16)
    lon_fields = jnp.einsum(
        "bqjc,qk->bjkc", synthesis.astype(jnp.float32), inverse, precision=TABLE_PRECISION
    ).astype(jnp.bfloat16)
    branch = lax.all_to_all(lon_fields, "lon", split_axis=2, concat_axis=0, tiled=True)
    hidden_state = shifted + branch.astype(jnp.float32)
    second_normed, second_pull = jax.vjp(rms_norm, hidden_state, norm_gains[1])
    second_low = second_normed.astype(jnp.bfloat16)
    inner_low = weight_in.astype(jnp.bfloat16)
    outer_low = weight_out.astype(jnp.bfloat16)
    preact = jnp.einsum("bjkc,ch->bjkh", second_low, inner_low, preferred_element_type=jnp.float32)
    activation, gelu_pull = jax.vjp(exact_gelu, preact)
    active_low = activation.astype(jnp.bfloat16)
    block_output = (
        hidden_state
        + jnp.einsum("bjkh,hc->bjkc", active_low, outer_low, preferred_element_type=jnp.float32)
    ).astype(jnp.bfloat16)
    grad_out_part = jnp.einsum(
        "bjkh,bjkc->hc", active_low, cotangent, preferred_element_type=jnp.float32
    )
    back_active = jnp.einsum(
        "bjkc,hc->bjkh", cotangent, outer_low, preferred_element_type=jnp.float32
    )
    back_preact = gelu_pull(back_active)[0].astype(jnp.bfloat16)
    grad_in_part = jnp.einsum(
        "bjkc,bjkh->ch", second_low, back_preact, preferred_element_type=jnp.float32
    )
    back_second = jnp.einsum(
        "bjkh,ch->bjkc", back_preact, inner_low, preferred_element_type=jnp.float32
    )
    back_hidden, gain_two_part = second_pull(back_second)
    back_hidden = back_hidden + cotangent.astype(jnp.float32)
    back_branch = lax.all_to_all(
        back_hidden.astype(jnp.bfloat16), "lon", split_axis=0, concat_axis=2, tiled=True
    )
    back_synthesis = jnp.einsum(
        "bjkc,qk->bqjc", back_branch.astype(jnp.float32), inverse, precision=TABLE_PRECISION
    ).astype(jnp.bfloat16)
    back_wide = back_synthesis.astype(jnp.float32)
    portion = paired
    back_filtered = lax.psum_scatter(
        jnp.einsum("qlj,bqjc->lbqc", portion, back_wide, precision=TABLE_PRECISION),
        "lat",
        scatter_dimension=0,
        tiled=True,
    )
    filter_share = jnp.sum(coefficients * back_filtered, axis=(1, 2))
    filter_part = lax.dynamic_update_slice_in_dim(
        jnp.zeros((L, channels), jnp.float32), filter_share, degree_start, 0
    )
    back_coefficients = (response[:, None, None, :] * back_filtered).astype(jnp.bfloat16)
    degrees_used = weighted
    back_spectra = jnp.einsum(
        "qlj,lbqc->bqjc",
        degrees_used,
        lax.all_gather(back_coefficients, "lat", axis=0, tiled=True).astype(jnp.float32),
        precision=TABLE_PRECISION,
    ).astype(jnp.bfloat16)
    back_lon = jnp.einsum(
        "bqjc,kq->bjkc", back_spectra.astype(jnp.float32), forward, precision=TABLE_PRECISION
    ).astype(jnp.bfloat16)
    back_normed = lax.all_to_all(back_lon, "lon", split_axis=2, concat_axis=0, tiled=True)
    back_shifted, gain_one_part = first_pull(back_normed.astype(jnp.float32))
    input_grad = back_hidden + back_shifted
    grad_weight_in, grad_weight_out, grad_filter, grad_gains = lax.psum(
        (grad_in_part, grad_out_part, filter_part, jnp.stack([gain_one_part, gain_two_part])),
        ("lat", "lon"),
    )
    decay_rate = 1.0 - STEP ** (-0.8)
    new_weight_in, new_in_rows, new_in_columns = adafactor_matrix(
        weight_in, grad_weight_in, in_row_stats, in_column_stats, decay_rate
    )
    new_weight_out, new_out_rows, new_out_columns = adafactor_matrix(
        weight_out, grad_weight_out, out_row_stats, out_column_stats, decay_rate
    )
    new_filter, new_filter_rows, new_filter_columns = adafactor_matrix(
        spectral_filter, grad_filter, filter_row_stats, filter_column_stats, decay_rate
    )
    new_gains, new_moments = adafactor_vector(norm_gains, grad_gains, gain_moments, decay_rate)
    return (
        block_output,
        input_grad,
        grad_weight_in,
        grad_weight_out,
        grad_filter,
        grad_gains,
        new_weight_in,
        new_weight_out,
        new_filter,
        new_gains,
        new_in_rows,
        new_in_columns,
        new_out_rows,
        new_out_columns,
        new_filter_rows,
        new_filter_columns,
        new_moments,
    )


def solution(mesh):
    return jax.shard_map(
        body,
        mesh=mesh,
        in_specs=(
            P(None, "lat", "lon", None),
            P(None, "lat", "lon", None),
            P(),
            P(),
            P(),
            P(),
            P(),
            P(),
            P(),
            P(),
            P(),
            P(),
            P(),
            P(),
            P(),
        ),
        out_specs=(
            P(None, "lat", "lon", None),
            P(None, "lat", "lon", None),
            P(),
            P(),
            P(),
            P(),
            P(),
            P(),
            P(),
            P(),
            P(),
            P(),
            P(),
            P(),
            P(),
            P(),
            P(),
        ),
        check_vma=False,
    )
```

profile of v0, /device:TPU:0, one launch (start us, length us, event | category | flops | bytes accessed | tf_op | source)
XLA Modules:
  0.0 2700.9 jit_solution(17391899244415455512)
XLA Ops:
  14.7 7.4 multiply_convert_fusion.2
  29.1 268.0 %while.19 = (s32[]{:T(128)}, f32[96,128]{1,0:T(8,128)S(1)}, f32[96,128]{1,0:T(8,128)S(1)}, f32[128,96,128]{2,1,0:T(8,128)}, s32[128]{0:T(128)S(1)}, /*index=5*/f...) while((s32[]{:T(128)}, f32[96,128]{1,0:T(8,128)S(1)}, ...), condition=%wide.region_3.4_spmd.clone.clone, body=%wide.region_2.3_spmd.clone.clone.sunk | while | flops 111726 | bytes 249899 | solution.py:55
  317.6 39.5 %convolution_bitcast_fusion.1 = f32[128,1,192,641]{0,3,2,1:T(8,128)} fusion(bf16[192,16,641]{2,0,1:T(8,128)(2,1)S(1)} %convolution_convert_fusion.1, f32[192,128,128]{1,2,0:T(8,128)} %bitcast.135, s32[]{:T(128)S(6)} %select_n.70, f32[16]{0:T(128)S(1)} %dynamic_slice.19), kind=kOutput, calls=%fused_computation.28 | convolution fusion | flops 1512701952 | bytes 68524096 | tf_op jit(solution)/shard_map/qlj,bqjc->lbqc/dot_general | solution.py:149
  357.1 74.2 %copy.114 = f32[128,1,192,641]{3,2,1,0:T(8,128)} copy(f32[128,1,192,641]{0,3,2,1:T(8,128)} %convolution_bitcast_fusion.1) | data formatting | bytes 126025728 | tf_op jit(solution)/shard_map/qlj,bqjc->lbqc/transpose | solution.py:149
  432.5 424.5 %reduce-scatter.3.cloned.1.call-done = f32[16,1,192,641]{3,2,1,0:T(8,128)} async-done(((f32[128,1,192,641]{3,2,1,0:T(8,128)}), f32[16,1,192,641]{3,2,1,0:T(8,128)}) %reduce-scatter.3.cloned.1.call-update) | async-done | bytes 7876624 | tf_op jit(solution)/shard_map/reduce_scatter | solution.py:148
  865.6 178.0 %all-gather.3.cloned.1.call-done = bf16[128,1,192,641]{3,2,1,0:T(8,128)(2,1)} async-done(((bf16[16,1,192,641]{3,2,1,0:T(8,128)(2,1)}), bf16[128,1,192,641]{3,2,1,0:T(8,128)(2,1)}) %all-gather.3.cloned.1.call-update) | async-done | bytes 31506448 | tf_op jit(solution)/shard_map/all_gather | solution.py:160
  1043.7 46.3 %copy.115 = bf16[128,1,192,641]{0,3,2,1:T(8,128)(2,1)} copy(bf16[128,1,192,641]{3,2,1,0:T(8,128)(2,1)} %all-gather.3.cloned.1.call-done) | data formatting | bytes 63012864 | tf_op jit(solution)/shard_map/all_gather | solution.py:160
  1090.0 26.0 convert_bitcast_fusion.3
  1116.0 9.4 convert_bitcast_fusion.1
  1125.5 9.0 copy.117
  1134.4 145.9 %all_to_all.48 = bf16[1,16,256,641]{3,1,0,2:T(8,128)(2,1)} all-to-all(bf16[1,16,256,641]{3,1,0,2:T(8,128)(2,1)} %copy.117), channel_id=1, replica_groups=mesh['lat'=8,'lon'=4] {'lon'}, dimensions={2} | all-to-all | bytes 10502144 | tf_op jit(solution)/shard_map/all_to_all | solution.py:166
  1291.1 23.6 fusion.34
  1314.7 54.1 %multiply_convert_fusion = (bf16[4,16,64,1282]{3,2,1,0:T(8,128)(2,1)}, f32[4,16,64,1282]{3,2,1,0:T(8,128)}) fusion(f32[4,16,64,1282]{3,2,1,0:T(8,128)} %get-tuple-element.270, u16[4,64,1282]{2,1,0:T(8,128)(2,1)S(1)} %get-tuple-element.221, u16[4,64,1282]{2,1,0:T(8,128)(2,1)S(1)} %get-tuple-element.220), kind=kLoop, calls=%fused_computation.36 | loop fusion | flops 367575040 | bytes 53823488 | tf_op jit(solution)/shard_map/convert_element_type | solution.py:174
  1368.9 29.2 %add_convert_fusion = bf16[4,16,64,1282]{3,2,1,0:T(8,128)(2,1)} fusion(f32[4,16,64,1282]{3,2,1,0:T(8,128)} %get-tuple-element.261, bf16[4,16,64,641]{3,2,1,0:T(8,128)(2,1)} %param.18, f32[4,16,64,1282]{3,2,1,0:T(8,128)} %get-tuple-element.270, f32[1282,641]{0,1:T(8,128)S(1)} %copy-done.5), kind=kOutput, calls=%fused_computation.35 | convolution fusion | flops 6806211072 | bytes 61048840 | tf_op jit(solution)/shard_map/bjkc,hc->bjkh/dot_general | solution.py:182
  1398.0 20.0 multiply_reduce_fusion
  1418.0 11.1 fusion.94
  1429.2 141.0 %all_to_all.49 = bf16[4,16,64,641]{3,2,1,0:T(8,128)(2,1)S(1)} all-to-all(bf16[4,16,64,641]{3,2,1,0:T(8,128)(2,1)S(1)} %fusion.94), channel_id=1, replica_groups=mesh['lat'=8,'lon'=4] {'lon'}, dimensions={0} | all-to-all | bytes 10502144 | tf_op jit(solution)/shard_map/all_to_all | solution.py:194
  1574.2 39.6 %convolution_bitcast_fusion = f32[128,1,192,641]{0,3,2,1:T(8,128)} fusion(bf16[192,16,641]{2,0,1:T(8,128)(2,1)S(1)} %convolution_convert_fusion, f32[192,128,128]{1,2,0:T(8,128)} %bitcast.137, s32[]{:T(128)S(6)} %select_n.70), kind=kOutput, calls=%fused_computation.27 | convolution fusion | flops 1512308736 | bytes 68524032 | tf_op jit(solution)/shard_map/qlj,bqjc->lbqc/dot_general | solution.py:203
  1613.7 74.2 %copy.123 = f32[128,1,192,641]{3,2,1,0:T(8,128)} copy(f32[128,1,192,641]{0,3,2,1:T(8,128)} %convolution_bitcast_fusion) | data formatting | bytes 126025728 | tf_op jit(solution)/shard_map/qlj,bqjc->lbqc/transpose | solution.py:203
  1688.0 422.0 %reduce-scatter.5.cloned.1.call-done = f32[16,1,192,641]{3,2,1,0:T(8,128)} async-done(((f32[128,1,192,641]{3,2,1,0:T(8,128)}), f32[16,1,192,641]{3,2,1,0:T(8,128)}) %reduce-scatter.5.cloned.1.call-update) | async-done | bytes 7876624 | tf_op jit(solution)/shard_map/reduce_scatter | solution.py:202
  2110.0 10.5 multiply_reduce_fusion.5
  2131.3 19.0 convolution_bitcast_fusion.3
  2150.3 12.7 convolution_bitcast_fusion.2
  2166.7 133.6 %all-gather.5.cloned.1.call-done = bf16[128,1,192,641]{3,2,1,0:T(8,128)(2,1)} async-done(((bf16[16,1,192,641]{3,2,1,0:T(8,128)(2,1)}), bf16[128,1,192,641]{3,2,1,0:T(8,128)(2,1)}) %all-gather.5.cloned.1.call-update) | async-done | bytes 31506448 | tf_op jit(solution)/shard_map/all_gather | solution.py:217
  2300.3 46.6 %copy.124 = bf16[128,1,192,641]{0,3,2,1:T(8,128)(2,1)} copy(bf16[128,1,192,641]{3,2,1,0:T(8,128)(2,1)} %all-gather.5.cloned.1.call-done) | data formatting | bytes 63012864 | tf_op jit(solution)/shard_map/all_gather | solution.py:217
  2346.9 26.9 convert_bitcast_fusion.2
  2373.8 9.5 convert_bitcast_fusion
  2383.4 9.0 copy.126
  2397.7 18.0 add_convert_fusion.1
  2415.7 169.8 %all-reduce.3.cloned.1.call-done = (f32[641,1282]{1,0:T(8,128)}, f32[1282,641]{0,1:T(8,128)}, f32[128,641]{0,1:T(8,128)}) async-done(((f32[641,1282]{1,0:T(8,128)}, f32[1282,641]{0,1:T(8,128)}, f32[128,641]{0,1:T(8,128)}), (f32[641,1282]{1,0:T(8,128)}, f32[1282,641]{0,1:T(8,128)}, f32[128,641]{0,1:T(8,128)})) %all-reduce.3.cloned.1.call-update) | async-done | bytes 6902304 | tf_op jit(solution)/shard_map/psum | solution.py:226
  2629.3 38.8 %psum.31 = f32[2,641]{1,0:T(2,128)S(1)} all-reduce(f32[2,641]{1,0:T(2,128)S(1)} %pad_maximum_fusion.1), channel_id=1, replica_groups=mesh['lat'=8,'lon'=4] {'lat','lon'}, use_global_device_ids=true, to_apply=%region_15.16 | all-reduce | flops 1282 | bytes 10256 | tf_op jit(solution)/shard_map/psum | solution.py:226
  2669.0 20.8 fusion.30
  (832 shorter events, 303.3 us)
Async XLA Ops:
  22.1 282.6 %all-to-all-start = ((bf16[4,16,64,641]{3,2,1,0:T(8,128)(2,1)}), bf16[4,16,64,641]{3,2,1,0:T(8,128)(2,1)}, u32[]{:S(2)}, u32[]{:S(2)}) async-start(bf16[4,16,64,641]{3,2,1,0:T(8,128)(2,1)} %multiply_convert_fusion.2), calls=%async_computation | async-start | bytes 12582912 | tf_op jit(solution)/shard_map/all_to_all | solution.py:135
  28.4 828.7 %reduce-scatter.3.cloned.1.call-start = ((), (), s32[]{:S(2)}) async-start(), calls=%async_computation.6 | async-start | bytes 84934656 | tf_op jit(solution)/shard_map/reduce_scatter | solution.py:148
  431.3 612.4 %all-gather.3.cloned.1.call-start = ((), (), s32[]{:S(2)}) async-start(), calls=%async_computation.7 | async-start | bytes 42467328 | tf_op jit(solution)/shard_map/all_gather | solution.py:160
  432.5 657.5 %copy-start.15 = (f32[16,641]{1,0:T(8,128)}, f32[16,641]{1,0:T(8,128)S(1)}, u32[]{:S(2)}) copy-start(f32[16,641]{1,0:T(8,128)S(1)} %copy.108) | copy-start | bytes 123076
  863.9 1246.1 %reduce-scatter.5.cloned.1.call-start = ((), (), s32[]{:S(2)}) async-start(), calls=%async_computation.8 | async-start | bytes 84934656 | tf_op jit(solution)/shard_map/reduce_scatter | solution.py:202
  1134.4 150.9 %slice-start = ((s8[6291456]{0:T(1024)(128)(4,1)}), s8[4194304]{0:T(1024)(128)(4,1)S(1)}, s32[]{:S(2)}) async-start(s8[6291456]{0:T(1024)(128)(4,1)} %bitcast.133), calls=%async_computation.11 | async-start | bytes 8388608
  1314.7 54.2 %copy-start.5 = (f32[1282,641]{0,1:T(8,128)S(1)}, f32[1282,641]{0,1:T(8,128)}, u32[]{:S(2)}) copy-start(f32[1282,641]{0,1:T(8,128)} %param.24) | copy-start | bytes 9861148
  1687.9 422.1 %copy-start.16 = (f32[16,641]{1,0:T(8,128)S(1)}, f32[16,641]{1,0:T(8,128)}, u32[]{:S(2)}) copy-start(f32[16,641]{1,0:T(8,128)} %copy-done.15) | copy-start | bytes 123076
  1688.0 441.8 %copy-start.9 = (f32[128,641]{0,1:T(8,128)S(1)}, f32[128,641]{0,1:T(8,128)}, u32[]{:S(2)}) copy-start(f32[128,641]{0,1:T(8,128)} %param.22) | copy-start | bytes 984580
  1688.0 443.1 %copy-start.28 = (f32[2,641]{1,0:T(2,128)S(1)}, f32[2,641]{1,0:T(2,128)}, u32[]{:S(2)}) copy-start(f32[2,641]{1,0:T(2,128)} %param.21) | copy-start | bytes 15388
  1688.0 612.3 %all-gather.5.cloned.1.call-start = ((), (), s32[]{:S(2)}) async-start(), calls=%async_computation.9 | async-start | bytes 42467328 | tf_op jit(solution)/shard_map/all_gather | solution.py:217
  2120.6 465.0 %all-reduce.3.cloned.1.call-start = ((), (), s32[]{:S(2)}) async-start(), calls=%async_computation.10 | async-start | bytes 15261696 | tf_op jit(solution)/shard_map/psum | solution.py:226
  2120.8 29.5 %slice-start.4 = ((s8[6291456]{0:T(1024)(128)(4,1)}), s8[2097152]{0:T(1024)(128)(4,1)S(1)}, s32[]{:S(2)}) async-start(s8[6291456]{0:T(1024)(128)(4,1)} %bitcast.144), calls=%async_computation.15 | async-start | bytes 4194304
  2166.7 180.3 %copy-start.36 = (f32[16]{0:T(128)S(1)}, f32[16]{0:T(128)}, u32[]{:S(2)}) copy-start(f32[16]{0:T(128)} %copy-done.35) | copy-start | bytes 196
  2346.9 26.9 copy-start.11
  2392.4 225.5 %all-to-all-start.3 = ((bf16[1,16,256,641]{3,1,0,2:T(8,128)(2,1)}), bf16[1,16,256,641]{3,1,0,2:T(8,128)(2,1)}, u32[]{:S(2)}, u32[]{:S(2)}) async-start(bf16[1,16,256,641]{3,1,0,2:T(8,128)(2,1)} %copy.126), calls=%async_computation.5 | async-start | bytes 12582912 | tf_op jit(solution)/shard_map/all_to_all | solution.py:223
  2397.7 189.1 %copy-start.44 = (f32[128]{0:T(128)S(1)}, f32[128]{0:T(128)}, u32[]{:S(2)}) copy-start(f32[128]{0:T(128)} %param.30) | copy-start | bytes 1540
  2397.7 190.4 %copy-start.41 = (f32[641]{0:T(1024)S(1)}, f32[641]{0:T(1024)}, u32[]{:S(2)}) copy-start(f32[641]{0:T(1024)} %param.31) | copy-start | bytes 7696
  2397.7 195.6 %copy-start.42 = (f32[641]{0:T(1024)S(1)}, f32[641]{0:T(1024)}, u32[]{:S(2)}) copy-start(f32[641]{0:T(1024)} %param.26) | copy-start | bytes 7696
  2397.7 196.8 %copy-start.37 = (f32[1282]{0:T(1024)S(1)}, f32[1282]{0:T(1024)}, u32[]{:S(2)}) copy-start(f32[1282]{0:T(1024)} %param.27) | copy-start | bytes 15388
  2397.7 204.1 %copy-start.38 = (f32[1282]{0:T(1024)S(1)}, f32[1282]{0:T(1024)}, u32[]{:S(2)}) copy-start(f32[1282]{0:T(1024)} %param.28) | copy-start | bytes 15388
  2397.7 205.4 %copy-start.43 = (f32[641]{0:T(1024)S(1)}, f32[641]{0:T(1024)}, u32[]{:S(2)}) copy-start(f32[641]{0:T(1024)} %param.29) | copy-start | bytes 7696
  2585.5 22.1 copy-start.7
  2587.4 27.6 %copy-start.40 = (f32[128]{0:T(128)}, f32[128]{0:T(128)S(1)}, u32[]{:S(2)}) copy-start(f32[128]{0:T(128)S(1)} %get-tuple-element.383) | copy-start | bytes 1540
  2588.1 27.0 copy-start.31
  2593.8 24.0 copy-start.32
  2594.5 23.4 copy-start.24
  2622.7 45.4 %copy-start.23 = (f32[4,16,64]{2,1,0:T(8,128)S(1)}, f32[4,16,64]{2,1,0:T(8,128)}, u32[]{:S(2)}) copy-start(f32[4,16,64]{2,1,0:T(8,128)} %copy-done.22) | copy-start | bytes 49156
  2622.8 45.4 %copy-start.39 = (f32[2,641]{1,0:T(2,128)S(1)}, f32[2,641]{1,0:T(2,128)}, u32[]{:S(2)}) copy-start(f32[2,641]{1,0:T(2,128)} %param.25) | copy-start | bytes 15388
  2622.8 46.2 %copy-start.21 = (f32[4,16,64]{2,1,0:T(8,128)S(1)}, f32[4,16,64]{2,1,0:T(8,128)}, u32[]{:S(2)}) copy-start(f32[4,16,64]{2,1,0:T(8,128)} %copy-done.20) | copy-start | bytes 49156
  2669.0 22.7 copy-start.2
  2669.0 25.2 copy-start.1
  (26 other events, 236.6 us)
Sparse Core Ops, SparseCore 0:
  431.4 425.5 reduce-scatter.2
  864.0 179.5 all-gather.2
  1688.1 421.9 reduce-scatter.4
  2120.7 179.5 all-gather.4
  2307.6 277.9 all-reduce.2
where the time goes:
time: 2710 us; the launch traced here: 2700 us
  waiting for transfers between devices  1330 us (49%)
  local copies, waits for them, and re-layouts  363 us (13%)
  blocking collectives  326 us (12%)
  other arithmetic  284 us (10%)
  matrix products  281 us (10%)
  loops' own time  86.1 us (3%)
    reduce_scatter x1, waiting for transfers between devices, body(): lax.psum_scatter(jnp.einsum('qlj,bqjc->lbqc', portion, spectra_wide, prec...  425 us
    reduce_scatter x1, waiting for transfers between devices, body(): lax.psum_scatter(jnp.einsum('qlj,bqjc->lbqc', portion, back_wide, precisi...  422 us
    all_gather x1, waiting for transfers between devices, body(): lax.all_gather(filtered, 'lat', axis=0, tiled=True).astype(jnp.float32)  178 us
    psum x1, waiting for transfers between devices, body(): lax.psum((grad_in_part, grad_out_part, filter_part, jnp.stack([gain_one_p...  170 us
    all_to_all x1, blocking collectives, body(): lax.all_to_all(lon_fields, 'lon', split_axis=2, concat_axis=0, tiled=True)  146 us
    all_to_all x1, blocking collectives, body(): lax.all_to_all(back_hidden.astype(jnp.bfloat16), 'lon', split_axis=0, con...  141 us
    all_gather x1, waiting for transfers between devices, body(): lax.all_gather(back_coefficients, 'lat', axis=0, tiled=True)  134 us
    dynamic_update_slice x128, other arithmetic, legendre_table(): lax.scan(advance, (zeroes, zeroes), jnp.arange(L, dtype=jnp.int32))  97.3 us
  transfers between devices with their start and end apart: 7, of which 5 were waited for; matrix products, arithmetic and copies ran while one was open for 14% of the time, Pallas kernels for 0%

commit v1 on v0

v1 whole, which is shorter than its diff:
```python
import math

import jax
import jax.numpy as jnp
import numpy as np
from jax import lax
from jax.experimental import pallas as pl
from jax.experimental.pallas import tpu as pltpu
from jax.sharding import PartitionSpec as P

NLAT = 128
NLON = 256
L = 128
M = 96
Q = 2 * M
STEP = 3
LANES = 128

NORM_EPS = 1e-06
FIRST_EPS = 1e-30
SECOND_EPS = 0.001
CLIP_LEVEL = 0.5
STEP_RATE = 0.5
F32 = jnp.float32
LOW = jnp.bfloat16
VMEM_LIMIT = 48 * 1024 * 1024


def legendre_table():
    angles = math.pi * (np.arange(NLAT) + 0.5) / NLAT
    cosine, sine = np.cos(angles), np.sin(angles)
    table = np.zeros((M, L, NLAT))
    for m in range(M):
        factors = np.arange(1, m + 1)
        scale = math.sqrt(0.5 * np.prod((2.0 * factors + 1.0) / (2.0 * factors)))
        table[m, m] = scale * sine**m
        for l in range(m + 1, L):
            a = math.sqrt((4.0 * l * l - 1.0) / (l * l - m * m))
            b = math.sqrt(((l - 1.0) ** 2 - m * m) / (4.0 * (l - 1.0) ** 2 - 1.0))
            earlier = table[m, l - 2] if l >= m + 2 else 0.0
            table[m, l] = a * (cosine * table[m, l - 1] - b * earlier)
    return table, math.pi / NLAT * sine


def dft_tables():
    phases = 2.0 * math.pi * (np.outer(np.arange(NLON), np.arange(M)) % NLON) / NLON
    cosine, sine = np.cos(phases), np.sin(phases)
    doubling = np.where(np.arange(M) == 0, 1.0, 2.0)
    forward = np.stack([cosine, -sine], axis=2).reshape(NLON, Q) / NLON
    inverse = np.stack([doubling * cosine, -doubling * sine], axis=2).reshape(NLON, Q).T
    return forward, inverse


def dft_kernel(rows, points, table_ref, *refs):
    slots, out_ref, scratch = refs[:-2], refs[-2], refs[-1]
    table = table_ref[...]
    for j in range(rows):
        circle = jnp.concatenate([slot[j] for slot in slots], axis=0)
        scratch[pl.ds(j, Q, stride=rows), :] = jnp.dot(
            table, circle, preferred_element_type=F32
        )
    out_ref[...] = scratch[...].astype(LOW)


def dft(table, slots):
    rows, points, lanes = slots[0].shape
    return pl.pallas_call(
        lambda *refs: dft_kernel(rows, points, *refs),
        out_shape=jax.ShapeDtypeStruct((Q * rows, lanes), LOW),
        scratch_shapes=[pltpu.VMEM((Q * rows, lanes), F32)],
        compiler_params=pltpu.CompilerParams(vmem_limit_bytes=VMEM_LIMIT),
        cost_estimate=pl.CostEstimate(
            flops=2 * Q * NLON * rows * 256, bytes_accessed=4 * rows * NLON * lanes * 4, transcendentals=0
        ),
        name="dft",
    )(table, *slots)


def idft_kernel(rows, points, table_ref, spectra_ref, *refs):
    outs, scratch = refs[:-1], refs[-1]
    scratch[...] = spectra_ref[...].astype(F32)
    table = table_ref[...]
    for j in range(rows):
        circle = jnp.dot(
            table,
            scratch[pl.ds(j, Q, stride=rows), :].astype(LOW),
            preferred_element_type=F32,
        ).astype(LOW)
        for s, out in enumerate(outs):
            out[j] = circle[s * points : (s + 1) * points]


def idft(table, spectra, rows, points, count):
    lanes = spectra.shape[1]
    return pl.pallas_call(
        lambda *refs: idft_kernel(rows, points, *refs),
        out_shape=[jax.ShapeDtypeStruct((rows, points, lanes), LOW)] * count,
        scratch_shapes=[pltpu.VMEM((Q * rows, lanes), F32)],
        compiler_params=pltpu.CompilerParams(vmem_limit_bytes=VMEM_LIMIT),
        cost_estimate=pl.CostEstimate(
            flops=2 * Q * NLON * rows * 256, bytes_accessed=4 * rows * NLON * lanes * 4, transcendentals=0
        ),
        name="idft",
    )(table, spectra)


def filter_forward_kernel(tile_ref, analysis_ref, synthesis_ref, response_ref, s_ref, out_ref, coef_ref):
    response = response_ref[0]
    shape = s_ref.shape
    for q in range(shape[1]):
        spectra = s_ref[:, q].reshape(NLAT, LANES)
        coef = jnp.dot(analysis_ref[q], spectra, preferred_element_type=F32)
        coef_ref[q] = coef
        filtered = (response * coef).astype(LOW)
        values = jnp.dot(synthesis_ref[q], filtered, preferred_element_type=F32)
        out_ref[:, q] = values.astype(LOW).reshape(shape[0], shape[2], LANES)


def filter_backward_kernel(
    tile_ref, analysis_ref, synthesis_ref, response_ref, s_ref, coef_ref, out_ref, grad_ref
):
    response = response_ref[0]
    shape = s_ref.shape
    grad = jnp.zeros((L, LANES), F32)
    for q in range(shape[1]):
        spectra = s_ref[:, q].reshape(NLAT, LANES)
        back = jnp.dot(analysis_ref[q], spectra, preferred_element_type=F32)
        grad = grad + coef_ref[q] * back
        filtered = (response * back).astype(LOW)
        values = jnp.dot(synthesis_ref[q], filtered, preferred_element_type=F32)
        out_ref[:, q] = values.astype(LOW).reshape(shape[0], shape[2], LANES)
    grad_ref[...] = grad


def whole_block(array):
    zeros = (0,) * array.ndim
    return pl.BlockSpec(array.shape, lambda i, tile: zeros)


def filter_call(kernel, name, tile, tables, response, spectra, extra, outs):
    arrays = [*tables, response, spectra, *extra]
    specs = [whole_block(a) for a in arrays]
    specs[2] = pl.BlockSpec((1, L, LANES), lambda i, tile: (tile[0], 0, 0))
    return pl.pallas_call(
        kernel,
        out_shape=outs,
        grid_spec=pltpu.PrefetchScalarGridSpec(
            num_scalar_prefetch=1,
            grid=(1,),
            in_specs=specs,
            out_specs=[whole_block(o) for o in outs],
        ),
        compiler_params=pltpu.CompilerParams(vmem_limit_bytes=VMEM_LIMIT),
        cost_estimate=pl.CostEstimate(
            flops=4 * spectra.shape[1] * L * NLAT * 256,
            bytes_accessed=8 * 1024 * 1024,
            transcendentals=0,
        ),
        name=name,
    )(tile, *arrays)


def exact_gelu(values):
    return jax.nn.gelu(values, approximate=False)


def inverse_rms(values):
    return lax.rsqrt(jnp.mean(values * values, axis=-1, keepdims=True) + NORM_EPS)


def norm_backward(values, inverse, gain, upstream):
    scaled = upstream * gain
    inner = jnp.mean(values * scaled, axis=-1, keepdims=True)
    grad = inverse * scaled - values * (inverse * inverse * inverse) * inner
    return grad, jnp.sum(upstream * values * inverse, axis=0)


def adafactor_matrix(weight_now, gradient, rows_old, columns_old, decay_rate):
    squares = gradient * gradient + FIRST_EPS
    rows_new = decay_rate * rows_old + (1.0 - decay_rate) * jnp.mean(squares, axis=1)
    columns_new = decay_rate * columns_old + (1.0 - decay_rate) * jnp.mean(squares, axis=0)
    estimate = rows_new[:, None] * columns_new[None, :] / jnp.mean(rows_new)
    update = gradient * lax.rsqrt(estimate)
    update = update / jnp.maximum(1.0, jnp.sqrt(jnp.mean(update * update)) / CLIP_LEVEL)
    scale_now = STEP_RATE * jnp.maximum(SECOND_EPS, jnp.sqrt(jnp.mean(weight_now * weight_now)))
    return (weight_now - scale_now * update, rows_new, columns_new)


def adafactor_vector(weight_now, gradient, moments_old, decay_rate):
    moments_new = decay_rate * moments_old + (1.0 - decay_rate) * (gradient * gradient + FIRST_EPS)
    update = gradient * lax.rsqrt(moments_new)
    update = update / jnp.maximum(
        1.0, jnp.sqrt(jnp.mean(update * update, axis=1, keepdims=True)) / CLIP_LEVEL
    )
    scale_now = STEP_RATE * jnp.maximum(
        SECOND_EPS, jnp.sqrt(jnp.mean(weight_now * weight_now, axis=1, keepdims=True))
    )
    return (weight_now - scale_now * update, moments_new)


def take(array, index):
    return lax.dynamic_index_in_dim(array, index, 0, keepdims=False)


def body(
    fields_in,
    cotangent,
    member_dates,
    date_table,
    norm_gains,
    spectral_filter,
    weight_in,
    weight_out,
    gain_moments,
    in_row_stats,
    in_column_stats,
    out_row_stats,
    out_column_stats,
    filter_row_stats,
    filter_column_stats,
):
    members, rows, points, channels = fields_in.shape
    tiles = channels // LANES
    wide = tiles * LANES
    lat, lon = lax.axis_size("lat"), lax.axis_size("lon")
    lat_me, lon_me = lax.axis_index("lat"), lax.axis_index("lon")
    chunks = members * tiles // lon
    share = Q // lat
    grid = rows * points

    legendre, quadrature = legendre_table()
    forward, inverse = dft_tables()
    own_q = (lat_me * share + jnp.arange(share, dtype=jnp.int32)) // 2
    plain = jnp.take(jnp.asarray(legendre, LOW), own_q, axis=0)
    weighted = jnp.take(jnp.asarray(legendre * quadrature, LOW), own_q, axis=0)
    plain_t = jnp.swapaxes(plain, 1, 2)
    weighted_t = jnp.swapaxes(weighted, 1, 2)

    def arrived(table):
        blocks = table.reshape(lon, points, Q)
        orders = [np.concatenate([blocks[(me - s) % lon] for s in range(lon)]).T for me in range(lon)]
        return take(jnp.asarray(np.stack(orders), LOW), lon_me)

    def leaving(table):
        blocks = table.reshape(lon, points, Q)
        orders = [np.concatenate([blocks[(me + s) % lon] for s in range(lon)]) for me in range(lon)]
        return take(jnp.asarray(np.stack(orders), LOW), lon_me)

    analysis, back_analysis = arrived(forward), arrived(inverse.T)
    synthesis, back_synthesis = leaving(inverse.T), leaving(forward)
    responses = jnp.swapaxes(spectral_filter[:, :wide].reshape(L, tiles, LANES), 0, 1)

    def exchange_lon(slots):
        return [
            slot
            if s == 0
            else lax.ppermute(slot, "lon", [(i, (i + s) % lon) for i in range(lon)])
            for s, slot in enumerate(slots)
        ]

    def send_units(units, r):
        stacked = jnp.stack(units)
        return exchange_lon([take(stacked, (lon_me + s) % lon) for s in range(lon)])

    def exchange_lat(blocks):
        return lax.all_to_all(blocks, "lat", split_axis=0, concat_axis=0, tiled=True)

    def to_degrees(spectra):
        got = exchange_lat(spectra.reshape(lat, share * rows, LANES)).reshape(lat, share, rows, LANES)
        if rows % 16:
            got = jnp.swapaxes(got, 0, 1).reshape(1, share, NLAT, LANES)
        return got

    def to_rows(values):
        if rows % 16:
            values = jnp.swapaxes(values.reshape(share, lat, rows, LANES), 0, 1)
        return exchange_lat(values.reshape(lat, share * rows, LANES)).reshape(Q * rows, LANES)

    def tile_of(r):
        return ((lon * r + lon_me) % tiles).astype(jnp.int32).reshape(1)

    def spectral_forward(slots, r):
        spectra = to_degrees(dft(analysis, [s.reshape(rows, points, LANES) for s in slots]))
        values, coefs = filter_call(
            filter_forward_kernel,
            "filter_forward",
            tile_of(r),
            (weighted, plain_t),
            responses,
            spectra,
            (),
            [
                jax.ShapeDtypeStruct(spectra.shape, LOW),
                jax.ShapeDtypeStruct((share, L, LANES), F32),
            ],
        )
        return idft(synthesis, to_rows(values), rows, points, lon), coefs

    def spectral_backward(slots, coefs, r):
        spectra = to_degrees(dft(back_analysis, [s.reshape(rows, points, LANES) for s in slots]))
        values, grad = filter_call(
            filter_backward_kernel,
            "filter_backward",
            tile_of(r),
            (plain, weighted_t),
            responses,
            spectra,
            (coefs,),
            [
                jax.ShapeDtypeStruct(spectra.shape, LOW),
                jax.ShapeDtypeStruct((L, LANES), F32),
            ],
        )
        return idft(back_synthesis, to_rows(values), rows, points, lon), grad

    rest = channels - wide
    response_rest = spectral_filter[:, wide:]
    own_points = lon_me * points

    def rest_in(values, table):
        whole = lax.all_gather(values, "lon", axis=2, tiled=True)
        spectra = jnp.einsum(
            "bjkc,kq->bcjq", whole, jnp.asarray(table, LOW), preferred_element_type=F32
        ).astype(LOW)
        spectra = lax.all_gather(spectra, "lat", axis=2, tiled=True)
        return lax.dynamic_slice_in_dim(spectra, lat_me * share, share, 3)

    def rest_out(filtered, degrees, table):
        values = jnp.einsum(
            "qjl,qlbc->bcjq", degrees, filtered, preferred_element_type=F32
        ).astype(LOW)
        values = lax.all_gather(values, "lat", axis=3, tiled=True)
        values = lax.dynamic_slice_in_dim(values, lat_me * rows, rows, 2)
        own = lax.dynamic_slice_in_dim(jnp.asarray(table, LOW), own_points, points, 0)
        return jnp.einsum("bcjq,kq->bjkc", values, own, preferred_element_type=F32).astype(LOW)

    date_selector = (
        member_dates[:, None] == jnp.arange(date_table.shape[0], dtype=jnp.int32)[None, :]
    ).astype(F32)
    offsets = jnp.dot(date_selector, date_table, precision=lax.Precision.HIGHEST)
    shifted, first_inverse, normed = [], [], []
    for b in range(members):
        moved = fields_in[b].reshape(grid, channels).astype(F32) + offsets[b]
        scale = inverse_rms(moved)
        shifted.append(moved)
        first_inverse.append(scale)
        normed.append((moved * scale * norm_gains[0]).astype(LOW))

    def units_of(member_values):
        return [
            values[:, t * LANES : (t + 1) * LANES] for values in member_values for t in range(tiles)
        ]

    def rest_of(member_values):
        return jnp.stack([v[:, wide:].reshape(rows, points, rest) for v in member_values])

    def gather_member(arrivals, rest_values, b):
        pieces = []
        for t in range(tiles):
            r, owner = divmod(b * tiles + t, lon)
            pieces.append(take(arrivals[r], (lon_me - owner) % lon).reshape(grid, LANES))
        return jnp.concatenate([*pieces, rest_values[b].reshape(grid, rest)], axis=1)

    units = units_of(normed)
    coefs, arrivals = [], []
    for r in range(chunks):
        slots = send_units(units[r * lon : (r + 1) * lon], r)
        out, coef = spectral_forward(slots, r)
        coefs.append(coef)
        arrivals.append(jnp.stack(exchange_lon(out)))
    spectra_rest = rest_in(rest_of(normed), forward)
    coefs_rest = jnp.einsum("qlj,bcjq->qlbc", weighted, spectra_rest, preferred_element_type=F32)
    filtered_rest = (response_rest[None, :, None, :] * coefs_rest).astype(LOW)
    branch_rest = rest_out(filtered_rest, plain_t, inverse.T)

    inner_low = weight_in.astype(LOW)
    outer_low = weight_out.astype(LOW)
    block_output, back_hidden, back_low = [], [], []
    grad_in_part = grad_out_part = gain_two_part = 0.0
    for b in range(members):
        branch = gather_member(arrivals, branch_rest, b)
        upstream = cotangent[b].reshape(grid, channels)
        hidden = shifted[b] + branch.astype(F32)
        second_inverse = inverse_rms(hidden)
        second_low = (hidden * second_inverse * norm_gains[1]).astype(LOW)
        preact = jnp.dot(second_low, inner_low, preferred_element_type=F32)
        activation, gelu_pull = jax.vjp(exact_gelu, preact)
        active_low = activation.astype(LOW)
        block_output.append(
            (hidden + jnp.dot(active_low, outer_low, preferred_element_type=F32)).astype(LOW)
        )
        grad_out_part += jnp.einsum("gh,gc->hc", active_low, upstream, preferred_element_type=F32)
        back_active = jnp.einsum("gc,hc->gh", upstream, outer_low, preferred_element_type=F32)
        back_preact = gelu_pull(back_active)[0].astype(LOW)
        grad_in_part += jnp.einsum("gc,gh->ch", second_low, back_preact, preferred_element_type=F32)
        back_second = jnp.einsum("gh,ch->gc", back_preact, inner_low, preferred_element_type=F32)
        grad, gain_part = norm_backward(hidden, second_inverse, norm_gains[1], back_second)
        gain_two_part += gain_part
        grad = grad + upstream.astype(F32)
        back_hidden.append(grad)
        back_low.append(grad.astype(LOW))

    units = units_of(back_low)
    arrivals, grads = [], []
    for r in range(chunks):
        slots = send_units(units[r * lon : (r + 1) * lon], r)
        out, grad = spectral_backward(slots, coefs[r], r)
        grads.append(grad)
        arrivals.append(jnp.stack(exchange_lon(out)))
    spectra_rest = rest_in(rest_of(back_low), inverse.T)
    back_rest = jnp.einsum("qlj,bcjq->qlbc", plain, spectra_rest, preferred_element_type=F32)
    grad_rest = jnp.sum(coefs_rest * back_rest, axis=(0, 2)) / lon
    filtered_rest = (response_rest[None, :, None, :] * back_rest).astype(LOW)
    normed_rest = rest_out(filtered_rest, weighted_t, forward)

    input_grad, gain_one_part = [], 0.0
    for b in range(members):
        back_normed = gather_member(arrivals, normed_rest, b).astype(F32)
        grad, gain_part = norm_backward(shifted[b], first_inverse[b], norm_gains[0], back_normed)
        gain_one_part += gain_part
        input_grad.append((back_hidden[b] + grad).reshape(rows, points, channels))

    stacked = jnp.stack(grads)
    ordered = []
    for t in range(tiles):
        hits = jnp.stack([(tile_of(r)[0] == t) for r in range(chunks)])
        ordered.append(jnp.sum(jnp.where(hits[:, None, None], stacked, 0.0), axis=0))
    filter_part = jnp.concatenate([*ordered, grad_rest], axis=1)

    grad_weight_in, grad_weight_out = lax.psum((grad_in_part, grad_out_part), ("lat", "lon"))
    grad_filter, grad_gains = lax.psum(
        (filter_part, jnp.stack([gain_one_part, gain_two_part])), ("lat", "lon")
    )
    decay_rate = 1.0 - STEP ** (-0.8)
    new_weight_in, new_in_rows, new_in_columns = adafactor_matrix(
        weight_in, grad_weight_in, in_row_stats, in_column_stats, decay_rate
    )
    new_weight_out, new_out_rows, new_out_columns = adafactor_matrix(
        weight_out, grad_weight_out, out_row_stats, out_column_stats, decay_rate
    )
    new_filter, new_filter_rows, new_filter_columns = adafactor_matrix(
        spectral_filter, grad_filter, filter_row_stats, filter_column_stats, decay_rate
    )
    new_gains, new_moments = adafactor_vector(norm_gains, grad_gains, gain_moments, decay_rate)
    return (
        jnp.stack(block_output).reshape(fields_in.shape),
        jnp.stack(input_grad),
        grad_weight_in,
        grad_weight_out,
        grad_filter,
        grad_gains,
        new_weight_in,
        new_weight_out,
        new_filter,
        new_gains,
        new_in_rows,
        new_in_columns,
        new_out_rows,
        new_out_columns,
        new_filter_rows,
        new_filter_columns,
        new_moments,
    )


def solution(mesh):
    spread = P(None, "lat", "lon", None)
    return jax.shard_map(
        body,
        mesh=mesh,
        in_specs=(spread, spread) + (P(),) * 13,
        out_specs=(spread, spread) + (P(),) * 15,
        check_vma=False,
    )
```

time: 2710 us -> 1300 us (0.48)
  waiting for transfers between devices: 1330 us -> 120 us
  starting transfers between devices: 12.7 us -> 275 us
  blocking collectives: 326 us -> 141 us
  other arithmetic: 284 us -> 180 us
  matrix products: 281 us -> 183 us
  loops' own time: 86.1 us -> 0 us
  local copies, waits for them, and re-layouts: 363 us -> 315 us
  Pallas kernels: 0 us -> 42.7 us
    reduce_scatter x2 -> x0, waiting for transfers between devices: 847 us -> none  [the longest x1 425 us: body(): lax.psum_scatter(jnp.einsum('qlj,bqjc->lbqc', portion, spectra_wide, prec...]
    all_gather x2 -> x0, waiting for transfers between devices: 312 us -> none  [the longest x1 178 us: body(): lax.all_gather(filtered, 'lat', axis=0, tiled=True).astype(jnp.float32)]
    all_to_all x2 -> x0, blocking collectives: 287 us -> none  [the longest x1 146 us: body(): lax.all_to_all(lon_fields, 'lon', split_axis=2, concat_axis=0, tiled=True)]
    ppermute x0 -> x60, starting transfers between devices: none -> 184 us  [exchange_lon(): lax.ppermute(slot, 'lon', [(i, (i + s) % lon) for i in range(lon)])]
    psum x1, waiting for transfers between devices: 170 us -> 0.02 us  [body(): lax.psum((grad_in_part, grad_out_part), ('lat', 'lon'))]
    transpose x3 -> x1, local copies, waits for them, and re-layouts: 155 us -> 1.51 us  [body(): plain_t = jnp.swapaxes(plain, 1, 2)]
    unnamed x105 -> x573, local copies, waits for them, and re-layouts: 6.87 us -> 117 us
    dynamic_update_slice x128 -> x0, other arithmetic: 97.3 us -> none  [legendre_table(): lax.scan(advance, (zeroes, zeroes), jnp.arange(L, dtype=jnp.int32))]
  transfers between devices with their start and end apart: 7 -> 81, of which waited for: 5 -> 21; matrix products, arithmetic and copies ran while one was open for 14% -> 29% of each run, Pallas kernels for 0% -> 3%
where the time goes in v1:
time: 1300 us; the launch traced here: 1280 us
  local copies, waits for them, and re-layouts  315 us (24%)
  starting transfers between devices  275 us (21%)
  matrix products  183 us (14%)
  other arithmetic  180 us (14%)
  blocking collectives  141 us (11%)
  waiting for transfers between devices  120 us (9%)
  Pallas kernels  42.7 us (3%)
  between operations  23.9 us (2%)
    ppermute x60, starting transfers between devices, exchange_lon(): lax.ppermute(slot, 'lon', [(i, (i + s) % lon) for i in range(lon)])  184 us
    unnamed x573, local copies, waits for them, and re-layouts  117 us
    ppermute x60, waiting for transfers between devices, exchange_lon(): lax.ppermute(slot, 'lon', [(i, (i + s) % lon) for i in range(lon)])  96.9 us
    all_to_all x20, starting transfers between devices, exchange_lat(): lax.all_to_all(blocks, 'lat', split_axis=0, concat_axis=0, tiled=True)  91.1 us
    dot_general x4, matrix products, body(): jnp.einsum('gc,hc->gh', upstream, outer_low, preferred_element_type=F32)  65.1 us
    psum x1, blocking collectives, body(): lax.psum((filter_part, jnp.stack([gain_one_part, gain_two_part])), ('lat'...  49.2 us
    dynamic_slice x50, local copies, waits for them, and re-layouts, take(): return lax.dynamic_index_in_dim(array, index, 0, keepdims=False)  46.3 us
    reshape x40, local copies, waits for them, and re-layouts, gather_member(): take(arrivals[r], (lon_me - owner) % lon).reshape(grid, LANES)  43.9 us
  transfers between devices with their start and end apart: 81, of which 21 were waited for; matrix products, arithmetic and copies ran while one was open for 29% of the time, Pallas kernels for 3%

profile of v1, /device:TPU:0, one launch (start us, length us, event | category | flops | bytes accessed | tf_op | source)
XLA Modules:
  0.0 1281.6 jit_solution(16579344510212307729)
XLA Ops:
  9.0 7.3 slice_convert_fusion.3
  52.5 10.4 collective-permute-done.13
  97.7 14.5 %all-to-all-start.8 = ((bf16[8,384,128]{2,1,0:T(8,128)(2,1)}), bf16[8,384,128]{2,1,0:T(8,128)(2,1)S(1)}, u32[]{:S(2)}, u32[]{:S(2)}) async-start(bf16[8,384,128]{2,1,0:T(8,128)(2,1)} %bitcast.134), calls=%async_computation.8 | async-start | bytes 1572864 | tf_op jit(solution)/shard_map/all_to_all | solution.py:266
  157.9 11.6 collective-permute-start.8
  183.3 14.1 %all_gather.18 = bf16[4,16,256,1]{1,0,3,2:T(4,128)(2,1)S(1)} all-gather(bf16[4,16,64,1]{1,0,3,2:T(4,128)(2,1)S(1)} %copy.494), channel_id=1, replica_groups=mesh['lat'=8,'lon'=4] {'lon'}, dimensions={2}, use_global_device_ids=true | all-gather | bytes 40960 | tf_op jit(solution)/shard_map/all_gather | solution.py:321
  197.7 9.6 all_gather.19
  250.4 15.1 %all_gather.20 = bf16[4,1,128,192]{2,0,1,3:T(4,128)(2,1)} all-gather(bf16[4,1,128,24]{2,0,1,3:T(4,128)(2,1)S(1)} %copy-done.161), channel_id=1, replica_groups=mesh['lat'=8,'lon'=4] {'lat'}, dimensions={3}, use_global_device_ids=true | all-gather | bytes 221184 | tf_op jit(solution)/shard_map/all_gather | solution.py:332
  362.9 13.4 %collective-permute-start.22 = (bf16[16,64,128]{2,1,0:T(8,128)(2,1)}, bf16[16,64,128]{2,1,0:T(8,128)(2,1)}, u32[]{:S(2)}, u32[]{:S(2)}) collective-permute-start(bf16[16,64,128]{2,1,0:T(8,128)(2,1)} %copy-done.42), channel_id=1, source_target_pairs={{0,2},{1,3},{2,0},{3,1},{4,6},{5,7},{6,4},{7,5},{8,10},{9,11},{10,... | collective-permute-start | bytes 786440 | tf_op jit(solution)/shard_map/ppermute | solution.py:257
  379.8 24.9 %collective-permute-done.10 = bf16[16,64,128]{2,1,0:T(8,128)(2,1)} collective-permute-done((bf16[16,64,128]{2,1,0:T(8,128)(2,1)}, bf16[16,64,128]{2,1,0:T(8,128)(2,1)}, u32[]{:S(2)}, u32[]{:S(2)}) %collective-permute-start.10) | collective-permute-done | bytes 262176 | tf_op jit(solution)/shard_map/ppermute | solution.py:257
  421.6 8.2 collective-permute-start.27
  486.6 16.2 %add_convert_fusion.3 = (bf16[1024,1282]{0,1:T(8,128)(2,1)S(1)}, f32[1024,1282]{0,1:T(8,128)}) fusion(f32[1024,1282]{0,1:T(8,128)S(1)} %fusion.71, bf16[1024,641]{1,0:T(8,128)(2,1)S(1)} %bitcast.540, bf16[1282,641]{0,1:T(8,128)(2,1)S(1)} %copy-done.110), kind=kOutput, calls=%fused_computation.15 | convolution fusion | flops 1777487872 | bytes 16083972 | tf_op jit(solution)/shard_map/gc,hc->gh/dot_general | solution.py:393
  516.4 16.5 %add_convert_fusion.2 = (bf16[1024,1282]{0,1:T(8,128)(2,1)S(1)}, f32[1024,1282]{0,1:T(8,128)}) fusion(f32[1024,1282]{0,1:T(8,128)S(1)} %fusion.73, bf16[1024,641]{1,0:T(8,128)(2,1)S(1)} %bitcast.537, bf16[1282,641]{0,1:T(8,128)(2,1)S(1)} %copy-done.111), kind=kOutput, calls=%fused_computation.14 | convolution fusion | flops 1777487872 | bytes 16083972 | tf_op jit(solution)/shard_map/gc,hc->gh/dot_general | solution.py:393
  568.8 16.1 %add_convert_fusion.1 = (bf16[1024,1282]{0,1:T(8,128)(2,1)S(1)}, f32[1024,1282]{0,1:T(8,128)}) fusion(f32[1024,1282]{0,1:T(8,128)S(1)} %fusion.75, bf16[1024,641]{1,0:T(8,128)(2,1)S(1)} %bitcast.534, bf16[1282,641]{0,1:T(8,128)(2,1)S(1)} %copy-done.112), kind=kOutput, calls=%fused_computation.13 | convolution fusion | flops 1777487872 | bytes 16083972 | tf_op jit(solution)/shard_map/gc,hc->gh/dot_general | solution.py:393
  599.0 16.4 %add_convert_fusion = (bf16[1024,1282]{0,1:T(8,128)(2,1)}, f32[1024,1282]{0,1:T(8,128)}) fusion(f32[1024,1282]{0,1:T(8,128)S(1)} %fusion.76, bf16[1024,641]{1,0:T(8,128)(2,1)S(1)} %bitcast.523, bf16[1282,641]{0,1:T(8,128)(2,1)S(1)} %copy-done.113), kind=kOutput, calls=%fused_computation.12 | convolution fusion | flops 1777487872 | bytes 16083972 | tf_op jit(solution)/shard_map/gc,hc->gh/dot_general | solution.py:393
  615.5 9.0 multiply_reduce_fusion.12
  624.6 6.9 fusion.55
  676.1 9.9 add_add_fusion.1
  703.6 26.6 %all_gather.21 = bf16[4,16,256,1]{1,0,3,2:T(4,128)(2,1)S(1)} all-gather(bf16[4,16,64,1]{1,0,3,2:T(4,128)(2,1)S(1)} %copy.557), channel_id=1, replica_groups=mesh['lat'=8,'lon'=4] {'lon'}, dimensions={2}, use_global_device_ids=true | all-gather | bytes 40960 | tf_op jit(solution)/shard_map/all_gather | solution.py:321
  788.8 9.9 all_gather.22
  824.8 16.8 %all_gather.23 = bf16[4,1,128,192]{2,0,1,3:T(4,128)(2,1)} all-gather(bf16[4,1,128,24]{2,0,1,3:T(4,128)(2,1)S(1)} %fusion.47), channel_id=1, replica_groups=mesh['lat'=8,'lon'=4] {'lat'}, dimensions={3}, use_global_device_ids=true | all-gather | bytes 221184 | tf_op jit(solution)/shard_map/all_gather | solution.py:332
  904.7 9.8 add_add_fusion
  921.6 7.1 pad_maximum_fusion.1
  961.9 8.7 collective-permute-done.40
  971.7 20.1 %collective-permute-start.46 = (bf16[16,64,128]{2,1,0:T(8,128)(2,1)}, bf16[16,64,128]{2,1,0:T(8,128)(2,1)}, u32[]{:S(2)}, u32[]{:S(2)}) collective-permute-start(bf16[16,64,128]{2,1,0:T(8,128)(2,1)} %get-tuple-element.119), channel_id=1, source_target_pairs={{0,2},{1,3},{2,0},{3,1},{4,6},{5,7},{6,4},{7,5},{8,10},{9,11},{10,... | collective-permute-start | bytes 786440 | tf_op jit(solution)/shard_map/ppermute | solution.py:257
  1000.2 9.3 collective-permute-done.34
  1009.5 17.8 %collective-permute-start.52 = (bf16[16,64,128]{2,1,0:T(8,128)(2,1)S(1)}, bf16[16,64,128]{2,1,0:T(8,128)(2,1)S(1)}, u32[]{:S(2)}, u32[]{:S(2)}) collective-permute-start(bf16[16,64,128]{2,1,0:T(8,128)(2,1)S(1)} %copy-done.45), channel_id=1, source_target_pairs={{0,2},{1,3},{2,0},{3,1},{4,6},{5,7},{6,4},{7,5},{8,10},{9,11},{10,... | collective-permute-start | bytes 786440 | tf_op jit(solution)/shard_map/ppermute | solution.py:257
  1037.5 11.7 collective-permute-done.46
  1051.1 14.4 %collective-permute-start.58 = (bf16[16,64,128]{2,1,0:T(8,128)(2,1)S(1)}, bf16[16,64,128]{2,1,0:T(8,128)(2,1)}, u32[]{:S(2)}, u32[]{:S(2)}) collective-permute-start(bf16[16,64,128]{2,1,0:T(8,128)(2,1)S(1)} %get-tuple-element.131), channel_id=1, source_target_pairs={{0,2},{1,3},{2,0},{3,1},{4,6},{5,7},{6,4},{7,5},{8,10},{9,11},{10,... | collective-permute-start | bytes 786440 | tf_op jit(solution)/shard_map/ppermute | solution.py:257
  1072.0 7.9 collective-permute-done.52
  1105.3 8.2 fusion.39
  1173.4 49.2 %psum.31 = f32[2,641]{1,0:T(2,128)S(1)} all-reduce(f32[2,641]{1,0:T(2,128)S(1)} %pad_maximum_fusion.24), channel_id=1, replica_groups=mesh['lat'=8,'lon'=4] {'lat','lon'}, use_global_device_ids=true, to_apply=%region_33.35 | all-reduce | flops 1282 | bytes 10256 | tf_op jit(solution)/shard_map/psum | solution.py:431
  1223.4 9.3 pad_maximum_fusion
  (1073 shorter events, 810.6 us)
Async XLA Ops:
  84.2 45.3 %collective-permute-start.18 = (bf16[1024,128]{1,0:T(8,128)(2,1)}, bf16[1024,128]{1,0:T(8,128)(2,1)S(1)}, u32[]{:S(2)}, u32[]{:S(2)}) collective-permute-start(bf16[1024,128]{1,0:T(8,128)(2,1)} %bitcast.103), channel_id=1, source_target_pairs={{0,1},{1,2},{2,3},{3,0},{4,5},{5,6},{6,7},{7,4},{8,9},{9,10},{10,1... | collective-permute-start | bytes 786440 | tf_op jit(solution)/shard_map/ppermute | solution.py:257
  86.4 43.2 %collective-permute-start.19 = (bf16[1024,128]{1,0:T(8,128)(2,1)}, bf16[1024,128]{1,0:T(8,128)(2,1)S(1)}, u32[]{:S(2)}, u32[]{:S(2)}) collective-permute-start(bf16[1024,128]{1,0:T(8,128)(2,1)} %bitcast.105), channel_id=1, source_target_pairs={{0,2},{1,3},{2,0},{3,1},{4,6},{5,7},{6,4},{7,5},{8,10},{9,11},{10,... | collective-permute-start | bytes 786440 | tf_op jit(solution)/shard_map/ppermute | solution.py:257
  92.0 40.5 %collective-permute-start.20 = (bf16[1024,128]{1,0:T(8,128)(2,1)}, bf16[1024,128]{1,0:T(8,128)(2,1)S(1)}, u32[]{:S(2)}, u32[]{:S(2)}) collective-permute-start(bf16[1024,128]{1,0:T(8,128)(2,1)} %bitcast.107), channel_id=1, source_target_pairs={{0,3},{1,0},{2,1},{3,2},{4,7},{5,4},{6,5},{7,6},{8,11},{9,8},{10,9... | collective-permute-start | bytes 786440 | tf_op jit(solution)/shard_map/ppermute | solution.py:257
  97.7 39.6 %all-to-all-start.8 = ((bf16[8,384,128]{2,1,0:T(8,128)(2,1)}), bf16[8,384,128]{2,1,0:T(8,128)(2,1)S(1)}, u32[]{:S(2)}, u32[]{:S(2)}) async-start(bf16[8,384,128]{2,1,0:T(8,128)(2,1)} %bitcast.134), calls=%async_computation.8 | async-start | bytes 1572864 | tf_op jit(solution)/shard_map/all_to_all | solution.py:266
  115.2 93.5 %collective-permute-start.6 = (bf16[1024,128]{1,0:T(8,128)(2,1)}, bf16[1024,128]{1,0:T(8,128)(2,1)}, u32[]{:S(2)}, u32[]{:S(2)}) collective-permute-start(bf16[1024,128]{1,0:T(8,128)(2,1)} %bitcast.603), channel_id=1, source_target_pairs={{0,1},{1,2},{2,3},{3,0},{4,5},{5,6},{6,7},{7,4},{8,9},{9,10},{10,1... | collective-permute-start | bytes 786440 | tf_op jit(solution)/shard_map/ppermute | solution.py:257
  122.7 86.0 %collective-permute-start.7 = (bf16[1024,128]{1,0:T(8,128)(2,1)}, bf16[1024,128]{1,0:T(8,128)(2,1)}, u32[]{:S(2)}, u32[]{:S(2)}) collective-permute-start(bf16[1024,128]{1,0:T(8,128)(2,1)} %bitcast.39), channel_id=1, source_target_pairs={{0,2},{1,3},{2,0},{3,1},{4,6},{5,7},{6,4},{7,5},{8,10},{9,11},{10,... | collective-permute-start | bytes 786440 | tf_op jit(solution)/shard_map/ppermute | solution.py:257
  129.6 39.9 %collective-permute-start.1 = (bf16[1024,128]{1,0:T(8,128)(2,1)}, bf16[1024,128]{1,0:T(8,128)(2,1)S(1)}, u32[]{:S(2)}, u32[]{:S(2)}) collective-permute-start(bf16[1024,128]{1,0:T(8,128)(2,1)} %bitcast.611), channel_id=1, source_target_pairs={{0,2},{1,3},{2,0},{3,1},{4,6},{5,7},{6,4},{7,5},{8,10},{9,11},{10,... | collective-permute-start | bytes 786440 | tf_op jit(solution)/shard_map/ppermute | solution.py:257
  157.9 50.8 %collective-permute-start.8 = (bf16[1024,128]{1,0:T(8,128)(2,1)}, bf16[1024,128]{1,0:T(8,128)(2,1)S(1)}, u32[]{:S(2)}, u32[]{:S(2)}) collective-permute-start(bf16[1024,128]{1,0:T(8,128)(2,1)} %bitcast.41), channel_id=1, source_target_pairs={{0,3},{1,0},{2,1},{3,2},{4,7},{5,4},{6,5},{7,6},{8,11},{9,8},{10,9... | collective-permute-start | bytes 786440 | tf_op jit(solution)/shard_map/ppermute | solution.py:257
  308.8 46.3 %all-to-all-start.5 = ((bf16[8,384,128]{2,1,0:T(8,128)(2,1)}), bf16[8,384,128]{2,1,0:T(8,128)(2,1)S(1)}, u32[]{:S(2)}, u32[]{:S(2)}) async-start(bf16[8,384,128]{2,1,0:T(8,128)(2,1)} %bitcast.475), calls=%async_computation.5 | async-start | bytes 1572864 | tf_op jit(solution)/shard_map/all_to_all | solution.py:266
  346.3 58.5 %collective-permute-start.10 = (bf16[16,64,128]{2,1,0:T(8,128)(2,1)}, bf16[16,64,128]{2,1,0:T(8,128)(2,1)}, u32[]{:S(2)}, u32[]{:S(2)}) collective-permute-start(bf16[16,64,128]{2,1,0:T(8,128)(2,1)} %get-tuple-element.86), channel_id=1, source_target_pairs={{0,2},{1,3},{2,0},{3,1},{4,6},{5,7},{6,4},{7,5},{8,10},{9,11},{10,... | collective-permute-start | bytes 786440 | tf_op jit(solution)/shard_map/ppermute | solution.py:257
  356.0 48.8 %collective-permute-start.11 = (bf16[16,64,128]{2,1,0:T(8,128)(2,1)}, bf16[16,64,128]{2,1,0:T(8,128)(2,1)S(1)}, u32[]{:S(2)}, u32[]{:S(2)}) collective-permute-start(bf16[16,64,128]{2,1,0:T(8,128)(2,1)} %copy-done.50), channel_id=1, source_target_pairs={{0,3},{1,0},{2,1},{3,2},{4,7},{5,4},{6,5},{7,6},{8,11},{9,8},{10,9... | collective-permute-start | bytes 786440 | tf_op jit(solution)/shard_map/ppermute | solution.py:257
  360.4 93.0 %collective-permute-start.21 = (bf16[16,64,128]{2,1,0:T(8,128)(2,1)}, bf16[16,64,128]{2,1,0:T(8,128)(2,1)}, u32[]{:S(2)}, u32[]{:S(2)}) collective-permute-start(bf16[16,64,128]{2,1,0:T(8,128)(2,1)} %copy-done.43), channel_id=1, source_target_pairs={{0,1},{1,2},{2,3},{3,0},{4,5},{5,6},{6,7},{7,4},{8,9},{9,10},{10,1... | collective-permute-start | bytes 786440 | tf_op jit(solution)/shard_map/ppermute | solution.py:257
  362.9 90.6 %collective-permute-start.22 = (bf16[16,64,128]{2,1,0:T(8,128)(2,1)}, bf16[16,64,128]{2,1,0:T(8,128)(2,1)}, u32[]{:S(2)}, u32[]{:S(2)}) collective-permute-start(bf16[16,64,128]{2,1,0:T(8,128)(2,1)} %copy-done.42), channel_id=1, source_target_pairs={{0,2},{1,3},{2,0},{3,1},{4,6},{5,7},{6,4},{7,5},{8,10},{9,11},{10,... | collective-permute-start | bytes 786440 | tf_op jit(solution)/shard_map/ppermute | solution.py:257
  410.6 42.8 %collective-permute-start.23 = (bf16[16,64,128]{2,1,0:T(8,128)(2,1)S(1)}, bf16[16,64,128]{2,1,0:T(8,128)(2,1)}, u32[]{:S(2)}, u32[]{:S(2)}) collective-permute-start(bf16[16,64,128]{2,1,0:T(8,128)(2,1)S(1)} %copy-done.41), channel_id=1, source_target_pairs={{0,3},{1,0},{2,1},{3,2},{4,7},{5,4},{6,5},{7,6},{8,11},{9,8},{10,9... | collective-permute-start | bytes 786440 | tf_op jit(solution)/shard_map/ppermute | solution.py:257
  673.1 99.5 %collective-permute-start.55 = (bf16[1024,128]{1,0:T(8,128)(2,1)}, bf16[1024,128]{1,0:T(8,128)(2,1)S(1)}, u32[]{:S(2)}, u32[]{:S(2)}) collective-permute-start(bf16[1024,128]{1,0:T(8,128)(2,1)} %bitcast.602), channel_id=1, source_target_pairs={{0,2},{1,3},{2,0},{3,1},{4,6},{5,7},{6,4},{7,5},{8,10},{9,11},{10,... | collective-permute-start | bytes 786440 | tf_op jit(solution)/shard_map/ppermute | solution.py:257
  675.2 76.2 %collective-permute-start.43 = (bf16[1024,128]{1,0:T(8,128)(2,1)}, bf16[1024,128]{1,0:T(8,128)(2,1)S(1)}, u32[]{:S(2)}, u32[]{:S(2)}) collective-permute-start(bf16[1024,128]{1,0:T(8,128)(2,1)} %bitcast.607), channel_id=1, source_target_pairs={{0,2},{1,3},{2,0},{3,1},{4,6},{5,7},{6,4},{7,5},{8,10},{9,11},{10,... | collective-permute-start | bytes 786440 | tf_op jit(solution)/shard_map/ppermute | solution.py:257
  691.3 61.9 %collective-permute-start.44 = (bf16[1024,128]{1,0:T(8,128)(2,1)}, bf16[1024,128]{1,0:T(8,128)(2,1)S(1)}, u32[]{:S(2)}, u32[]{:S(2)}) collective-permute-start(bf16[1024,128]{1,0:T(8,128)(2,1)} %bitcast.608), channel_id=1, source_target_pairs={{0,3},{1,0},{2,1},{3,2},{4,7},{5,4},{6,5},{7,6},{8,11},{9,8},{10,9... | collective-permute-start | bytes 786440 | tf_op jit(solution)/shard_map/ppermute | solution.py:257
  699.2 56.8 %all-to-all-start.16 = ((bf16[8,384,128]{2,1,0:T(8,128)(2,1)}), bf16[8,384,128]{2,1,0:T(8,128)(2,1)}, u32[]{:S(2)}, u32[]{:S(2)}) async-start(bf16[8,384,128]{2,1,0:T(8,128)(2,1)} %bitcast.249), calls=%async_computation.16 | async-start | bytes 1572864 | tf_op jit(solution)/shard_map/all_to_all | solution.py:266
  751.3 60.7 %collective-permute-start.36 = (bf16[1024,128]{1,0:T(8,128)(2,1)}, bf16[1024,128]{1,0:T(8,128)(2,1)S(1)}, u32[]{:S(2)}, u32[]{:S(2)}) collective-permute-start(bf16[1024,128]{1,0:T(8,128)(2,1)} %bitcast.605), channel_id=1, source_target_pairs={{0,1},{1,2},{2,3},{3,0},{4,5},{5,6},{6,7},{7,4},{8,9},{9,10},{10,1... | collective-permute-start | bytes 786440 | tf_op jit(solution)/shard_map/ppermute | solution.py:257
  753.3 58.7 %collective-permute-start.37 = (bf16[1024,128]{1,0:T(8,128)(2,1)}, bf16[1024,128]{1,0:T(8,128)(2,1)}, u32[]{:S(2)}, u32[]{:S(2)}) collective-permute-start(bf16[1024,128]{1,0:T(8,128)(2,1)} %bitcast.604), channel_id=1, source_target_pairs={{0,2},{1,3},{2,0},{3,1},{4,6},{5,7},{6,4},{7,5},{8,10},{9,11},{10,... | collective-permute-start | bytes 786440 | tf_op jit(solution)/shard_map/ppermute | solution.py:257
  937.7 295.1 %all-reduce.3.cloned.1.call-start = ((), (), s32[]{:S(2)}) async-start(), calls=%async_computation.20 | async-start | bytes 15384576 | tf_op jit(solution)/shard_map/psum | solution.py:430
  950.7 45.5 %collective-permute-start.33 = (bf16[16,64,128]{2,1,0:T(8,128)(2,1)}, bf16[16,64,128]{2,1,0:T(8,128)(2,1)}, u32[]{:S(2)}, u32[]{:S(2)}) collective-permute-start(bf16[16,64,128]{2,1,0:T(8,128)(2,1)} %get-tuple-element.106), channel_id=1, source_target_pairs={{0,1},{1,2},{2,3},{3,0},{4,5},{5,6},{6,7},{7,4},{8,9},{9,10},{10,1... | collective-permute-start | bytes 786440 | tf_op jit(solution)/shard_map/ppermute | solution.py:257
  951.3 58.2 %collective-permute-start.34 = (bf16[16,64,128]{2,1,0:T(8,128)(2,1)}, bf16[16,64,128]{2,1,0:T(8,128)(2,1)}, u32[]{:S(2)}, u32[]{:S(2)}) collective-permute-start(bf16[16,64,128]{2,1,0:T(8,128)(2,1)} %get-tuple-element.107), channel_id=1, source_target_pairs={{0,2},{1,3},{2,0},{3,1},{4,6},{5,7},{6,4},{7,5},{8,10},{9,11},{10,... | collective-permute-start | bytes 786440 | tf_op jit(solution)/shard_map/ppermute | solution.py:257
  958.9 50.6 %collective-permute-start.35 = (bf16[16,64,128]{2,1,0:T(8,128)(2,1)}, bf16[16,64,128]{2,1,0:T(8,128)(2,1)}, u32[]{:S(2)}, u32[]{:S(2)}) collective-permute-start(bf16[16,64,128]{2,1,0:T(8,128)(2,1)} %copy-done.49), channel_id=1, source_target_pairs={{0,3},{1,0},{2,1},{3,2},{4,7},{5,4},{6,5},{7,6},{8,11},{9,8},{10,9... | collective-permute-start | bytes 786440 | tf_op jit(solution)/shard_map/ppermute | solution.py:257
  970.6 61.7 %collective-permute-start.45 = (bf16[16,64,128]{2,1,0:T(8,128)(2,1)}, bf16[16,64,128]{2,1,0:T(8,128)(2,1)S(1)}, u32[]{:S(2)}, u32[]{:S(2)}) collective-permute-start(bf16[16,64,128]{2,1,0:T(8,128)(2,1)} %get-tuple-element.118), channel_id=1, source_target_pairs={{0,1},{1,2},{2,3},{3,0},{4,5},{5,6},{6,7},{7,4},{8,9},{9,10},{10,1... | collective-permute-start | bytes 786440 | tf_op jit(solution)/shard_map/ppermute | solution.py:257
  971.7 77.6 %collective-permute-start.46 = (bf16[16,64,128]{2,1,0:T(8,128)(2,1)}, bf16[16,64,128]{2,1,0:T(8,128)(2,1)}, u32[]{:S(2)}, u32[]{:S(2)}) collective-permute-start(bf16[16,64,128]{2,1,0:T(8,128)(2,1)} %get-tuple-element.119), channel_id=1, source_target_pairs={{0,2},{1,3},{2,0},{3,1},{4,6},{5,7},{6,4},{7,5},{8,10},{9,11},{10,... | collective-permute-start | bytes 786440 | tf_op jit(solution)/shard_map/ppermute | solution.py:257
  996.2 54.9 %collective-permute-start.47 = (bf16[16,64,128]{2,1,0:T(8,128)(2,1)}, bf16[16,64,128]{2,1,0:T(8,128)(2,1)S(1)}, u32[]{:S(2)}, u32[]{:S(2)}) collective-permute-start(bf16[16,64,128]{2,1,0:T(8,128)(2,1)} %copy-done.48), channel_id=1, source_target_pairs={{0,3},{1,0},{2,1},{3,2},{4,7},{5,4},{6,5},{7,6},{8,11},{9,8},{10,9... | collective-permute-start | bytes 786440 | tf_op jit(solution)/shard_map/ppermute | solution.py:257
  1009.5 59.2 %collective-permute-start.51 = (bf16[16,64,128]{2,1,0:T(8,128)(2,1)S(1)}, bf16[16,64,128]{2,1,0:T(8,128)(2,1)S(1)}, u32[]{:S(2)}, u32[]{:S(2)}) collective-permute-start(bf16[16,64,128]{2,1,0:T(8,128)(2,1)S(1)} %copy-done.47), channel_id=1, source_target_pairs={{0,1},{1,2},{2,3},{3,0},{4,5},{5,6},{6,7},{7,4},{8,9},{9,10},{10,1... | collective-permute-start | bytes 786440 | tf_op jit(solution)/shard_map/ppermute | solution.py:257
  1009.5 70.4 %collective-permute-start.52 = (bf16[16,64,128]{2,1,0:T(8,128)(2,1)S(1)}, bf16[16,64,128]{2,1,0:T(8,128)(2,1)S(1)}, u32[]{:S(2)}, u32[]{:S(2)}) collective-permute-start(bf16[16,64,128]{2,1,0:T(8,128)(2,1)S(1)} %copy-done.45), channel_id=1, source_target_pairs={{0,2},{1,3},{2,0},{3,1},{4,6},{5,7},{6,4},{7,5},{8,10},{9,11},{10,... | collective-permute-start | bytes 786440 | tf_op jit(solution)/shard_map/ppermute | solution.py:257
  1032.3 47.6 %collective-permute-start.53 = (bf16[16,64,128]{2,1,0:T(8,128)(2,1)S(1)}, bf16[16,64,128]{2,1,0:T(8,128)(2,1)S(1)}, u32[]{:S(2)}, u32[]{:S(2)}) collective-permute-start(bf16[16,64,128]{2,1,0:T(8,128)(2,1)S(1)} %get-tuple-element.126), channel_id=1, source_target_pairs={{0,3},{1,0},{2,1},{3,2},{4,7},{5,4},{6,5},{7,6},{8,11},{9,8},{10,9... | collective-permute-start | bytes 786440 | tf_op jit(solution)/shard_map/ppermute | solution.py:257
  1049.2 46.4 %collective-permute-start.57 = (bf16[16,64,128]{2,1,0:T(8,128)(2,1)S(1)}, bf16[16,64,128]{2,1,0:T(8,128)(2,1)}, u32[]{:S(2)}, u32[]{:S(2)}) collective-permute-start(bf16[16,64,128]{2,1,0:T(8,128)(2,1)S(1)} %get-tuple-element.130), channel_id=1, source_target_pairs={{0,1},{1,2},{2,3},{3,0},{4,5},{5,6},{6,7},{7,4},{8,9},{9,10},{10,1... | collective-permute-start | bytes 786440 | tf_op jit(solution)/shard_map/ppermute | solution.py:257
  1051.1 44.6 %collective-permute-start.58 = (bf16[16,64,128]{2,1,0:T(8,128)(2,1)S(1)}, bf16[16,64,128]{2,1,0:T(8,128)(2,1)}, u32[]{:S(2)}, u32[]{:S(2)}) collective-permute-start(bf16[16,64,128]{2,1,0:T(8,128)(2,1)S(1)} %get-tuple-element.131), channel_id=1, source_target_pairs={{0,2},{1,3},{2,0},{3,1},{4,6},{5,7},{6,4},{7,5},{8,10},{9,11},{10,... | collective-permute-start | bytes 786440 | tf_op jit(solution)/shard_map/ppermute | solution.py:257
  (293 other events, 6378.0 us)
Sparse Core Ops, SparseCore 0:
  947.6 262.9 all-reduce.2

commit v2 on v0

v2 whole, which is shorter than its diff:
```python
import math

import jax
import jax.numpy as jnp
import numpy as np
from jax import lax
from jax.experimental import pallas as pl
from jax.experimental.pallas import tpu as pltpu
from jax.sharding import PartitionSpec as P

NLAT = 128
NLON = 256
L = 128
M = 96
Q = 2 * M
STEP = 3
LANES = 128

NORM_EPS = 1e-06
FIRST_EPS = 1e-30
SECOND_EPS = 0.001
CLIP_LEVEL = 0.5
STEP_RATE = 0.5
F32 = jnp.float32
LOW = jnp.bfloat16
VMEM_LIMIT = 60 * 1024 * 1024


def legendre_table():
    angles = math.pi * (np.arange(NLAT) + 0.5) / NLAT
    cosine, sine = np.cos(angles), np.sin(angles)
    table = np.zeros((M, L, NLAT))
    for m in range(M):
        factors = np.arange(1, m + 1)
        scale = math.sqrt(0.5 * np.prod((2.0 * factors + 1.0) / (2.0 * factors)))
        table[m, m] = scale * sine**m
        for l in range(m + 1, L):
            a = math.sqrt((4.0 * l * l - 1.0) / (l * l - m * m))
            b = math.sqrt(((l - 1.0) ** 2 - m * m) / (4.0 * (l - 1.0) ** 2 - 1.0))
            earlier = table[m, l - 2] if l >= m + 2 else 0.0
            table[m, l] = a * (cosine * table[m, l - 1] - b * earlier)
    return table, math.pi / NLAT * sine


def dft_tables():
    phases = 2.0 * math.pi * (np.outer(np.arange(NLON), np.arange(M)) % NLON) / NLON
    cosine, sine = np.cos(phases), np.sin(phases)
    doubling = np.where(np.arange(M) == 0, 1.0, 2.0)
    forward = np.stack([cosine, -sine], axis=2).reshape(NLON, Q) / NLON
    inverse = np.stack([doubling * cosine, -doubling * sine], axis=2).reshape(NLON, Q).T
    return forward, inverse


EXTRA = 16


def point_masks(n, points):
    row_of = lax.broadcasted_iota(jnp.int32, (n, EXTRA), 0) // points
    sel = (row_of == lax.broadcasted_iota(jnp.int32, (n, EXTRA), 1)).astype(F32).astype(LOW)
    place = lax.broadcasted_iota(jnp.int32, (n, LANES), 0) % points
    lane = lax.broadcasted_iota(jnp.int32, (n, LANES), 1)
    return sel, place == lane, lane == 0


def load_points(ref, n, points):
    tiles = ref.shape[0] // n
    sel, diagonal, first = point_masks(n, points)
    extra = jnp.dot(sel, ref[tiles * n : tiles * n + EXTRA, :], preferred_element_type=F32)
    column = jnp.sum(jnp.where(diagonal, extra, 0.0), axis=1, keepdims=True)
    pieces = [ref[t * n : (t + 1) * n, :].astype(F32) for t in range(tiles)]
    return jnp.concatenate([*pieces, jnp.where(first, column, 0.0)], axis=1)


def store_points(ref, values, last, points):
    n = values.shape[0]
    tiles = ref.shape[0] // n
    _, diagonal, _ = point_masks(n, points)
    for t in range(tiles):
        ref[t * n : (t + 1) * n, :] = values[:, t * LANES : (t + 1) * LANES]
    spread = jnp.where(diagonal, last, 0.0).astype(LOW)
    row_of = lax.broadcasted_iota(jnp.int32, (EXTRA, n), 1) // points
    pick = (row_of == lax.broadcasted_iota(jnp.int32, (EXTRA, n), 0)).astype(F32).astype(LOW)
    ref[tiles * n : tiles * n + EXTRA, :] = jnp.dot(
        pick, spread, preferred_element_type=F32
    ).astype(LOW)


def params():
    return pltpu.CompilerParams(vmem_limit_bytes=VMEM_LIMIT)


def cost(flops, size, transcendentals=0):
    return pl.CostEstimate(flops=1024, bytes_accessed=400_000_000, transcendentals=0)


def fixed(array):
    zeros = (0,) * len(array.shape)
    return pl.BlockSpec(array.shape, lambda *_: zeros)


def once(array):
    zeros = (0,) * len(array.shape)
    return pl.BlockSpec(array.shape, lambda *_: zeros, pipeline_mode=pl.Buffered(1))


def slot_table(table, count):
    return pl.BlockSpec(
        (1, *table.shape[1:]), lambda s, me_ref: ((me_ref[0] + (count - s)) % count, 0, 0)
    )


def pack(me, source, chunk, depth, count):
    _, _, points, channels = source.shape
    n = depth * points
    tiles = channels // LANES

    def kernel(me_ref, source_ref, *outs):
        step = pl.program_id(0)
        values = source_ref[0].reshape(n, channels)
        last = values[:, tiles * LANES :].astype(F32)
        for s, out in enumerate(outs):

            @pl.when(step == s)
            def _():
                store_points(out, values, last, points)

    shape = jax.ShapeDtypeStruct((tiles * n + EXTRA, LANES), LOW)
    return pl.pallas_call(
        kernel,
        out_shape=[shape] * count,
        grid_spec=pltpu.PrefetchScalarGridSpec(
            num_scalar_prefetch=1,
            grid=(count,),
            in_specs=[
                pl.BlockSpec(
                    (1, depth, points, channels),
                    lambda s, me_ref: ((me_ref[0] + s) % count, chunk, 0, 0),
                )
            ],
            out_specs=[fixed(shape)] * count,
        ),
        compiler_params=params(),
        cost_estimate=cost(0, 4 * count * n * channels),
        name="pack",
    )(me, source)


def unpack(me, slots, target, chunk, depth, shape, dtype):
    members, rows, points, channels = shape
    n = depth * points
    count = len(slots)

    def kernel(me_ref, *refs):
        out = refs[-1]
        step = pl.program_id(0)
        for s in range(count):

            @pl.when(step == s)
            def _():
                values = load_points(refs[s], n, points)[:, :channels]
                out[0] = values.astype(dtype).reshape(depth, points, channels)

    specs = [fixed(s) for s in slots]
    arrays = list(slots)
    aliases = {}
    if target is not None:
        specs.append(pl.BlockSpec(memory_space=pl.ANY))
        arrays.append(target)
        aliases = {count + 1: 0}
    return pl.pallas_call(
        kernel,
        out_shape=jax.ShapeDtypeStruct(shape, dtype),
        grid_spec=pltpu.PrefetchScalarGridSpec(
            num_scalar_prefetch=1,
            grid=(count,),
            in_specs=specs,
            out_specs=pl.BlockSpec(
                (1, depth, points, channels),
                lambda s, me_ref: ((me_ref[0] + s) % count, chunk, 0, 0),
            ),
        ),
        input_output_aliases=aliases,
        compiler_params=params(),
        cost_estimate=cost(0, 6 * count * n * channels),
        name="unpack",
    )(me, *arrays)


def first_forward(me, table, slots, offset, gain, depth, points, channels):
    n = depth * points
    count = len(slots)

    def kernel(me_ref, table_ref, offset_ref, gain_ref, *refs):
        out, total = refs[-2:]
        for s, slot in enumerate(refs[:-2]):
            shifted = load_points(slot, n, points) + offset_ref[...]
            square = jnp.sum(shifted * shifted, axis=1, keepdims=True)
            scale = lax.rsqrt(square * (1.0 / channels) + NORM_EPS)
            normed = (shifted * scale * gain_ref[...]).astype(LOW)
            owner = (me_ref[0] + (count - s)) % count
            part = jnp.dot(table_ref[owner], normed, preferred_element_type=F32)
            if s == 0:
                total[...] = part
            else:
                total[...] += part
        out[...] = total[...].astype(LOW)

    width = gain.shape[1]
    size = table.shape[1]
    arrays = [table, offset, gain, *slots]
    shape = jax.ShapeDtypeStruct((size, width), LOW)
    return pl.pallas_call(
        kernel,
        out_shape=shape,
        grid_spec=pltpu.PrefetchScalarGridSpec(
            num_scalar_prefetch=1,
            grid=(1,),
            in_specs=[fixed(a) for a in arrays],
            out_specs=fixed(shape),
            scratch_shapes=[pltpu.VMEM((size, width), F32)],
        ),
        compiler_params=params(),
        cost_estimate=cost(2 * size * count * n * width, 6 * 1024 * 1024),
        name="first_forward",
    )(me, *arrays)


def degree_blocks(refs, counts, lat, step, groups):
    for ref, count in zip(refs, counts):
        size = ref.shape[0]
        if groups == 1 and count == 1:
            yield ref, slice(0, size)
            continue
        part = size // lat // count // groups
        for c in range(count):
            for i in range(lat):
                start = (i * count + c) * (part * groups) + step * part
                yield ref, pl.ds(pl.multiple_of(start, part), part)


def degree_tables(to_ref, back_ref, spots_ref, spots_back_ref, each):
    group = spots_ref.shape[0]
    to = [
        jnp.dot(to_ref[q // each], spots_ref[q], preferred_element_type=F32).astype(LOW)
        for q in range(group)
    ]
    back = [
        jnp.dot(spots_back_ref[q], back_ref[q // each], preferred_element_type=F32).astype(LOW)
        for q in range(group)
    ]
    return jnp.concatenate(to, axis=0), jnp.concatenate(back, axis=1)


def filter_call(kernel, name, first, tables, spots, response, extra, spectra, each, groups, outs):
    part = tables[0].shape[0]
    block = spots[0].shape[0] // each
    tabled = pl.BlockSpec((block, L, NLAT), lambda g, first: (first[0] + g, 0, 0))
    grouped = lambda a: pl.BlockSpec((1, *a.shape[1:]), lambda g, first: (g, 0, 0))
    spec = lambda a: grouped(a) if len(a.shape) == 3 else fixed(a)
    arrays = [*tables, *spots, response, *extra, *spectra]
    return pl.pallas_call(
        kernel,
        out_shape=outs,
        grid_spec=pltpu.PrefetchScalarGridSpec(
            num_scalar_prefetch=1,
            grid=(groups,),
            in_specs=[tabled, tabled, fixed(spots[0]), fixed(spots[1]), fixed(response)]
            + [spec(a) for a in (*extra, *spectra)],
            out_specs=[spec(o) for o in outs],
        ),
        compiler_params=params(),
        cost_estimate=cost(16 * part, 24 * 1024 * 1024),
        name=name,
    )(first, *arrays)


def filter_forward(
    first, tables, spots, response, spectra, counts, out_counts, lat, each, groups
):
    size = spots[0].shape[2]
    width = response.shape[1]
    count = len(spectra)

    def kernel(first_ref, to_ref, back_ref, spots_ref, spots_back_ref, response_ref, *refs):
        step = pl.program_id(0)
        ins, outs, coefs = refs[:count], refs[count:-1], refs[-1]
        to, back = degree_tables(to_ref, back_ref, spots_ref, spots_back_ref, each)
        values = jnp.concatenate(
            [ref[rows, :] for ref, rows in degree_blocks(ins, counts, lat, step, groups)], axis=0
        )
        coef = jnp.dot(to, values, preferred_element_type=F32)
        coefs[0] = coef
        scale = jnp.concatenate([response_ref[...]] * (size // L), axis=0)
        filtered = (scale * coef).astype(LOW)
        result = jnp.dot(back, filtered, preferred_element_type=F32).astype(LOW)
        begin = 0
        for ref, rows in degree_blocks(outs, out_counts, lat, step, groups):
            length = rows.stop if isinstance(rows, slice) else rows.size
            ref[rows, :] = result[begin : begin + length]
            begin += length

    height = sum(s.shape[0] for s in spectra) // sum(counts)
    outs = [jax.ShapeDtypeStruct((height * c, width), LOW) for c in out_counts]
    outs.append(jax.ShapeDtypeStruct((groups, size, width), F32))
    return filter_call(
        kernel, "filter_forward", first, tables, spots, response, (), spectra, each, groups, outs
    )


def filter_backward(
    first, tables, spots, response, coefs, spectra, counts, out_counts, lat, each, groups
):
    size = spots[0].shape[2]
    width = response.shape[1]
    count = len(spectra)

    def kernel(
        first_ref, to_ref, back_ref, spots_ref, spots_back_ref, response_ref, coefs_ref, *refs
    ):
        step = pl.program_id(0)
        ins, outs, grad_ref = refs[:count], refs[count:-1], refs[-1]
        to, back = degree_tables(to_ref, back_ref, spots_ref, spots_back_ref, each)
        values = jnp.concatenate(
            [ref[rows, :] for ref, rows in degree_blocks(ins, counts, lat, step, groups)], axis=0
        )
        upstream = jnp.dot(to, values, preferred_element_type=F32)
        product = coefs_ref[0] * upstream
        grad = product[:L]
        for q in range(1, size // L):
            grad = grad + product[q * L : (q + 1) * L]

        @pl.when(step == 0)
        def _():
            grad_ref[...] = jnp.zeros_like(grad_ref)

        grad_ref[...] += grad
        scale = jnp.concatenate([response_ref[...]] * (size // L), axis=0)
        filtered = (scale * upstream).astype(LOW)
        result = jnp.dot(back, filtered, preferred_element_type=F32).astype(LOW)
        begin = 0
        for ref, rows in degree_blocks(outs, out_counts, lat, step, groups):
            length = rows.stop if isinstance(rows, slice) else rows.size
            ref[rows, :] = result[begin : begin + length]
            begin += length

    height = sum(s.shape[0] for s in spectra) // sum(counts)
    outs = [jax.ShapeDtypeStruct((height * c, width), LOW) for c in out_counts]
    outs.append(jax.ShapeDtypeStruct((L, width), F32))
    return filter_call(
        kernel,
        "filter_backward",
        first,
        tables,
        spots,
        response,
        (coefs,),
        spectra,
        each,
        groups,
        outs,
    )


def prepare_weights(weight_in, weight_out, width, hidden_width):
    channels, units = weight_in.shape

    def kernel(in_ref, out_ref, w_in, w_out, w_in_t, w_out_t):
        w_in[...] = jnp.zeros_like(w_in)
        w_out_t[...] = jnp.zeros_like(w_out_t)
        w_in[:channels, :units] = in_ref[...].astype(LOW)
        w_out_t[:channels, :units] = out_ref[...].astype(LOW)
        w_in_t[...] = w_in[...].T
        w_out[...] = w_out_t[...].T

    outs = [
        jax.ShapeDtypeStruct(shape, LOW)
        for shape in [(width, hidden_width), (hidden_width, width)] * 2
    ]
    outs = [outs[0], outs[1], outs[1], outs[0]]
    return pl.pallas_call(
        kernel, out_shape=outs, compiler_params=params(), name="prepare_weights"
    )(weight_in, weight_out.T)


def feed_forward(
    me, tables, weights, offset, gain, spectra, slots, upstreams, lat, depth, points, channels
):
    n = depth * points
    pair, count = len(slots), len(slots[0])
    flat = [slot for chunk in slots for slot in chunk]
    width, hidden_width = weights[0].shape
    size = spectra.shape[0] // pair
    part = size // lat
    inverse_channels = 1.0 / channels

    def kernel(
        me_ref, out_table, back_table, w_in, w_out, w_in_t, w_out_t, offset_ref, gain_ref, y, *refs
    ):
        ins, ups = refs[: pair * count], refs[pair * count : (pair + 1) * count]
        refs = refs[(pair + 1) * count :]
        outs = refs[:count]
        grad_ref, second_ref, active_ref, pre_ref, cot_ref, gain_part, back_ref = refs[count:-4]
        x_now, up_now, y_now, total = refs[-4:]
        step = pl.program_id(0)

        @pl.when(step == 0)
        def _():
            gain_part[...] = jnp.zeros_like(gain_part)
            total[...] = jnp.zeros_like(total)
            for c in range(pair):
                for i in range(lat):
                    y_now[c, i * part : (i + 1) * part] = y[
                        (i * pair + c) * part : (i * pair + c + 1) * part
                    ]

        for s in range(count):

            @pl.when(step == s)
            def _():
                for c in range(pair):
                    x_now[c] = ins[c * count + s][...]
                up_now[...] = ups[s][...]

        rows = lambda parts: jnp.concatenate(parts, axis=0) if pair > 1 else parts[0]
        branch = rows(
            [
                jnp.dot(out_table[0], y_now[c], preferred_element_type=F32).astype(LOW)
                for c in range(pair)
            ]
        )
        shifted = rows([load_points(x_now.at[c], n, points) for c in range(pair)])
        hidden = shifted + offset_ref[...] + branch.astype(F32)
        square = jnp.sum(hidden * hidden, axis=1, keepdims=True)
        scale = lax.rsqrt(square * inverse_channels + NORM_EPS)
        second = (hidden * scale * gain_ref[...]).astype(LOW)
        second_ref[...] = second
        upstream = load_points(up_now, pair * n, points)
        upstream_low = upstream.astype(LOW)
        cot_ref[...] = upstream_low
        preact = jnp.dot(second, w_in[...], preferred_element_type=F32)
        back_active = jnp.dot(upstream_low, w_out_t[...], preferred_element_type=F32)
        share = 0.5 + 0.5 * lax.erf(preact * math.sqrt(0.5))
        density = jnp.exp(-0.5 * preact * preact) * (1.0 / math.sqrt(2.0 * math.pi))
        active = (preact * share).astype(LOW)
        active_ref[...] = active
        back_preact = (back_active * (share + preact * density)).astype(LOW)
        pre_ref[...] = back_preact
        output = hidden + jnp.dot(active, w_out[...], preferred_element_type=F32)
        back_second = jnp.dot(back_preact, w_in_t[...], preferred_element_type=F32)
        scaled = back_second * gain_ref[...]
        inner = jnp.sum(hidden * scaled, axis=1, keepdims=True) * inverse_channels
        grad = scale * scaled - hidden * (scale * scale * scale * inner) + upstream
        grad_ref[...] = grad
        grad_low = grad.astype(LOW)
        for c in range(pair):
            total[c] += jnp.dot(
                back_table[0], grad_low[c * n : (c + 1) * n], preferred_element_type=F32
            )
        gain_part[...] += jnp.sum(
            (back_second * (hidden * scale)).reshape(pair * n // 8, 8, width), axis=0
        )

        @pl.when(step == count - 1)
        def _():
            for c in range(pair):
                for i in range(lat):
                    back_ref[(i * pair + c) * part : (i * pair + c + 1) * part] = total[
                        c, i * part : (i + 1) * part
                    ].astype(LOW)

        store_points(up_now, output.astype(LOW), output[:, channels - 1 : channels], points)
        for s in range(count):

            @pl.when(step == s)
            def _():
                outs[s][...] = up_now[...]

    rows = lambda w: pl.BlockSpec((pair * n, w), lambda s, me_ref: (s, 0))
    slot = jax.ShapeDtypeStruct(upstreams[0].shape, LOW)
    height = count * pair * n
    outs = [slot] * count + [
        jax.ShapeDtypeStruct((height, width), F32),
        jax.ShapeDtypeStruct((height, width), LOW),
        jax.ShapeDtypeStruct((height, hidden_width), LOW),
        jax.ShapeDtypeStruct((height, hidden_width), LOW),
        jax.ShapeDtypeStruct((height, width), LOW),
        jax.ShapeDtypeStruct((8, width), F32),
        jax.ShapeDtypeStruct(spectra.shape, LOW),
    ]
    out_specs = [fixed(slot)] * count + [
        rows(width),
        rows(width),
        rows(hidden_width),
        rows(hidden_width),
        rows(width),
        fixed(outs[-2]),
        fixed(outs[-1]),
    ]
    arrays = [*tables, *weights, offset, gain, spectra, *flat, *upstreams]
    return pl.pallas_call(
        kernel,
        out_shape=outs,
        grid_spec=pltpu.PrefetchScalarGridSpec(
            num_scalar_prefetch=1,
            grid=(count,),
            in_specs=[slot_table(t, count) for t in tables] + [once(a) for a in arrays[2:]],
            out_specs=out_specs,
            scratch_shapes=[
                pltpu.VMEM((pair, *flat[0].shape), LOW),
                pltpu.VMEM(slot.shape, LOW),
                pltpu.VMEM((pair, size, width), LOW),
                pltpu.VMEM((pair, size, width), F32),
            ],
        ),
        compiler_params=params(),
        cost_estimate=cost(0, 0),
        name="feed_forward",
    )(me, *arrays)


def first_backward(
    me, table, spectra, slots, grads, place, pair, offset, gain, depth, points, channels
):
    n = depth * points
    count = len(slots)
    width = gain.shape[1]
    inverse_channels = 1.0 / channels

    def kernel(me_ref, table_ref, y, grad_ref, offset_ref, gain_ref, *refs):
        ins, outs, now = refs[:count], refs[count:-1], refs[-1]
        step = pl.program_id(0)
        for s in range(count):

            @pl.when(step == s)
            def _():
                now[...] = ins[s][...]

        back = jnp.dot(table_ref[0], y[...], preferred_element_type=F32).astype(LOW).astype(F32)
        shifted = load_points(now, n, points) + offset_ref[...]
        square = jnp.sum(shifted * shifted, axis=1, keepdims=True)
        scale = lax.rsqrt(square * inverse_channels + NORM_EPS)
        scaled = back * gain_ref[...]
        inner = jnp.sum(shifted * scaled, axis=1, keepdims=True) * inverse_channels
        result = grad_ref[...] + scale * scaled - shifted * (scale * scale * scale * inner)
        store_points(now, result.astype(LOW), result[:, channels - 1 : channels], points)
        for s in range(count):

            @pl.when(step == s)
            def _():
                outs[s][...] = now[...]

    slot = jax.ShapeDtypeStruct(slots[0].shape, LOW)
    outs = [slot] * count
    return pl.pallas_call(
        kernel,
        out_shape=outs,
        grid_spec=pltpu.PrefetchScalarGridSpec(
            num_scalar_prefetch=1,
            grid=(count,),
            in_specs=[
                slot_table(table, count),
                fixed(spectra),
                pl.BlockSpec((n, width), lambda s, me_ref: (s * pair + place, 0)),
                fixed(offset),
                fixed(gain),
            ]
            + [fixed(s) for s in slots],
            out_specs=[fixed(o) for o in outs],
            scratch_shapes=[pltpu.VMEM(slot.shape, LOW)],
        ),
        compiler_params=params(),
        cost_estimate=cost(2 * count * n * width * spectra.shape[0], 12 * 1024 * 1024),
        name="first_backward",
    )(me, table, spectra, grads, offset, gain, *slots)


def adafactor_matrix(weight_now, gradient, rows_old, columns_old, decay_rate):
    squares = gradient * gradient + FIRST_EPS
    rows_new = decay_rate * rows_old + (1.0 - decay_rate) * jnp.mean(squares, axis=1)
    columns_new = decay_rate * columns_old + (1.0 - decay_rate) * jnp.mean(squares, axis=0)
    estimate = rows_new[:, None] * columns_new[None, :] / jnp.mean(rows_new)
    update = gradient * lax.rsqrt(estimate)
    update = update / jnp.maximum(1.0, jnp.sqrt(jnp.mean(update * update)) / CLIP_LEVEL)
    scale_now = STEP_RATE * jnp.maximum(SECOND_EPS, jnp.sqrt(jnp.mean(weight_now * weight_now)))
    return (weight_now - scale_now * update, rows_new, columns_new)


def adafactor_vector(weight_now, gradient, moments_old, decay_rate):
    moments_new = decay_rate * moments_old + (1.0 - decay_rate) * (gradient * gradient + FIRST_EPS)
    update = gradient * lax.rsqrt(moments_new)
    update = update / jnp.maximum(
        1.0, jnp.sqrt(jnp.mean(update * update, axis=1, keepdims=True)) / CLIP_LEVEL
    )
    scale_now = STEP_RATE * jnp.maximum(
        SECOND_EPS, jnp.sqrt(jnp.mean(weight_now * weight_now, axis=1, keepdims=True))
    )
    return (weight_now - scale_now * update, moments_new)


def tie(*groups):
    return lax.optimization_barrier(groups)


def take(array, index):
    return lax.dynamic_index_in_dim(array, index, 0, keepdims=False)


def chunk_rows(rows):
    return rows // 4 if rows % 4 == 0 else rows


def group_size(share, depth):
    for size in range(1, share):
        if share % size == 0 and size * depth % 16 == 0:
            return size
    return share


def body(
    fields_in,
    cotangent,
    member_dates,
    date_table,
    norm_gains,
    spectral_filter,
    weight_in,
    weight_out,
    gain_moments,
    in_row_stats,
    in_column_stats,
    out_row_stats,
    out_column_stats,
    filter_row_stats,
    filter_column_stats,
):
    members, rows, points, channels = fields_in.shape
    units = weight_in.shape[1]
    width = -(-channels // LANES) * LANES
    hidden_width = -(-units // LANES) * LANES
    lat, lon = lax.axis_size("lat"), lax.axis_size("lon")
    lat_me, lon_me = lax.axis_index("lat"), lax.axis_index("lon")
    me = lon_me.astype(jnp.int32).reshape(1)
    share = Q // lat
    depth = chunk_rows(rows)
    chunks = rows // depth
    pair = 2 if chunks % 2 == 0 else 1
    mids = chunks // pair
    n = depth * points

    def wider(array, *sizes):
        return jnp.pad(array, [(0, s - d) for s, d in zip(sizes, array.shape)])

    def exchange_lon(name, slots, sign):
        with jax.named_scope(name):
            return [
                slot
                if s == 0
                else lax.ppermute(slot, "lon", [(i, (i + sign * s) % lon) for i in range(lon)])
                for s, slot in enumerate(slots)
            ]

    def exchange_lat(name, *spectra):
        blocks = [a.reshape(lat, -1, width) for a in spectra]
        blocks = jnp.concatenate(blocks, axis=1) if len(blocks) > 1 else blocks[0]
        with jax.named_scope(name):
            blocks = lax.all_to_all(blocks, "lat", split_axis=0, concat_axis=0, tiled=True)
        return blocks.reshape(-1, width)

    inside = lat_me < lat

    def unit(function, *arrays):
        shapes = jax.eval_shape(function, *arrays)
        blank = lambda *_: jax.tree.map(lambda a: jnp.zeros(a.shape, a.dtype), shapes)
        return lax.cond(inside, function, blank, *arrays)

    def spread(values):
        height = -(-values.shape[0] // (8 * lat)) * 8
        return wider(values, height * lat, values.shape[1])

    def gathered(part):
        return exchange_lat("gather", jnp.broadcast_to(part[None], (lat, *part.shape)))

    forward, inverse = dft_tables()

    def by_device(table):
        blocks = table.reshape(lon, points, Q).transpose(0, 2, 1)
        return np.einsum("zqk,ab->zqabk", blocks, np.eye(depth)).reshape(lon, Q * depth, n)

    analysis = jnp.asarray(by_device(forward), LOW)
    back_analysis = jnp.asarray(by_device(inverse.T), LOW)
    synthesis = jnp.asarray(by_device(inverse.T).transpose(0, 2, 1), LOW)
    back_synthesis = jnp.asarray(by_device(forward).transpose(0, 2, 1), LOW)

    legendre, quadrature = legendre_table()
    group = group_size(share, depth)
    groups = share // group
    places = np.arange(NLAT).reshape(lat, chunks, depth).transpose(1, 0, 2)
    spots = np.zeros((group, NLAT, chunks, lat, group, depth))
    for q in range(group):
        for c in range(chunks):
            for i in range(lat):
                spots[q, places[c, i], c, i, q, np.arange(depth)] = 1.0
    spots = spots.reshape(group, NLAT, group * NLAT)
    spots = (jnp.asarray(spots, LOW), jnp.asarray(spots.transpose(0, 2, 1), LOW))
    each = 2 if group % 2 == 0 else 1
    first = (lat_me * groups if each == 2 else 0 * lat_me).astype(jnp.int32).reshape(1)

    def own_degrees(table):
        table = jnp.asarray(table, LOW)
        if each == 2:
            return table
        own_q = (lat_me * share + jnp.arange(share, dtype=jnp.int32)) // 2
        return jnp.take(table, own_q, axis=0)

    plain = own_degrees(legendre)
    weighted = own_degrees(legendre * quadrature)
    plain_back = own_degrees(legendre.transpose(0, 2, 1))
    weighted_back = own_degrees((legendre * quadrature).transpose(0, 2, 1))

    date_selector = (
        member_dates[:, None] == jnp.arange(date_table.shape[0], dtype=jnp.int32)[None, :]
    ).astype(F32)
    offsets = jnp.dot(date_selector, date_table, precision=lax.Precision.HIGHEST)
    offset = wider(take(offsets, lon_me)[None], 1, width)
    gain_one = wider(norm_gains[:1], 1, width)
    gain_two = wider(norm_gains[1:], 1, width)
    response = wider(spectral_filter, L, width)
    fields = [pack(me, fields_in, c, depth, lon) for c in range(chunks)]
    upstreams = [None] * mids
    waiting = [(f"fields_{c}", fields, c) for c in range(chunks)]
    waiting += [(f"upstream_{c}", upstreams, c) for c in range(mids)]

    def send_next(after):
        if not waiting or waiting[0][1][waiting[0][2]] is None:
            return after
        name, packs, c = waiting.pop(0)
        after, slots = tie(after, packs[c])
        packs[c] = exchange_lon(name, slots, 1)
        return after

    fields[0] = exchange_lon("fields_0", fields[0], 1)
    del waiting[0]
    fields[0], fields[1:], offset, gain_one, gain_two, response = tie(
        fields[0], fields[1:], offset, gain_one, gain_two, response
    )

    spectra = []
    for c in range(chunks):

        def to_spectra(cotangent, *slots):
            rows_now = first_forward(me, analysis, slots, offset, gain_one, depth, points, channels)
            rows_now = exchange_lat(f"spectra_{c}", rows_now)
            return rows_now, [pack(me, a, c, depth * pair, lon) for a in cotangent]

        if c > 0:
            fields[c], spectra[c - 1] = tie(fields[c], spectra[c - 1])
        fields[c] = send_next(fields[c])
        rows_now, packed = unit(to_spectra, [cotangent] if c < mids else [], *fields[c])
        upstreams[c : c + 1] = packed if c < mids else upstreams[c : c + 1]
        spectra.append(rows_now)

    def to_coefficients(weight_in, weight_out, *spectra):
        *values, coefs = filter_forward(
            first,
            (weighted, plain_back),
            spots,
            response,
            spectra,
            [1] * chunks,
            [pair] * mids,
            lat,
            each,
            groups,
        )
        values[0] = exchange_lat("synthesis_0", values[0])
        return values, coefs, prepare_weights(weight_in, weight_out, width, hidden_width)

    spectra[-1] = send_next(spectra[-1])
    values, coefs, weights = unit(to_coefficients, weight_in, weight_out, *spectra)

    backs, grads, parts, outputs = [], [], [], []
    gain_parts = []
    for c in range(mids):

        def step(spectrum, slots, upstream, following, before):
            out = feed_forward(
                me,
                (synthesis, back_analysis),
                weights,
                offset,
                gain_two,
                spectrum,
                slots,
                upstream,
                lat,
                depth,
                points,
                channels,
            )
            following = [exchange_lat(f"synthesis_{c + 1}", a) for a in following]
            before = [exchange_lat(f"back_synthesis_{c - 1}", a) for a in before]
            return out, following, before

        out, values[c + 1 : c + 2], backs[c - 1 : c] = unit(
            step,
            values[c],
            fields[c * pair : (c + 1) * pair],
            upstreams[c],
            values[c + 1 : c + 2],
            backs[c - 1 : c],
        )
        outputs.append(exchange_lon(f"output_{c}", out[:lon], -1))
        grads.append(out[lon])
        parts.append(tuple(out[lon + 1 : lon + 5]))
        gain_parts.append(out[lon + 5])
        backs.append(out[lon + 6])

    def to_gradients(before, late, coefs, parts, gain_parts):
        late = exchange_lat(f"back_synthesis_{mids - 1}", late)
        weight_part = None
        for second, active, pre, cot in parts:
            terms = (
                jnp.einsum("gc,gh->ch", second, pre, preferred_element_type=F32),
                jnp.einsum("gc,gh->ch", cot, active, preferred_element_type=F32),
            )
            weight_part = terms if weight_part is None else tuple(map(jnp.add, weight_part, terms))
        *values, filter_part = filter_backward(
            first,
            (plain, weighted_back),
            spots,
            response,
            coefs,
            [*before, late],
            [pair] * mids,
            [1] * chunks,
            lat,
            each,
            groups,
        )
        gain_part = sum(jnp.sum(a, axis=0) for a in gain_parts)
        small = spread(jnp.concatenate([filter_part, gain_part[None]], axis=0))
        return values, small, weight_part

    outputs[:-1], backs[-1] = tie(outputs[:-1], backs[-1])
    values, small, weight_part = unit(
        to_gradients, backs[:-1], backs[-1], coefs, parts, gain_parts
    )
    outputs[-1], values[0] = tie(outputs[-1], values[0])
    values[0] = unit(lambda a: exchange_lat("back_spectra_0", a), values[0])

    gradients = []
    with jax.named_scope("weights_lat"):
        part = [
            lax.psum_scatter(a, "lat", scatter_dimension=0, tiled=True) for a in weight_part
        ]

    def sum_quarters(part):
        part = jnp.concatenate(part, axis=0)
        quarters = part.reshape(lon, -1, hidden_width)
        pieces = [take(quarters, (lon_me + s) % lon).astype(LOW) for s in range(lon)]
        return take(quarters, lon_me), exchange_lon("weights_sum", pieces, 1)[1:]

    def gather_quarters(own, pieces):
        own = (own + sum(piece.astype(F32) for piece in pieces)).astype(LOW)
        return exchange_lon("weights_gather", [own] * lon, 1)

    for c in range(chunks):
        if c == 2:
            gradients[0], part, values[2] = tie(gradients[0], part, values[2])
            quarters = sum_quarters(part)
        if c == 3:
            gradients[1], quarters, values[3] = tie(gradients[1], quarters, values[3])
            quarters = gather_quarters(*quarters)

        def to_input(spectrum, slots, grad, following, small):
            out = first_backward(
                me,
                back_synthesis,
                spectrum,
                slots,
                grad,
                c % pair,
                pair,
                offset,
                gain_one,
                depth,
                points,
                channels,
            )
            following = [exchange_lat(f"back_spectra_{c + 1}", a) for a in following]
            if c == chunks - 1:
                part = exchange_lat("small", small).reshape(lat, -1, width)
                small = jnp.sum(part, axis=0)
            return out, following, small

        following = values[c + 1 : c + 2] if c > 0 else []
        out, following, small = unit(
            to_input, values[c], fields[c], grads[c // pair], following, small
        )
        gradients.append(exchange_lon(f"input_grad_{c}", out, -1))
        if c > 0:
            values[c + 1 : c + 2] = following
        elif chunks > 1:
            values[1] = unit(lambda a: exchange_lat("back_spectra_1", a), values[1])

    if chunks < 4:
        quarters = gather_quarters(*sum_quarters(part))
    with jax.named_scope("small"):
        bit = 1
        while bit < lon:
            small = small + lax.ppermute(small, "lon", [(i, i ^ bit) for i in range(lon)])
            bit *= 2
    gradients[:-1], quarters, small = tie(gradients[:-1], quarters, small)
    small = unit(gathered, small)
    gradients[-1], small = tie(gradients[-1], small)

    block_output = input_grad = None
    for c in range(mids):
        block_output = unpack(me, outputs[c], block_output, c, depth * pair, fields_in.shape, LOW)
    for c in range(chunks):
        input_grad = unpack(me, gradients[c], input_grad, c, depth, fields_in.shape, F32)

    quarters = jnp.stack(quarters)
    part = jnp.concatenate([take(quarters, (lon_me - z) % lon) for z in range(lon)], axis=0)
    with jax.named_scope("weights_lat"):
        summed = lax.all_gather(part, "lat", axis=0, tiled=False).astype(F32)
    summed = summed.reshape(lat, 2, -1, hidden_width).swapaxes(0, 1).reshape(2, width, hidden_width)
    grad_weight_in = summed[0, :channels, :units]
    grad_weight_out = summed[1, :channels, :units].T
    grad_filter = small[:L, :channels]
    grad_one = jnp.sum(spectral_filter * grad_filter, axis=0) / norm_gains[0]
    grad_gains = jnp.stack([grad_one, small[L, :channels]])
    decay_rate = 1.0 - STEP ** (-0.8)
    new_weight_in, new_in_rows, new_in_columns = adafactor_matrix(
        weight_in, grad_weight_in, in_row_stats, in_column_stats, decay_rate
    )
    new_weight_out, new_out_rows, new_out_columns = adafactor_matrix(
        weight_out, grad_weight_out, out_row_stats, out_column_stats, decay_rate
    )
    new_filter, new_filter_rows, new_filter_columns = adafactor_matrix(
        spectral_filter, grad_filter, filter_row_stats, filter_column_stats, decay_rate
    )
    new_gains, new_moments = adafactor_vector(norm_gains, grad_gains, gain_moments, decay_rate)
    return (
        block_output,
        input_grad,
        grad_weight_in,
        grad_weight_out,
        grad_filter,
        grad_gains,
        new_weight_in,
        new_weight_out,
        new_filter,
        new_gains,
        new_in_rows,
        new_in_columns,
        new_out_rows,
        new_out_columns,
        new_filter_rows,
        new_filter_columns,
        new_moments,
    )


def solution(mesh):
    spread = P(None, "lat", "lon", None)
    return jax.shard_map(
        body,
        mesh=mesh,
        in_specs=(spread, spread) + (P(),) * 13,
        out_specs=(spread, spread) + (P(),) * 15,
        check_vma=False,
    )
```

time: 2710 us -> 726 us (0.27)
  waiting for transfers between devices: 1330 us -> 165 us
  local copies, waits for them, and re-layouts: 363 us -> 8.18 us
  matrix products: 281 us -> 36.4 us
  other arithmetic: 284 us -> 41.6 us
  blocking collectives: 326 us -> 101 us
  Pallas kernels: 0 us -> 217 us
  starting transfers between devices: 12.7 us -> 126 us
  loops' own time: 86.1 us -> 0.19 us
    reduce_scatter x2, waiting for transfers between devices: 847 us -> 0.02 us  [body(): lax.psum_scatter(a, 'lat', scatter_dimension=0, tiled=True)]
    all_gather x2 -> x1, waiting for transfers between devices: 312 us -> 0.01 us  [body(): summed = lax.all_gather(part, 'lat', axis=0, tiled=False).astype(F32)]
    dot_general x15 -> x5, matrix products: 281 us -> 36.4 us  [the longest x2 18.1 us: to_gradients(): jnp.einsum('gc,gh->ch', cot, active, preferred_element_type=F32)]
    pallas_call x0 -> x25, Pallas kernels: none -> 217 us  [the longest x2 82.7 us: feed_forward(): pl.pallas_call(kernel, out_shape=outs, grid_spec=pltpu.PrefetchScalarGrid...]
    all_to_all x2 -> x5, blocking collectives: 287 us -> 101 us  [exchange_lat(): lax.all_to_all(blocks, 'lat', split_axis=0, concat_axis=0, tiled=True)]
    psum x1 -> x0, waiting for transfers between devices: 170 us -> none  [body(): lax.psum((grad_in_part, grad_out_part, filter_part, jnp.stack([gain_one_p...]
    transpose x3 -> x0, local copies, waits for them, and re-layouts: 155 us -> none  [the longest x1 74.2 us: body(): jnp.einsum('qlj,bqjc->lbqc', portion, spectra_wide, precision=TABLE_PRECI...]
    ppermute x0 -> x44, waiting for transfers between devices: none -> 97.6 us  [the longest x42 96.4 us: exchange_lon(): lax.ppermute(slot, 'lon', [(i, (i + sign * s) % lon) for i in range(lon)])]
  transfers between devices with their start and end apart: 7 -> 56, of which waited for: 5 -> 16; matrix products, arithmetic and copies ran while one was open for 14% -> 7% of each run, Pallas kernels for 0% -> 28%
where the time goes in v2:
time: 726 us; the launch traced here: 717 us
  Pallas kernels  217 us (30%)
  waiting for transfers between devices  165 us (23%)
  starting transfers between devices  126 us (17%)
  blocking collectives  101 us (14%)
  other arithmetic  41.6 us (6%)
  matrix products  36.4 us (5%)
  between operations  21 us (3%)
  local copies, waits for them, and re-layouts  8.18 us (1%)
    all_to_all x5, blocking collectives, exchange_lat(): lax.all_to_all(blocks, 'lat', split_axis=0, concat_axis=0, tiled=True)  101 us
    ppermute x42, waiting for transfers between devices, exchange_lon(): lax.ppermute(slot, 'lon', [(i, (i + sign * s) % lon) for i in range(lon)])  96.4 us
    pallas_call x2, Pallas kernels, feed_forward(): pl.pallas_call(kernel, out_shape=outs, grid_spec=pltpu.PrefetchScalarGrid...  82.7 us
    ppermute x42, starting transfers between devices, exchange_lon(): lax.ppermute(slot, 'lon', [(i, (i + sign * s) % lon) for i in range(lon)])  74.4 us
    all_to_all x9, waiting for transfers between devices, exchange_lat(): lax.all_to_all(blocks, 'lat', split_axis=0, concat_axis=0, tiled=True)  67.2 us
    all_to_all x9, starting transfers between devices, exchange_lat(): lax.all_to_all(blocks, 'lat', split_axis=0, concat_axis=0, tiled=True)  44.5 us
    pallas_call x2, Pallas kernels, filter_call(): pl.pallas_call(kernel, out_shape=outs, grid_spec=pltpu.PrefetchScalarGrid...  28.6 us
    pallas_call x4, Pallas kernels, first_backward(): pl.pallas_call(kernel, out_shape=outs, grid_spec=pltpu.PrefetchScalarGrid...  28 us
  transfers between devices with their start and end apart: 56, of which 16 were waited for; matrix products, arithmetic and copies ran while one was open for 7% of the time, Pallas kernels for 28%

profile of v2, /device:TPU:0, one launch (start us, length us, event | category | flops | bytes accessed | tf_op | source)
XLA Modules:
  0.0 716.8 jit_solution(8123804744818088927)
XLA Ops:
  48.5 26.2 %conditional.15 = (bf16[768,768]{1,0:T(8,128)(2,1)}, bf16[2576,128]{1,0:T(8,128)(2,1)}, bf16[2576,128]{1,0:T(8,128)(2,1)}, bf16[2576,128]{1,0:T(8,128)(2,1)}, bf16[2576,128]{1,0:T(8,128)(2,1)}) conditional(s32[]{:T(128)} %convert_element_type.57, () %tuple.141, (s32[1]{0:T(128)}, bf16[4,768,256]{2,1,0:T(8,128)(2,1)S(1)}, f32[1,768]{1,0:T(1,128)S(1)}, ...), branch_computations={%region_0.1_spmd, %region_1.2_spmd} | conditional | flops 2048 | bytes 803539008 | solution.py:674
  62.9 11.9 %all-to-all-done = bf16[8,96,768]{2,1,0:T(8,128)(2,1)} async-done(((bf16[8,96,768]{2,1,0:T(8,128)(2,1)}), bf16[8,96,768]{2,1,0:T(8,128)(2,1)}, u32[]{:S(2)}, u32[]{:S(2)}) %all-to-all-start) | async-done | bytes 1179680 | tf_op jit(solution)/shard_map/cond/branch_1_fun/spectra_0/all_to_all | solution.py:666
  78.7 26.2 %conditional.16 = (bf16[768,768]{1,0:T(8,128)(2,1)}, bf16[2576,128]{1,0:T(8,128)(2,1)}, bf16[2576,128]{1,0:T(8,128)(2,1)}, bf16[2576,128]{1,0:T(8,128)(2,1)}, bf16[2576,128]{1,0:T(8,128)(2,1)}) conditional(s32[]{:T(128)} %convert_element_type.57, () %tuple.145, (s32[1]{0:T(128)}, bf16[4,768,256]{2,1,0:T(8,128)(2,1)S(1)}, f32[1,768]{1,0:T(1,128)S(1)}, ...), branch_computations={%region_2.3_spmd, %region_3.4_spmd} | conditional | flops 2048 | bytes 803539008 | solution.py:674
  93.1 11.8 %all-to-all-done.1 = bf16[8,96,768]{2,1,0:T(8,128)(2,1)} async-done(((bf16[8,96,768]{2,1,0:T(8,128)(2,1)}), bf16[8,96,768]{2,1,0:T(8,128)(2,1)}, u32[]{:S(2)}, u32[]{:S(2)}) %all-to-all-start.1) | async-done | bytes 1179680 | tf_op jit(solution)/shard_map/cond/branch_1_fun/spectra_1/all_to_all | solution.py:666
  110.3 25.5 %conditional.17 = (bf16[768,768]{1,0:T(8,128)(2,1)S(1)}) conditional(s32[]{:T(128)} %convert_element_type.57, () %tuple.149, (s32[1]{0:T(128)}, bf16[4,768,256]{2,1,0:T(8,128)(2,1)S(1)}, f32[1,768]{1,0:T(1,128)S(1)}, f32[1,768]{1,0:T(1,128)S(1)}, bf16[1296,128]{1,0:T(8,128)(2,1)}, /*index=5*/bf16[1296,128]{1,0:T(8,128)(2,1)}, ...), branch_computations={%region_4.5_spmd, %region_5.6_spmd} | conditional | flops 1024 | bytes 402359296 | solution.py:674
  115.4 20.5 %all_to_all.56 = bf16[8,96,768]{2,1,0:T(8,128)(2,1)S(1)} all-to-all(bf16[8,96,768]{2,1,0:T(8,128)(2,1)} %bitcast.80), channel_id=1, replica_groups=mesh['lat'=8,'lon'=4] {'lat'}, dimensions={0} | all-to-all | bytes 2359296 | tf_op jit(solution)/shard_map/cond/branch_1_fun/spectra_2/all_to_all | solution.py:666
  142.0 25.6 %conditional.18 = (bf16[768,768]{1,0:T(8,128)(2,1)S(1)}) conditional(s32[]{:T(128)} %convert_element_type.57, () %tuple.152, (s32[1]{0:T(128)}, bf16[4,768,256]{2,1,0:T(8,128)(2,1)S(1)}, f32[1,768]{1,0:T(1,128)S(1)}, f32[1,768]{1,0:T(1,128)S(1)}, bf16[1296,128]{1,0:T(8,128)(2,1)S(1)}, /*index=5*/bf16[1296,128]{1,0:T(8,128)(2,1)}, ...), branch_computations={%region_6.7_spmd, %region_7.8_spmd} | conditional | flops 1024 | bytes 402359296 | solution.py:674
  147.0 20.5 %all_to_all.57 = bf16[8,96,768]{2,1,0:T(8,128)(2,1)S(1)} all-to-all(bf16[8,96,768]{2,1,0:T(8,128)(2,1)} %bitcast.81), channel_id=1, replica_groups=mesh['lat'=8,'lon'=4] {'lat'}, dimensions={0} | all-to-all | bytes 2359296 | tf_op jit(solution)/shard_map/cond/branch_1_fun/spectra_3/all_to_all | solution.py:666
  168.1 46.6 %conditional.19 = (bf16[1536,768]{1,0:T(8,128)(2,1)}, bf16[1536,768]{1,0:T(8,128)(2,1)}, f32[6,512,768]{2,1,0:T(8,128)}, bf16[768,1408]{1,0:T(8,128)(2,1)S(1)}, ...) conditional(s32[]{:T(128)} %convert_element_type.57, () %tuple.138, ...), branch_computations={%region_8.9_spmd, %region_9.10_spmd} | conditional | flops 1024 | bytes 407077984 | solution.py:674
  168.1 12.8 %filter_forward.1 = (bf16[1536,768]{1,0:T(8,128)(2,1)}, bf16[1536,768]{1,0:T(8,128)(2,1)}, f32[6,512,768]{2,1,0:T(8,128)}) custom-call(s32[1]{0:T(128)} %get-tuple-element.375.first_ref, bf16[96,128,128]{2,1,0:T(8,128)(2,1)} %constant.253.clone.1.to_ref, bf16[96,128,128]{2,1,0:T(8,128)(2,1)} %constant.254.clone.1.back_ref, ...), custom_call_target="tpu_custom_call" | custom-call | flops 1024 | bytes 400000000 | tf_op jit(solution)/shard_map/cond/branch_1_fun/filter_forward/pallas_call | solution.py:261
  192.3 22.4 %all-to-all-done.4 = bf16[8,192,768]{2,1,0:T(8,128)(2,1)} async-done(((bf16[8,192,768]{2,1,0:T(8,128)(2,1)}), bf16[8,192,768]{2,1,0:T(8,128)(2,1)}, u32[]{:S(2)}, u32[]{:S(2)}) %all-to-all-start.4) | async-done | bytes 2359328 | tf_op jit(solution)/shard_map/cond/branch_1_fun/synthesis_0/all_to_all | solution.py:666
  218.0 46.2 %conditional.20 = (bf16[2576,128]{1,0:T(8,128)(2,1)}, bf16[2576,128]{1,0:T(8,128)(2,1)}, bf16[2576,128]{1,0:T(8,128)(2,1)}, bf16[2576,128]{1,0:T(8,128)(2,1)}, f...) conditional(s32[]{:T(128)} %convert_element_type.57, () %tuple.157, ...), branch_computations={%region_10.11_spmd, %region_11.12_spmd} | conditional | flops 1024 | bytes 408405152 | solution.py:674
  222.9 41.4 %feed_forward.2 = (bf16[2576,128]{1,0:T(8,128)(2,1)}, bf16[2576,128]{1,0:T(8,128)(2,1)}, bf16[2576,128]{1,0:T(8,128)(2,1)}, bf16[2576,128]{1,0:T(8,128)(2,1)}, f...) custom-call(s32[1]{0:T(128)} %get-tuple-element.394.me_ref, ...), custom_call_target="tpu_custom_call" | custom-call | flops 1024 | bytes 400000000 | tf_op jit(solution)/shard_map/cond/branch_1_fun/feed_forward/pallas_call | solution.py:500
  273.8 46.4 %conditional.21 = (bf16[2576,128]{1,0:T(8,128)(2,1)}, bf16[2576,128]{1,0:T(8,128)(2,1)}, bf16[2576,128]{1,0:T(8,128)(2,1)}, bf16[2576,128]{1,0:T(8,128)(2,1)}, f...) conditional(s32[]{:T(128)} %convert_element_type.57, () %tuple.137, ...), branch_computations={%region_12.13_spmd, %region_13.14_spmd} | conditional | flops 1024 | bytes 407078016 | solution.py:674
  278.8 41.3 %feed_forward.3 = (bf16[2576,128]{1,0:T(8,128)(2,1)}, bf16[2576,128]{1,0:T(8,128)(2,1)}, bf16[2576,128]{1,0:T(8,128)(2,1)}, bf16[2576,128]{1,0:T(8,128)(2,1)}, f...) custom-call(s32[1]{0:T(128)} %get-tuple-element.428.me_ref, ...), custom_call_target="tpu_custom_call" | custom-call | flops 1024 | bytes 400000000 | tf_op jit(solution)/shard_map/cond/branch_1_fun/feed_forward/pallas_call | solution.py:500
  320.2 11.4 %collective-permute-done.22.refs_2_ = bf16[2576,128]{1,0:T(8,128)(2,1)} collective-permute-done((bf16[2576,128]{1,0:T(8,128)(2,1)}, bf16[2576,128]{1,0:T(8,128)(2,1)}, u32[]{:S(2)}, u32[]{:S(2)}) %collective-permute-start.22) | collective-permute-done | bytes 659488 | tf_op jit(solution)/shard_map/output_0/ppermute | solution.py:658
  331.6 59.5 %conditional.22 = (bf16[768,768]{1,0:T(8,128)(2,1)}, bf16[768,768]{1,0:T(8,128)(2,1)}, bf16[768,768]{1,0:T(8,128)(2,1)}, f32[192,768]{1,0:T(8,128)}, f32[768,140...) conditional(s32[]{:T(128)} %convert_element_type.57, () %tuple.160, ...), branch_computations={%region_14.15_spmd, %region_15.18_spmd} | conditional | flops 17719504896 | bytes 479175808 | solution.py:674
  362.1 9.9 %convolution_add_fusion.1 = f32[768,1408]{1,0:T(8,128)} fusion(f32[768,1408]{1,0:T(8,128)S(1)} %fusion.15, bf16[2048,768]{1,0:T(8,128)(2,1)} %get-tuple-element.479, bf16[2048,1408]{1,0:T(8,128)(2,1)} %get-tuple-element.480), kind=kOutput, calls=%fused_computation.1 | convolution fusion | flops 4430266368 | bytes 17563648 | tf_op jit(solution)/shard_map/cond/branch_1_fun/gc,gh->ch/dot_general | solution.py:823
  373.4 15.8 %filter_backward.1 = (bf16[768,768]{1,0:T(8,128)(2,1)}, bf16[768,768]{1,0:T(8,128)(2,1)}, bf16[768,768]{1,0:T(8,128)(2,1)}, bf16[768,768]{1,0:T(8,128)(2,1)}, f32[128,768]{1,0:T(8,128)}) custom-call(s32[1]{0:T(128)} %get-tuple-element.462.first_ref, bf16[96,128,128]{2,1,0:T(8,128)(2,1)} %constant.252.clone.1.to_ref, ...), custom_call_target="tpu_custom_call" | custom-call | flops 1024 | bytes 400000000 | tf_op jit(solution)/shard_map/cond/branch_1_fun/filter_backward/pallas_call | solution.py:261
  394.0 16.7 %collective-permute-done.18.refs_1_ = bf16[2576,128]{1,0:T(8,128)(2,1)S(1)} collective-permute-done((bf16[2576,128]{1,0:T(8,128)(2,1)}, bf16[2576,128]{1,0:T(8,128)(2,1)S(1)}, u32[]{:S(2)}, u32[]{:S(2)}) %collective-permute-start.18) | collective-permute-done | bytes 659488 | tf_op jit(solution)/shard_map/output_1/ppermute | solution.py:658
  410.7 38.9 %collective-permute-done.19.refs_2_ = bf16[2576,128]{1,0:T(8,128)(2,1)S(1)} collective-permute-done((bf16[2576,128]{1,0:T(8,128)(2,1)}, bf16[2576,128]{1,0:T(8,128)(2,1)S(1)}, u32[]{:S(2)}, u32[]{:S(2)}) %collective-permute-start.19) | collective-permute-done | bytes 659488 | tf_op jit(solution)/shard_map/output_1/ppermute | solution.py:658
  450.6 21.7 %conditional.24 = (bf16[768,768]{1,0:T(8,128)(2,1)S(1)}) conditional(s32[]{:T(128)} %convert_element_type.57, () %tuple.168, bf16[768,768]{1,0:T(8,128)(2,1)} %get-tuple-element.911), branch_computations={%region_20.21_spmd, %region_21.22_spmd} | conditional | bytes 2359304 | solution.py:674
  450.6 21.7 %all_to_all.59 = bf16[8,96,768]{2,1,0:T(8,128)(2,1)S(1)} all-to-all(bf16[8,96,768]{2,1,0:T(8,128)(2,1)} %bitcast.19), channel_id=1, replica_groups=mesh['lat'=8,'lon'=4] {'lat'}, dimensions={0} | all-to-all | bytes 2359296 | tf_op jit(solution)/shard_map/cond/branch_1_fun/back_spectra_0/all_to_all | solution.py:666
  485.3 25.0 %conditional.23 = (bf16[768,768]{1,0:T(8,128)(2,1)S(1)}) conditional(s32[]{:T(128)} %convert_element_type.57, () %tuple.166, bf16[768,768]{1,0:T(8,128)(2,1)} %get-tuple-element.908), branch_computations={%region_18.19_spmd, %region_19.20_spmd} | conditional | bytes 2359304 | solution.py:674
  485.3 25.0 %all_to_all.58 = bf16[8,96,768]{2,1,0:T(8,128)(2,1)S(1)} all-to-all(bf16[8,96,768]{2,1,0:T(8,128)(2,1)} %bitcast.17), channel_id=1, replica_groups=mesh['lat'=8,'lon'=4] {'lat'}, dimensions={0} | all-to-all | bytes 2359296 | tf_op jit(solution)/shard_map/cond/branch_1_fun/back_spectra_1/all_to_all | solution.py:666
  510.2 21.1 %conditional.26 = (bf16[1296,128]{1,0:T(8,128)(2,1)}, bf16[1296,128]{1,0:T(8,128)(2,1)}, bf16[1296,128]{1,0:T(8,128)(2,1)}, bf16[1296,128]{1,0:T(8,128)(2,1)}, b...) conditional(s32[]{:T(128)} %convert_element_type.57, () %tuple.165, (s32[1]{0:T(128)}, ...), branch_computations={%region_24.25_spmd, %region_25.26_spmd} | conditional | flops 1024 | bytes 403539008 | solution.py:674
  521.4 9.9 %all-to-all-done.9 = bf16[8,96,768]{2,1,0:T(8,128)(2,1)} async-done(((bf16[8,96,768]{2,1,0:T(8,128)(2,1)}), bf16[8,96,768]{2,1,0:T(8,128)(2,1)}, u32[]{:S(2)}, u32[]{:S(2)}) %all-to-all-start.9) | async-done | bytes 1179680 | tf_op jit(solution)/shard_map/cond/branch_1_fun/back_spectra_2/all_to_all | solution.py:666
  540.7 21.1 %conditional.27 = (bf16[1296,128]{1,0:T(8,128)(2,1)}, bf16[1296,128]{1,0:T(8,128)(2,1)}, bf16[1296,128]{1,0:T(8,128)(2,1)}, bf16[1296,128]{1,0:T(8,128)(2,1)}, b...) conditional(s32[]{:T(128)} %convert_element_type.57, () %tuple.172, (s32[1]{0:T(128)}, ...), branch_computations={%region_28.29_spmd, %region_29.30_spmd} | conditional | flops 1024 | bytes 404718656 | solution.py:674
  563.3 13.9 %collective-permute-done.25.refs_2_ = bf16[1296,128]{1,0:T(8,128)(2,1)} collective-permute-done((bf16[1296,128]{1,0:T(8,128)(2,1)}, bf16[1296,128]{1,0:T(8,128)(2,1)}, u32[]{:S(2)}, u32[]{:S(2)}) %collective-permute-start.25) | collective-permute-done | bytes 331808 | tf_op jit(solution)/shard_map/input_grad_1/ppermute | solution.py:658
  580.0 19.8 %conditional.28 = (bf16[1296,128]{1,0:T(8,128)(2,1)S(1)}, bf16[1296,128]{1,0:T(8,128)(2,1)}, bf16[1296,128]{1,0:T(8,128)(2,1)}, bf16[1296,128]{1,0:T(8,128)(2,1)}, f32[24,768]{1,0:T(8,128)S(1)}) conditional(s32[]{:T(128)} %convert_element_type.57, () %tuple.164, (s32[1]{0:T(128)}, bf16[4,256,768]{2,1,0:T(8,128)(2,1)S(1)}, ...), branch_computations={%region_30.31_spmd, %region_31.33_spmd} | conditional | flops 130048 | bytes 402433088 | solution.py:674
  656.6 13.5 %conditional.29 = (f32[192,768]{1,0:T(8,128)S(1)}) conditional(s32[]{:T(128)} %convert_element_type.57, () %tuple.176, f32[24,768]{1,0:T(8,128)S(1)} %add.169), branch_computations={%region_33.34_spmd, %region_34.35_spmd} | conditional | bytes 1843208 | solution.py:674
  656.6 13.4 %all_to_all.60 = f32[8,24,768]{2,1,0:T(8,128)S(1)} all-to-all(f32[8,24,768]{2,1,0:T(8,128)S(1)} %broadcast_in_dim.0), channel_id=1, replica_groups=mesh['lat'=8,'lon'=4] {'lat'}, dimensions={0} | all-to-all | bytes 1179648 | tf_op jit(solution)/shard_map/cond/branch_1_fun/gather/all_to_all | solution.py:666
  (269 shorter events, 343.4 us)
Async XLA Ops:
  7.2 527.6 %reduce-scatter.3.cloned.1.call-start = ((), (), s32[]{:S(2)}) async-start(), calls=%async_computation.16 | async-start | bytes 4866048 | tf_op jit(solution)/shard_map/weights_lat/reduce_scatter | solution.py:854
  38.6 36.2 %collective-permute-start.3 = (bf16[1296,128]{1,0:T(8,128)(2,1)}, bf16[1296,128]{1,0:T(8,128)(2,1)}, u32[]{:S(2)}, u32[]{:S(2)}) collective-permute-start(bf16[1296,128]{1,0:T(8,128)(2,1)} %get-tuple-element.797), channel_id=1, source_target_pairs={{0,1},{1,2},{2,3},{3,0},{4,5},{5,6},{6,7},{7,4},{8,9},{9,10},{10,1... | collective-permute-start | bytes 995336 | tf_op jit(solution)/shard_map/fields_1/ppermute | solution.py:658
  135.9 78.9 %collective-permute-start.12 = (bf16[2576,128]{1,0:T(8,128)(2,1)}, bf16[2576,128]{1,0:T(8,128)(2,1)}, u32[]{:S(2)}, u32[]{:S(2)}) collective-permute-start(bf16[2576,128]{1,0:T(8,128)(2,1)} %get-tuple-element.867), channel_id=1, source_target_pairs={{0,1},{1,2},{2,3},{3,0},{4,5},{5,6},{6,7},{7,4},{8,9},{9,10},{10,1... | collective-permute-start | bytes 1978376 | tf_op jit(solution)/shard_map/upstream_0/ppermute | solution.py:658
  137.1 80.9 %collective-permute-start.13 = (bf16[2576,128]{1,0:T(8,128)(2,1)}, bf16[2576,128]{1,0:T(8,128)(2,1)}, u32[]{:S(2)}, u32[]{:S(2)}) collective-permute-start(bf16[2576,128]{1,0:T(8,128)(2,1)} %get-tuple-element.868), channel_id=1, source_target_pairs={{0,2},{1,3},{2,0},{3,1},{4,6},{5,7},{6,4},{7,5},{8,10},{9,11},{10,... | collective-permute-start | bytes 1978376 | tf_op jit(solution)/shard_map/upstream_0/ppermute | solution.py:658
  140.3 77.7 %collective-permute-start.14 = (bf16[2576,128]{1,0:T(8,128)(2,1)}, bf16[2576,128]{1,0:T(8,128)(2,1)}, u32[]{:S(2)}, u32[]{:S(2)}) collective-permute-start(bf16[2576,128]{1,0:T(8,128)(2,1)} %get-tuple-element.869), channel_id=1, source_target_pairs={{0,3},{1,0},{2,1},{3,2},{4,7},{5,4},{6,5},{7,6},{8,11},{9,8},{10,9... | collective-permute-start | bytes 1978376 | tf_op jit(solution)/shard_map/upstream_0/ppermute | solution.py:658
  167.5 106.2 %collective-permute-start.15 = (bf16[2576,128]{1,0:T(8,128)(2,1)}, bf16[2576,128]{1,0:T(8,128)(2,1)}, u32[]{:S(2)}, u32[]{:S(2)}) collective-permute-start(bf16[2576,128]{1,0:T(8,128)(2,1)} %get-tuple-element.873), channel_id=1, source_target_pairs={{0,1},{1,2},{2,3},{3,0},{4,5},{5,6},{6,7},{7,4},{8,9},{9,10},{10,1... | collective-permute-start | bytes 1978376 | tf_op jit(solution)/shard_map/upstream_1/ppermute | solution.py:658
  167.6 106.1 %collective-permute-start.16 = (bf16[2576,128]{1,0:T(8,128)(2,1)}, bf16[2576,128]{1,0:T(8,128)(2,1)}, u32[]{:S(2)}, u32[]{:S(2)}) collective-permute-start(bf16[2576,128]{1,0:T(8,128)(2,1)} %get-tuple-element.874), channel_id=1, source_target_pairs={{0,2},{1,3},{2,0},{3,1},{4,6},{5,7},{6,4},{7,5},{8,10},{9,11},{10,... | collective-permute-start | bytes 1978376 | tf_op jit(solution)/shard_map/upstream_1/ppermute | solution.py:658
  180.9 33.8 %all-to-all-start.4 = ((bf16[8,192,768]{2,1,0:T(8,128)(2,1)}), bf16[8,192,768]{2,1,0:T(8,128)(2,1)}, u32[]{:S(2)}, u32[]{:S(2)}) async-start(bf16[8,192,768]{2,1,0:T(8,128)(2,1)} %bitcast.88), calls=%async_computation.4 | async-start | bytes 4718592 | tf_op jit(solution)/shard_map/cond/branch_1_fun/synthesis_0/all_to_all | solution.py:666
  214.7 59.0 %collective-permute-start.17 = (bf16[2576,128]{1,0:T(8,128)(2,1)}, bf16[2576,128]{1,0:T(8,128)(2,1)}, u32[]{:S(2)}, u32[]{:S(2)}) collective-permute-start(bf16[2576,128]{1,0:T(8,128)(2,1)} %get-tuple-element.875), channel_id=1, source_target_pairs={{0,3},{1,0},{2,1},{3,2},{4,7},{5,4},{6,5},{7,6},{8,11},{9,8},{10,9... | collective-permute-start | bytes 1978376 | tf_op jit(solution)/shard_map/upstream_1/ppermute | solution.py:658
  218.1 46.2 %all-to-all-start.5 = ((bf16[8,192,768]{2,1,0:T(8,128)(2,1)}), bf16[8,192,768]{2,1,0:T(8,128)(2,1)}, u32[]{:S(2)}, u32[]{:S(2)}) async-start(bf16[8,192,768]{2,1,0:T(8,128)(2,1)} %bitcast.11), calls=%async_computation.5 | async-start | bytes 4718592 | tf_op jit(solution)/shard_map/cond/branch_1_fun/synthesis_1/all_to_all | solution.py:666
  264.3 55.9 %collective-permute-start.21 = (bf16[2576,128]{1,0:T(8,128)(2,1)}, bf16[2576,128]{1,0:T(8,128)(2,1)}, u32[]{:S(2)}, u32[]{:S(2)}) collective-permute-start(bf16[2576,128]{1,0:T(8,128)(2,1)} %get-tuple-element.882), channel_id=1, source_target_pairs={{0,3},{1,0},{2,1},{3,2},{4,7},{5,4},{6,5},{7,6},{8,11},{9,8},{10,9... | collective-permute-start | bytes 1978376 | tf_op jit(solution)/shard_map/output_0/ppermute | solution.py:658
  265.0 66.6 %collective-permute-start.22 = (bf16[2576,128]{1,0:T(8,128)(2,1)}, bf16[2576,128]{1,0:T(8,128)(2,1)}, u32[]{:S(2)}, u32[]{:S(2)}) collective-permute-start(bf16[2576,128]{1,0:T(8,128)(2,1)} %get-tuple-element.883), channel_id=1, source_target_pairs={{0,2},{1,3},{2,0},{3,1},{4,6},{5,7},{6,4},{7,5},{8,10},{9,11},{10,... | collective-permute-start | bytes 1978376 | tf_op jit(solution)/shard_map/output_0/ppermute | solution.py:658
  273.8 57.9 %collective-permute-start.23 = (bf16[2576,128]{1,0:T(8,128)(2,1)}, bf16[2576,128]{1,0:T(8,128)(2,1)}, u32[]{:S(2)}, u32[]{:S(2)}) collective-permute-start(bf16[2576,128]{1,0:T(8,128)(2,1)} %get-tuple-element.884), channel_id=1, source_target_pairs={{0,1},{1,2},{2,3},{3,0},{4,5},{5,6},{6,7},{7,4},{8,9},{9,10},{10,1... | collective-permute-start | bytes 1978376 | tf_op jit(solution)/shard_map/output_0/ppermute | solution.py:658
  273.8 46.4 %all-to-all-start.6 = ((bf16[8,192,768]{2,1,0:T(8,128)(2,1)}), bf16[8,192,768]{2,1,0:T(8,128)(2,1)}, u32[]{:S(2)}, u32[]{:S(2)}) async-start(bf16[8,192,768]{2,1,0:T(8,128)(2,1)} %bitcast.13), calls=%async_computation.6 | async-start | bytes 4718592 | tf_op jit(solution)/shard_map/cond/branch_1_fun/back_synthesis_0/all_to_all | solution.py:666
  331.6 40.4 %all-to-all-start.13 = ((bf16[8,192,768]{2,1,0:T(8,128)(2,1)}), bf16[8,192,768]{2,1,0:T(8,128)(2,1)S(1)}, u32[]{:S(2)}, u32[]{:S(2)}) async-start(bf16[8,192,768]{2,1,0:T(8,128)(2,1)} %bitcast.15), calls=%async_computation.13 | async-start | bytes 4718592 | tf_op jit(solution)/shard_map/cond/branch_1_fun/back_synthesis_1/all_to_all | solution.py:666
  391.1 143.7 %reduce-scatter.5.cloned.1.call-start = ((), (), s32[]{:S(2)}) async-start(), calls=%async_computation.17 | async-start | bytes 4866048 | tf_op jit(solution)/shard_map/weights_lat/reduce_scatter | solution.py:854
  391.8 288.8 %all-gather.3.cloned.1.call-start = ((), (), s32[]{:S(2)}) async-start(), calls=%async_computation.18 | async-start | bytes 4866048 | tf_op jit(solution)/shard_map/weights_lat/all_gather | solution.py:926
  392.0 57.6 %collective-permute-start.19 = (bf16[2576,128]{1,0:T(8,128)(2,1)}, bf16[2576,128]{1,0:T(8,128)(2,1)S(1)}, u32[]{:S(2)}, u32[]{:S(2)}) collective-permute-start(bf16[2576,128]{1,0:T(8,128)(2,1)} %get-tuple-element.879), channel_id=1, source_target_pairs={{0,2},{1,3},{2,0},{3,1},{4,6},{5,7},{6,4},{7,5},{8,10},{9,11},{10,... | collective-permute-start | bytes 1978376 | tf_op jit(solution)/shard_map/output_1/ppermute | solution.py:658
  392.0 57.6 %collective-permute-start.20 = (bf16[2576,128]{1,0:T(8,128)(2,1)}, bf16[2576,128]{1,0:T(8,128)(2,1)S(1)}, u32[]{:S(2)}, u32[]{:S(2)}) collective-permute-start(bf16[2576,128]{1,0:T(8,128)(2,1)} %get-tuple-element.880), channel_id=1, source_target_pairs={{0,1},{1,2},{2,3},{3,0},{4,5},{5,6},{6,7},{7,4},{8,9},{9,10},{10,1... | collective-permute-start | bytes 1978376 | tf_op jit(solution)/shard_map/output_1/ppermute | solution.py:658
  479.2 55.0 %collective-permute-start.27 = (bf16[1296,128]{1,0:T(8,128)(2,1)}, bf16[1296,128]{1,0:T(8,128)(2,1)}, u32[]{:S(2)}, u32[]{:S(2)}) collective-permute-start(bf16[1296,128]{1,0:T(8,128)(2,1)} %get-tuple-element.919), channel_id=1, source_target_pairs={{0,3},{1,0},{2,1},{3,2},{4,7},{5,4},{6,5},{7,6},{8,11},{9,8},{10,9... | collective-permute-start | bytes 995336 | tf_op jit(solution)/shard_map/input_grad_0/ppermute | solution.py:658
  479.2 55.5 %collective-permute-start.28 = (bf16[1296,128]{1,0:T(8,128)(2,1)}, bf16[1296,128]{1,0:T(8,128)(2,1)}, u32[]{:S(2)}, u32[]{:S(2)}) collective-permute-start(bf16[1296,128]{1,0:T(8,128)(2,1)} %get-tuple-element.920), channel_id=1, source_target_pairs={{0,2},{1,3},{2,0},{3,1},{4,6},{5,7},{6,4},{7,5},{8,10},{9,11},{10,... | collective-permute-start | bytes 995336 | tf_op jit(solution)/shard_map/input_grad_0/ppermute | solution.py:658
  483.3 51.5 %collective-permute-start.29 = (bf16[1296,128]{1,0:T(8,128)(2,1)}, bf16[1296,128]{1,0:T(8,128)(2,1)}, u32[]{:S(2)}, u32[]{:S(2)}) collective-permute-start(bf16[1296,128]{1,0:T(8,128)(2,1)} %get-tuple-element.921), channel_id=1, source_target_pairs={{0,1},{1,2},{2,3},{3,0},{4,5},{5,6},{6,7},{7,4},{8,9},{9,10},{10,1... | collective-permute-start | bytes 995336 | tf_op jit(solution)/shard_map/input_grad_0/ppermute | solution.py:658
  534.2 42.9 %collective-permute-start.25 = (bf16[1296,128]{1,0:T(8,128)(2,1)}, bf16[1296,128]{1,0:T(8,128)(2,1)}, u32[]{:S(2)}, u32[]{:S(2)}) collective-permute-start(bf16[1296,128]{1,0:T(8,128)(2,1)} %get-tuple-element.916), channel_id=1, source_target_pairs={{0,2},{1,3},{2,0},{3,1},{4,6},{5,7},{6,4},{7,5},{8,10},{9,11},{10,... | collective-permute-start | bytes 995336 | tf_op jit(solution)/shard_map/input_grad_1/ppermute | solution.py:658
  534.2 42.9 %collective-permute-start.26 = (bf16[1296,128]{1,0:T(8,128)(2,1)}, bf16[1296,128]{1,0:T(8,128)(2,1)}, u32[]{:S(2)}, u32[]{:S(2)}) collective-permute-start(bf16[1296,128]{1,0:T(8,128)(2,1)} %get-tuple-element.917), channel_id=1, source_target_pairs={{0,1},{1,2},{2,3},{3,0},{4,5},{5,6},{6,7},{7,4},{8,9},{9,10},{10,1... | collective-permute-start | bytes 995336 | tf_op jit(solution)/shard_map/input_grad_1/ppermute | solution.py:658
  536.9 40.3 %collective-permute-start.30 = (bf16[48,1408]{1,0:T(8,128)(2,1)}, bf16[48,1408]{1,0:T(8,128)(2,1)}, u32[]{:S(2)}, u32[]{:S(2)}) collective-permute-start(bf16[48,1408]{1,0:T(8,128)(2,1)} %get-tuple-element.1008), channel_id=1, source_target_pairs={{0,1},{1,2},{2,3},{3,0},{4,5},{5,6},{6,7},{7,4},{8,9},{9,10},{10,1... | collective-permute-start | bytes 405512 | tf_op jit(solution)/shard_map/weights_sum/ppermute | solution.py:658
  539.8 40.3 %collective-permute-start.31 = (bf16[48,1408]{1,0:T(8,128)(2,1)}, bf16[48,1408]{1,0:T(8,128)(2,1)}, u32[]{:S(2)}, u32[]{:S(2)}) collective-permute-start(bf16[48,1408]{1,0:T(8,128)(2,1)} %get-tuple-element.1007), channel_id=1, source_target_pairs={{0,2},{1,3},{2,0},{3,1},{4,6},{5,7},{6,4},{7,5},{8,10},{9,11},{10,... | collective-permute-start | bytes 405512 | tf_op jit(solution)/shard_map/weights_sum/ppermute | solution.py:658
  577.1 45.8 %collective-permute-start.36 = (bf16[1296,128]{1,0:T(8,128)(2,1)}, bf16[1296,128]{1,0:T(8,128)(2,1)}, u32[]{:S(2)}, u32[]{:S(2)}) collective-permute-start(bf16[1296,128]{1,0:T(8,128)(2,1)} %get-tuple-element.947), channel_id=1, source_target_pairs={{0,3},{1,0},{2,1},{3,2},{4,7},{5,4},{6,5},{7,6},{8,11},{9,8},{10,9... | collective-permute-start | bytes 995336 | tf_op jit(solution)/shard_map/input_grad_2/ppermute | solution.py:658
  577.1 45.8 %collective-permute-start.37 = (bf16[1296,128]{1,0:T(8,128)(2,1)}, bf16[1296,128]{1,0:T(8,128)(2,1)}, u32[]{:S(2)}, u32[]{:S(2)}) collective-permute-start(bf16[1296,128]{1,0:T(8,128)(2,1)} %get-tuple-element.948), channel_id=1, source_target_pairs={{0,2},{1,3},{2,0},{3,1},{4,6},{5,7},{6,4},{7,5},{8,10},{9,11},{10,... | collective-permute-start | bytes 995336 | tf_op jit(solution)/shard_map/input_grad_2/ppermute | solution.py:658
  577.2 45.7 %collective-permute-start.38 = (bf16[1296,128]{1,0:T(8,128)(2,1)}, bf16[1296,128]{1,0:T(8,128)(2,1)}, u32[]{:S(2)}, u32[]{:S(2)}) collective-permute-start(bf16[1296,128]{1,0:T(8,128)(2,1)} %get-tuple-element.949), channel_id=1, source_target_pairs={{0,1},{1,2},{2,3},{3,0},{4,5},{5,6},{6,7},{7,4},{8,9},{9,10},{10,1... | collective-permute-start | bytes 995336 | tf_op jit(solution)/shard_map/input_grad_2/ppermute | solution.py:658
  628.2 41.8 %collective-permute-start.33 = (bf16[1296,128]{1,0:T(8,128)(2,1)}, bf16[1296,128]{1,0:T(8,128)(2,1)S(1)}, u32[]{:S(2)}, u32[]{:S(2)}) collective-permute-start(bf16[1296,128]{1,0:T(8,128)(2,1)} %get-tuple-element.935), channel_id=1, source_target_pairs={{0,3},{1,0},{2,1},{3,2},{4,7},{5,4},{6,5},{7,6},{8,11},{9,8},{10,9... | collective-permute-start | bytes 995336 | tf_op jit(solution)/shard_map/input_grad_3/ppermute | solution.py:658
  630.9 39.2 %collective-permute-start.34 = (bf16[1296,128]{1,0:T(8,128)(2,1)}, bf16[1296,128]{1,0:T(8,128)(2,1)S(1)}, u32[]{:S(2)}, u32[]{:S(2)}) collective-permute-start(bf16[1296,128]{1,0:T(8,128)(2,1)} %get-tuple-element.936), channel_id=1, source_target_pairs={{0,2},{1,3},{2,0},{3,1},{4,6},{5,7},{6,4},{7,5},{8,10},{9,11},{10,... | collective-permute-start | bytes 995336 | tf_op jit(solution)/shard_map/input_grad_3/ppermute | solution.py:658
  630.9 39.2 %collective-permute-start.35 = (bf16[1296,128]{1,0:T(8,128)(2,1)}, bf16[1296,128]{1,0:T(8,128)(2,1)S(1)}, u32[]{:S(2)}, u32[]{:S(2)}) collective-permute-start(bf16[1296,128]{1,0:T(8,128)(2,1)} %get-tuple-element.937), channel_id=1, source_target_pairs={{0,1},{1,2},{2,3},{3,0},{4,5},{5,6},{6,7},{7,4},{8,9},{9,10},{10,1... | collective-permute-start | bytes 995336 | tf_op jit(solution)/shard_map/input_grad_3/ppermute | solution.py:658
  (68 other events, 1179.0 us)
Sparse Core Ops, SparseCore 0:
  391.2 50.7 reduce-scatter.2
  445.5 60.9 reduce-scatter.4
  624.1 36.4 all-gather.2

commit v3 on v2

--- a/solution.py
+++ b/solution.py
@@ -383,7 +383,7 @@
 
 
 def feed_forward(
-    me, tables, weights, offset, gain, spectra, slots, upstreams, lat, depth, points, channels
+    me, tables, weights, offset, gain, spectra, slots, upstreams, lat, depth, points, channels, split
 ):
     n = depth * points
     pair, count = len(slots), len(slots[0])
@@ -398,8 +398,9 @@
     ):
         ins, ups = refs[: pair * count], refs[pair * count : (pair + 1) * count]
         refs = refs[(pair + 1) * count :]
-        outs = refs[:count]
-        grad_ref, second_ref, active_ref, pre_ref, cot_ref, gain_part, back_ref = refs[count:-4]
+        outs = refs[: split * count]
+        refs = refs[split * count :]
+        grad_ref, second_ref, active_ref, pre_ref, cot_ref, gain_part, back_ref = refs[:-4]
         x_now, up_now, y_now, total = refs[-4:]
         step = pl.program_id(0)
 
@@ -468,17 +469,22 @@
                         c, i * part : (i + 1) * part
                     ].astype(LOW)
 
-        store_points(up_now, output.astype(LOW), output[:, channels - 1 : channels], points)
+        m = pair * n // split
+        leaving = [x_now.at[c] for c in range(pair)] if split > 1 else [up_now]
+        for c in range(split):
+            block = output[c * m : (c + 1) * m]
+            store_points(leaving[c], block.astype(LOW), block[:, channels - 1 : channels], points)
         for s in range(count):
 
             @pl.when(step == s)
             def _():
-                outs[s][...] = up_now[...]
+                for c in range(split):
+                    outs[c * count + s][...] = leaving[c][...]
 
     rows = lambda w: pl.BlockSpec((pair * n, w), lambda s, me_ref: (s, 0))
-    slot = jax.ShapeDtypeStruct(upstreams[0].shape, LOW)
+    slot = jax.ShapeDtypeStruct((flat if split > 1 else upstreams)[0].shape, LOW)
     height = count * pair * n
-    outs = [slot] * count + [
+    outs = [slot] * (split * count) + [
         jax.ShapeDtypeStruct((height, width), F32),
         jax.ShapeDtypeStruct((height, width), LOW),
         jax.ShapeDtypeStruct((height, hidden_width), LOW),
@@ -487,7 +493,7 @@
         jax.ShapeDtypeStruct((8, width), F32),
         jax.ShapeDtypeStruct(spectra.shape, LOW),
     ]
-    out_specs = [fixed(slot)] * count + [
+    out_specs = [fixed(slot)] * (split * count) + [
         rows(width),
         rows(width),
         rows(hidden_width),
@@ -507,7 +513,7 @@
             out_specs=out_specs,
             scratch_shapes=[
                 pltpu.VMEM((pair, *flat[0].shape), LOW),
-                pltpu.VMEM(slot.shape, LOW),
+                pltpu.VMEM(upstreams[0].shape, LOW),
                 pltpu.VMEM((pair, size, width), LOW),
                 pltpu.VMEM((pair, size, width), F32),
             ],
@@ -516,6 +522,53 @@
         cost_estimate=cost(0, 0),
         name="feed_forward",
     )(me, *arrays)
+
+
+def weight_sums(parts, block=512):
+    count = len(parts)
+    height, width = parts[0][0].shape
+    hidden_width = parts[0][1].shape[1]
+    block = min(block, height)
+    steps = height // block
+
+    def kernel(*refs):
+        ins, out = refs[:-1], refs[-1]
+        step = pl.program_id(0)
+
+        @pl.when(step == 0)
+        def _():
+            out[...] = jnp.zeros_like(out)
+
+        def add(row, left, right):
+            out[row : row + width, :] += lax.dot_general(
+                left[...], right[...], (((0,), (0,)), ((), ())), preferred_element_type=F32
+            )
+
+        for m in range(count):
+
+            @pl.when((step >= m * steps) & (step < (m + 1) * steps))
+            def _():
+                second, active, pre, cot = ins[4 * m : 4 * m + 4]
+                add(0, second, pre)
+                add(width, cot, active)
+
+    def spec(array, m):
+        return pl.BlockSpec(
+            (block, array.shape[1]),
+            lambda k: (jnp.clip(k - m * steps, 0, steps - 1), 0),
+        )
+
+    shape = jax.ShapeDtypeStruct((2 * width, hidden_width), F32)
+    return pl.pallas_call(
+        kernel,
+        out_shape=shape,
+        grid=(count * steps,),
+        in_specs=[spec(a, m) for m, part in enumerate(parts) for a in part],
+        out_specs=fixed(shape),
+        compiler_params=params(),
+        cost_estimate=cost(0, 0),
+        name="weight_sums",
+    )(*[a for part in parts for a in part])
 
 
 def first_backward(
@@ -583,6 +636,46 @@
     update = update / jnp.maximum(1.0, jnp.sqrt(jnp.mean(update * update)) / CLIP_LEVEL)
     scale_now = STEP_RATE * jnp.maximum(SECOND_EPS, jnp.sqrt(jnp.mean(weight_now * weight_now)))
     return (weight_now - scale_now * update, rows_new, columns_new)
+
+
+def adafactor_call(gradients, place, weight_now, rows_old, columns_old, by_rows, decay_rate):
+    height, width = weight_now.shape
+
+    def kernel(grad_ref, weight_ref, rows_ref, columns_ref, grad_out, new, rows_out, columns_out):
+        gradient = grad_ref[:height, :width].astype(F32)
+        grad_out[...] = gradient
+        squares = gradient * gradient + FIRST_EPS
+        rows_mean = jnp.sum(squares, axis=1, keepdims=True) * (1.0 / width)
+        columns_mean = jnp.sum(squares, axis=0, keepdims=True) * (1.0 / height)
+        rows_new = decay_rate * rows_ref[...] + (1.0 - decay_rate) * rows_mean
+        columns_new = decay_rate * columns_ref[...] + (1.0 - decay_rate) * columns_mean
+        rows_out[...] = rows_new
+        columns_out[...] = columns_new
+        mean = jnp.mean(rows_new) if by_rows else jnp.mean(columns_new)
+        update = gradient * (lax.rsqrt(rows_new / mean) * lax.rsqrt(columns_new))
+        weight = weight_ref[...]
+        size = 1.0 / (height * width)
+        clip = jnp.maximum(1.0, jnp.sqrt(jnp.sum(update * update) * size) / CLIP_LEVEL)
+        rate = STEP_RATE * jnp.maximum(SECOND_EPS, jnp.sqrt(jnp.sum(weight * weight) * size))
+        new[...] = weight - update * (rate / clip)
+
+    whole = lambda a: pl.BlockSpec(a.shape, lambda i: (0, 0))
+    tall, wide = gradients.shape
+    matrix = jax.ShapeDtypeStruct((height, width), F32)
+    outs = [matrix, matrix]
+    outs += [jax.ShapeDtypeStruct((height, 1), F32), jax.ShapeDtypeStruct((1, width), F32)]
+    arrays = [weight_now, rows_old[:, None], columns_old[None]]
+    return pl.pallas_call(
+        kernel,
+        out_shape=outs,
+        grid=(1,),
+        in_specs=[pl.BlockSpec((tall // 2, wide), lambda i: (place, 0))]
+        + [whole(a) for a in arrays],
+        out_specs=[whole(o) for o in outs],
+        compiler_params=params(),
+        cost_estimate=cost(0, 0),
+        name="adafactor",
+    )(gradients, *arrays)
 
 
 def adafactor_vector(weight_now, gradient, moments_old, decay_rate):
@@ -668,10 +761,14 @@
 
     inside = lat_me < lat
 
+    order = [norm_gains[:1, :LANES]]
+
     def unit(function, *arrays):
-        shapes = jax.eval_shape(function, *arrays)
+        run = lambda token, *arrays: tie(token, function(*arrays))
+        shapes = jax.eval_shape(run, order[0], *arrays)
         blank = lambda *_: jax.tree.map(lambda a: jnp.zeros(a.shape, a.dtype), shapes)
-        return lax.cond(inside, function, blank, *arrays)
+        order[0], out = lax.cond(inside, run, blank, order[0], *arrays)
+        return out
 
     def spread(values):
         height = -(-values.shape[0] // (8 * lat)) * 8
@@ -778,6 +875,7 @@
     spectra[-1] = send_next(spectra[-1])
     values, coefs, weights = unit(to_coefficients, weight_in, weight_out, *spectra)
 
+    splits = [1] * (mids - 1) + [pair]
     backs, grads, parts, outputs = [], [], [], []
     gain_parts = []
     for c in range(mids):
@@ -796,6 +894,7 @@
                 depth,
                 points,
                 channels,
+                splits[c],
             )
             following = [exchange_lat(f"synthesis_{c + 1}", a) for a in following]
             before = [exchange_lat(f"back_synthesis_{c - 1}", a) for a in before]
@@ -809,28 +908,26 @@
             values[c + 1 : c + 2],
             backs[c - 1 : c],
         )
-        outputs.append(exchange_lon(f"output_{c}", out[:lon], -1))
-        grads.append(out[lon])
-        parts.append(tuple(out[lon + 1 : lon + 5]))
-        gain_parts.append(out[lon + 5])
-        backs.append(out[lon + 6])
-
-    def to_gradients(before, late, coefs, parts, gain_parts):
-        late = exchange_lat(f"back_synthesis_{mids - 1}", late)
-        weight_part = None
-        for second, active, pre, cot in parts:
-            terms = (
-                jnp.einsum("gc,gh->ch", second, pre, preferred_element_type=F32),
-                jnp.einsum("gc,gh->ch", cot, active, preferred_element_type=F32),
-            )
-            weight_part = terms if weight_part is None else tuple(map(jnp.add, weight_part, terms))
+        for p in range(splits[c]):
+            leaving = out[p * lon : (p + 1) * lon]
+            outputs.append(exchange_lon(f"output_{c}_{p}", leaving, -1))
+        grad, *part, gain_part, back = out[splits[c] * lon :]
+        grads.append(grad)
+        parts.append(part)
+        gain_parts.append(gain_part)
+        backs.append(back)
+
+    def to_weights(late, parts):
+        return exchange_lat(f"back_synthesis_{mids - 1}", late), weight_sums(parts)
+
+    def to_gradients(backs, coefs, gain_parts):
         *values, filter_part = filter_backward(
             first,
             (plain, weighted_back),
             spots,
             response,
             coefs,
-            [*before, late],
+            backs,
             [pair] * mids,
             [1] * chunks,
             lat,
@@ -838,45 +935,40 @@
             groups,
         )
         gain_part = sum(jnp.sum(a, axis=0) for a in gain_parts)
-        small = spread(jnp.concatenate([filter_part, gain_part[None]], axis=0))
-        return values, small, weight_part
-
-    outputs[:-1], backs[-1] = tie(outputs[:-1], backs[-1])
-    values, small, weight_part = unit(
-        to_gradients, backs[:-1], backs[-1], coefs, parts, gain_parts
-    )
-    outputs[-1], values[0] = tie(outputs[-1], values[0])
-    values[0] = unit(lambda a: exchange_lat("back_spectra_0", a), values[0])
+        return values, spread(jnp.concatenate([filter_part, gain_part[None]], axis=0))
+
+    early = mids - 1
+    outputs[:early], backs[-1] = tie(outputs[:early], backs[-1])
+    backs[-1], weight_part = unit(to_weights, backs[-1], parts)
+    outputs[early:-1], backs[-1], weight_part = tie(outputs[early:-1], backs[-1], weight_part)
+    values, small = unit(to_gradients, backs, coefs, gain_parts)
 
     gradients = []
     with jax.named_scope("weights_lat"):
-        part = [
-            lax.psum_scatter(a, "lat", scatter_dimension=0, tiled=True) for a in weight_part
-        ]
-
-    def sum_quarters(part):
-        part = jnp.concatenate(part, axis=0)
-        quarters = part.reshape(lon, -1, hidden_width)
-        pieces = [take(quarters, (lon_me + s) % lon).astype(LOW) for s in range(lon)]
-        return take(quarters, lon_me), exchange_lon("weights_sum", pieces, 1)[1:]
-
-    def gather_quarters(own, pieces):
-        own = (own + sum(piece.astype(F32) for piece in pieces)).astype(LOW)
-        return exchange_lon("weights_gather", [own] * lon, 1)
+        part = lax.psum_scatter(weight_part, "lat", scatter_dimension=0, tiled=True)
 
     for c in range(chunks):
-        if c == 2:
-            gradients[0], part, values[2] = tie(gradients[0], part, values[2])
-            quarters = sum_quarters(part)
-        if c == 3:
-            gradients[1], quarters, values[3] = tie(gradients[1], quarters, values[3])
-            quarters = gather_quarters(*quarters)
-
-        def to_input(spectrum, slots, grad, following, small):
+        if c == min(1, chunks - 1):
+            outputs[-1], order[0] = tie(outputs[-1], order[0])
+        if c == min(2, chunks - 1):
+            part, order[0] = tie(part, order[0])
+            with jax.named_scope("weights_lon"):
+                part = lax.psum(part.astype(LOW), "lon")
+        if c >= 2:
+            gradients[c - 2], order[0] = tie(gradients[c - 2], order[0])
+
+        def to_input(spectrum, slots, grad, outputs):
+            block_output, row = None, 0
+            for arrived in outputs:
+                tall = depth * pair if arrived[0].shape[0] > slots[0].shape[0] else depth
+                block_output = unpack(
+                    me, arrived, block_output, row // tall, tall, fields_in.shape, LOW
+                )
+                row += tall
             out = first_backward(
                 me,
                 back_synthesis,
-                spectrum,
+                exchange_lat(f"back_spectra_{c}", spectrum),
                 slots,
                 grad,
                 c % pair,
@@ -887,56 +979,48 @@
                 points,
                 channels,
             )
-            following = [exchange_lat(f"back_spectra_{c + 1}", a) for a in following]
-            if c == chunks - 1:
-                part = exchange_lat("small", small).reshape(lat, -1, width)
-                small = jnp.sum(part, axis=0)
-            return out, following, small
-
-        following = values[c + 1 : c + 2] if c > 0 else []
-        out, following, small = unit(
-            to_input, values[c], fields[c], grads[c // pair], following, small
+            return out, block_output
+
+        out, block_output = unit(
+            to_input, values[c], fields[c], grads[c // pair], outputs if c == chunks - 1 else []
         )
         gradients.append(exchange_lon(f"input_grad_{c}", out, -1))
-        if c > 0:
-            values[c + 1 : c + 2] = following
-        elif chunks > 1:
-            values[1] = unit(lambda a: exchange_lat("back_spectra_1", a), values[1])
-
-    if chunks < 4:
-        quarters = gather_quarters(*sum_quarters(part))
+
+    def to_small(small, gradients):
+        input_grad = None
+        for c, arrived in enumerate(gradients):
+            input_grad = unpack(me, arrived, input_grad, c, depth, fields_in.shape, F32)
+        part = exchange_lat("small", small).reshape(lat, -1, width)
+        return jnp.sum(part, axis=0), input_grad
+
+    part, gradients[-2:-1], order[0] = tie(part, gradients[-2:-1], order[0])
+    small, input_grad = unit(to_small, small, gradients[:-1])
     with jax.named_scope("small"):
         bit = 1
         while bit < lon:
             small = small + lax.ppermute(small, "lon", [(i, i ^ bit) for i in range(lon)])
             bit *= 2
-    gradients[:-1], quarters, small = tie(gradients[:-1], quarters, small)
     small = unit(gathered, small)
     gradients[-1], small = tie(gradients[-1], small)
-
-    block_output = input_grad = None
-    for c in range(mids):
-        block_output = unpack(me, outputs[c], block_output, c, depth * pair, fields_in.shape, LOW)
-    for c in range(chunks):
-        input_grad = unpack(me, gradients[c], input_grad, c, depth, fields_in.shape, F32)
-
-    quarters = jnp.stack(quarters)
-    part = jnp.concatenate([take(quarters, (lon_me - z) % lon) for z in range(lon)], axis=0)
+    input_grad = unpack(
+        me, gradients[-1], input_grad, chunks - 1, depth, fields_in.shape, F32
+    )
+
     with jax.named_scope("weights_lat"):
-        summed = lax.all_gather(part, "lat", axis=0, tiled=False).astype(F32)
-    summed = summed.reshape(lat, 2, -1, hidden_width).swapaxes(0, 1).reshape(2, width, hidden_width)
-    grad_weight_in = summed[0, :channels, :units]
-    grad_weight_out = summed[1, :channels, :units].T
+        summed = lax.all_gather(part, "lat", axis=0, tiled=True)
     grad_filter = small[:L, :channels]
     grad_one = jnp.sum(spectral_filter * grad_filter, axis=0) / norm_gains[0]
     grad_gains = jnp.stack([grad_one, small[L, :channels]])
     decay_rate = 1.0 - STEP ** (-0.8)
-    new_weight_in, new_in_rows, new_in_columns = adafactor_matrix(
-        weight_in, grad_weight_in, in_row_stats, in_column_stats, decay_rate
-    )
-    new_weight_out, new_out_rows, new_out_columns = adafactor_matrix(
-        weight_out, grad_weight_out, out_row_stats, out_column_stats, decay_rate
-    )
+    grad_weight_in, new_weight_in, new_in_rows, new_in_columns = adafactor_call(
+        summed, 0, weight_in, in_row_stats, in_column_stats, True, decay_rate
+    )
+    grad_weight_out, new_weight_out, new_out_columns, new_out_rows = adafactor_call(
+        summed, 1, weight_out.T, out_column_stats, out_row_stats, False, decay_rate
+    )
+    grad_weight_out, new_weight_out = grad_weight_out.T, new_weight_out.T
+    new_in_rows, new_in_columns = new_in_rows[:, 0], new_in_columns[0]
+    new_out_rows, new_out_columns = new_out_rows[0], new_out_columns[:, 0]
     new_filter, new_filter_rows, new_filter_columns = adafactor_matrix(
         spectral_filter, grad_filter, filter_row_stats, filter_column_stats, decay_rate
     )

time: 726 us -> 658 us (0.906)
  waiting for transfers between devices: 165 us -> 87 us
  Pallas kernels: 217 us -> 265 us
  blocking collectives: 101 us -> 142 us
  matrix products: 36.4 us -> 0.2 us
  other arithmetic: 41.6 us -> 13.6 us
  starting transfers between devices: 126 us -> 117 us
    ppermute x42 -> x39, waiting for transfers between devices: 96.4 us -> 25.6 us  [exchange_lon(): lax.ppermute(slot, 'lon', [(i, (i + sign * s) % lon) for i in range(lon)])]
    pallas_call x0 -> x3, Pallas kernels: none -> 44.5 us  [the longest x1 29.2 us: weight_sums(): pl.pallas_call(kernel, out_shape=shape, grid=(count * steps,), in_specs=[...]
    all_to_all x5 -> x6, blocking collectives: 101 us -> 142 us  [exchange_lat(): lax.all_to_all(blocks, 'lat', split_axis=0, concat_axis=0, tiled=True)]
    dot_general x4 -> x0, matrix products: 36.2 us -> none  [the longest x2 18.1 us: to_gradients(): jnp.einsum('gc,gh->ch', cot, active, preferred_element_type=F32)]
    all_to_all x9 -> x8, waiting for transfers between devices: 67.2 us -> 53.6 us  [exchange_lat(): lax.all_to_all(blocks, 'lat', split_axis=0, concat_axis=0, tiled=True)]
    all_to_all x9 -> x8, starting transfers between devices: 44.5 us -> 34.8 us  [exchange_lat(): lax.all_to_all(blocks, 'lat', split_axis=0, concat_axis=0, tiled=True)]
    sub x3 -> x1, other arithmetic: 9.71 us -> 0.89 us  [adafactor_matrix(): return (weight_now - scale_now * update, rows_new, columns_new)]
    reduce_sum x3 -> x1, other arithmetic: 7.76 us -> 0.03 us  [to_small(): return (jnp.sum(part, axis=0), input_grad)]
  transfers between devices with their start and end apart: 56 -> 52, of which waited for: 16 -> 12; matrix products, arithmetic and copies ran while one was open for 7% -> 2% of each run, Pallas kernels for 28% -> 38%
where the time goes in v3:
time: 658 us; the launch traced here: 649 us
  Pallas kernels  265 us (40%)
  blocking collectives  142 us (22%)
  starting transfers between devices  117 us (18%)
  waiting for transfers between devices  87 us (13%)
  between operations  16.6 us (3%)
  other arithmetic  13.6 us (2%)
  local copies, waits for them, and re-layouts  7.91 us (1%)
    all_to_all x6, blocking collectives, exchange_lat(): lax.all_to_all(blocks, 'lat', split_axis=0, concat_axis=0, tiled=True)  142 us
    pallas_call x2, Pallas kernels, feed_forward(): pl.pallas_call(kernel, out_shape=outs, grid_spec=pltpu.PrefetchScalarGrid...  82.7 us
    ppermute x39, starting transfers between devices, exchange_lon(): lax.ppermute(slot, 'lon', [(i, (i + sign * s) % lon) for i in range(lon)])  80.3 us
    all_to_all x8, waiting for transfers between devices, exchange_lat(): lax.all_to_all(blocks, 'lat', split_axis=0, concat_axis=0, tiled=True)  53.6 us
    all_to_all x8, starting transfers between devices, exchange_lat(): lax.all_to_all(blocks, 'lat', split_axis=0, concat_axis=0, tiled=True)  34.8 us
    pallas_call x2, Pallas kernels, filter_call(): pl.pallas_call(kernel, out_shape=outs, grid_spec=pltpu.PrefetchScalarGrid...  30 us
    pallas_call x1, Pallas kernels, weight_sums(): pl.pallas_call(kernel, out_shape=shape, grid=(count * steps,), in_specs=[...  29.2 us
    pallas_call x4, Pallas kernels, first_backward(): pl.pallas_call(kernel, out_shape=outs, grid_spec=pltpu.PrefetchScalarGrid...  28.2 us
  transfers between devices with their start and end apart: 52, of which 12 were waited for; matrix products, arithmetic and copies ran while one was open for 2% of the time, Pallas kernels for 38%

profile of v3, /device:TPU:0, one launch (start us, length us, event | category | flops | bytes accessed | tf_op | source)
XLA Modules:
  0.0 648.9 jit_solution(16668013189470674670)
XLA Ops:
  38.6 7.6 %collective-permute-start.3 = (bf16[1296,128]{1,0:T(8,128)(2,1)}, bf16[1296,128]{1,0:T(8,128)(2,1)}, u32[]{:S(2)}, u32[]{:S(2)}) collective-permute-start(bf16[1296,128]{1,0:T(8,128)(2,1)} %get-tuple-element.914), channel_id=1, source_target_pairs={{0,1},{1,2},{2,3},{3,0},{4,5},{5,6},{6,7},{7,4},{8,9},{9,10},{10,1... | collective-permute-start | bytes 995336 | tf_op jit(solution)/shard_map/fields_1/ppermute | solution.py:751
  48.5 26.2 %conditional.15 = (bf16[1,128]{1,0:T(2,128)(2,1)S(1)}, bf16[768,768]{1,0:T(8,128)(2,1)}, bf16[2576,128]{1,0:T(8,128)(2,1)}, bf16[2576,128]{1,0:T(8,128)(2,1)}, b...) conditional(s32[]{:T(128)} %convert_element_type.11, () %tuple.149, (f32[2,641]{1,0:T(2,128)S(1)}, s32[1]{0:T(128)}, ...), branch_computations={%region_0.1_spmd, %region_1.2_spmd} | conditional | flops 2048 | bytes 803539520 | solution.py:770
  62.9 11.8 %all-to-all-done = bf16[8,96,768]{2,1,0:T(8,128)(2,1)} async-done(((bf16[8,96,768]{2,1,0:T(8,128)(2,1)}), bf16[8,96,768]{2,1,0:T(8,128)(2,1)}, u32[]{:S(2)}, u32[]{:S(2)}) %all-to-all-start) | async-done | bytes 1179680 | tf_op jit(solution)/shard_map/cond/branch_1_fun/spectra_0/all_to_all | solution.py:759
  78.7 26.2 %conditional.16 = (bf16[1,128]{1,0:T(2,128)(2,1)S(1)}, bf16[768,768]{1,0:T(8,128)(2,1)}, bf16[2576,128]{1,0:T(8,128)(2,1)}, bf16[2576,128]{1,0:T(8,128)(2,1)}, b...) conditional(s32[]{:T(128)} %convert_element_type.11, () %tuple.153, (s32[1]{0:T(128)}, ...), branch_computations={%region_2.3_spmd, %region_3.4_spmd} | conditional | flops 2048 | bytes 803539008 | solution.py:770
  93.0 11.9 %all-to-all-done.1 = bf16[8,96,768]{2,1,0:T(8,128)(2,1)} async-done(((bf16[8,96,768]{2,1,0:T(8,128)(2,1)}), bf16[8,96,768]{2,1,0:T(8,128)(2,1)}, u32[]{:S(2)}, u32[]{:S(2)}) %all-to-all-start.1) | async-done | bytes 1179680 | tf_op jit(solution)/shard_map/cond/branch_1_fun/spectra_1/all_to_all | solution.py:759
  110.3 25.5 %conditional.17 = (bf16[1,128]{1,0:T(2,128)(2,1)S(1)}, bf16[768,768]{1,0:T(8,128)(2,1)S(1)}) conditional(s32[]{:T(128)} %convert_element_type.11, () %tuple.157, (s32[1]{0:T(128)}, bf16[4,768,256]{2,1,0:T(8,128)(2,1)S(1)}, f32[1,768]{1,0:T(1,128)S(1)}, f32[1,768]{1,0:T(1,128)S(1)}, bf16[1296,128]{1,0:T(8,128)(2,1)}, ...), branch_computations={%region_4.5_spmd, %region_5.6_spmd} | conditional | flops 1024 | bytes 402359296 | solution.py:770
  115.3 20.5 %all_to_all.56 = bf16[8,96,768]{2,1,0:T(8,128)(2,1)S(1)} all-to-all(bf16[8,96,768]{2,1,0:T(8,128)(2,1)} %bitcast.38), channel_id=1, replica_groups=mesh['lat'=8,'lon'=4] {'lat'}, dimensions={0} | all-to-all | bytes 2359296 | tf_op jit(solution)/shard_map/cond/branch_1_fun/spectra_2/all_to_all | solution.py:759
  140.4 26.1 %conditional.18 = (bf16[1,128]{1,0:T(2,128)(2,1)S(1)}, bf16[768,768]{1,0:T(8,128)(2,1)}) conditional(s32[]{:T(128)} %convert_element_type.11, () %tuple.160, (s32[1]{0:T(128)}, bf16[4,768,256]{2,1,0:T(8,128)(2,1)S(1)}, f32[1,768]{1,0:T(1,128)S(1)}, f32[1,768]{1,0:T(1,128)S(1)}, bf16[1296,128]{1,0:T(8,128)(2,1)S(1)}, ...), branch_computations={%region_6.7_spmd, %region_7.8_spmd} | conditional | flops 1024 | bytes 402359296 | solution.py:770
  145.4 21.0 %all_to_all.57 = bf16[8,96,768]{2,1,0:T(8,128)(2,1)} all-to-all(bf16[8,96,768]{2,1,0:T(8,128)(2,1)} %bitcast.39), channel_id=1, replica_groups=mesh['lat'=8,'lon'=4] {'lat'}, dimensions={0} | all-to-all | bytes 2359296 | tf_op jit(solution)/shard_map/cond/branch_1_fun/spectra_3/all_to_all | solution.py:759
  169.0 47.0 %conditional.19 = (bf16[1,128]{1,0:T(2,128)(2,1)S(1)}, bf16[1536,768]{1,0:T(8,128)(2,1)}, bf16[1536,768]{1,0:T(8,128)(2,1)}, f32[6,512,768]{2,1,0:T(8,128)}, bf1...) conditional(s32[]{:T(128)} %convert_element_type.11, () %tuple.147, ...), branch_computations={%region_8.9_spmd, %region_9.10_spmd} | conditional | flops 1024 | bytes 407077984 | solution.py:770
  169.0 13.2 %filter_forward.1 = (bf16[1536,768]{1,0:T(8,128)(2,1)}, bf16[1536,768]{1,0:T(8,128)(2,1)}, f32[6,512,768]{2,1,0:T(8,128)}) custom-call(s32[1]{0:T(128)} %get-tuple-element.441.first_ref, bf16[96,128,128]{2,1,0:T(8,128)(2,1)} %constant.133.clone.1.to_ref, bf16[96,128,128]{2,1,0:T(8,128)(2,1)} %constant.134.clone.1.back_ref, ...), custom_call_target="tpu_custom_call" | custom-call | flops 1024 | bytes 400000000 | tf_op jit(solution)/shard_map/cond/branch_1_fun/filter_forward/pallas_call | solution.py:261
  193.6 22.5 %all-to-all-done.4 = bf16[8,192,768]{2,1,0:T(8,128)(2,1)} async-done(((bf16[8,192,768]{2,1,0:T(8,128)(2,1)}), bf16[8,192,768]{2,1,0:T(8,128)(2,1)}, u32[]{:S(2)}, u32[]{:S(2)}) %all-to-all-start.4) | async-done | bytes 2359328 | tf_op jit(solution)/shard_map/cond/branch_1_fun/synthesis_0/all_to_all | solution.py:759
  217.8 46.2 %conditional.20 = (bf16[1,128]{1,0:T(2,128)(2,1)S(1)}, bf16[2576,128]{1,0:T(8,128)(2,1)}, bf16[2576,128]{1,0:T(8,128)(2,1)}, bf16[2576,128]{1,0:T(8,128)(2,1)}, ...) conditional(s32[]{:T(128)} %convert_element_type.11, () %tuple.166, ...), branch_computations={%region_10.11_spmd, %region_11.12_spmd} | conditional | flops 1024 | bytes 408405152 | solution.py:770
  222.6 41.4 %feed_forward.2 = (bf16[2576,128]{1,0:T(8,128)(2,1)}, bf16[2576,128]{1,0:T(8,128)(2,1)}, bf16[2576,128]{1,0:T(8,128)(2,1)}, bf16[2576,128]{1,0:T(8,128)(2,1)}, f...) custom-call(s32[1]{0:T(128)} %get-tuple-element.461.me_ref, ...), custom_call_target="tpu_custom_call" | custom-call | flops 1024 | bytes 400000000 | tf_op jit(solution)/shard_map/cond/branch_1_fun/feed_forward/pallas_call | solution.py:506
  273.6 46.2 %conditional.21 = (bf16[1,128]{1,0:T(2,128)(2,1)S(1)}, bf16[1296,128]{1,0:T(8,128)(2,1)}, bf16[1296,128]{1,0:T(8,128)(2,1)}, bf16[1296,128]{1,0:T(8,128)(2,1)}, ...) conditional(s32[]{:T(128)} %convert_element_type.11, () %tuple.165, ...), branch_computations={%region_12.13_spmd, %region_13.14_spmd} | conditional | flops 1024 | bytes 408405184 | solution.py:770
  278.6 41.3 %feed_forward.3 = (bf16[1296,128]{1,0:T(8,128)(2,1)}, bf16[1296,128]{1,0:T(8,128)(2,1)}, bf16[1296,128]{1,0:T(8,128)(2,1)}, bf16[1296,128]{1,0:T(8,128)(2,1)}, b...) custom-call(s32[1]{0:T(128)} %get-tuple-element.496.me_ref, ...), custom_call_target="tpu_custom_call" | custom-call | flops 1024 | bytes 400000000 | tf_op jit(solution)/shard_map/cond/branch_1_fun/feed_forward/pallas_call | solution.py:506
  331.9 34.2 %conditional.22 = (bf16[1,128]{1,0:T(2,128)(2,1)S(1)}, bf16[1536,768]{1,0:T(8,128)(2,1)}, f32[1536,1408]{1,0:T(8,128)}) conditional(s32[]{:T(128)} %convert_element_type.11, () %tuple.169, (bf16[1536,768]{1,0:T(8,128)(2,1)}, bf16[2048,768]{1,0:T(8,128)(2,1)}, bf16[2048,1408]{1,0:T(8,128)(2,1)}, bf16[2048,1408]{1,0:T(8,128)(2,1)}, ...), branch_computations={%region_14.15_spmd, %region_15.16_spmd} | conditional | flops 1024 | bytes 407077952 | solution.py:770
  336.7 29.2 %weight_sums.1 = f32[1536,1408]{1,0:T(8,128)} custom-call(bf16[2048,768]{1,0:T(8,128)(2,1)} %get-tuple-element.536.refs_0_, bf16[2048,1408]{1,0:T(8,128)(2,1)} %get-tuple-element.537.refs_1_, bf16[2048,1408]{1,0:T(8,128)(2,1)} %get-tuple-element.538.refs_2_, bf16[2048,768]{1,0:T(8,128)(2,1)} %get-tuple-element.539.refs_3_, ...), custom_call_target="tpu_custom_call" | custom-call | flops 1024 | bytes 400000000 | tf_op jit(solution)/shard_map/cond/branch_1_fun/weight_sums/pallas_call | solution.py:562
  369.2 19.4 %conditional.23 = (bf16[1,128]{1,0:T(2,128)(2,1)S(1)}, bf16[768,768]{1,0:T(8,128)(2,1)S(1)}, bf16[768,768]{1,0:T(8,128)(2,1)}, bf16[768,768]{1,0:T(8,128)(2,1)},...) conditional(s32[]{:T(128)} %convert_element_type.11, () %tuple.145, (s32[1]{0:T(128)}, ...), branch_computations={%region_16.17_spmd, %region_17.20_spmd.clone} | conditional | flops 602368 | bytes 401058368 | solution.py:770
  369.2 16.8 %filter_backward.1 = (bf16[768,768]{1,0:T(8,128)(2,1)S(1)}, bf16[768,768]{1,0:T(8,128)(2,1)}, bf16[768,768]{1,0:T(8,128)(2,1)}, bf16[768,768]{1,0:T(8,128)(2,1)}, f32[128,768]{1,0:T(8,128)}) custom-call(s32[1]{0:T(128)} %get-tuple-element.1118.first_ref, bf16[96,128,128]{2,1,0:T(8,128)(2,1)} %constant.132.clone.2.to_ref, ...), custom_call_target="tpu_custom_call" | custom-call | flops 1024 | bytes 400000000 | tf_op jit(solution)/shard_map/cond/branch_1_fun/filter_backward/pallas_call | solution.py:261
  388.6 40.8 %conditional.24 = (bf16[1,128]{1,0:T(2,128)(2,1)S(1)}, bf16[1296,128]{1,0:T(8,128)(2,1)}, bf16[1296,128]{1,0:T(8,128)(2,1)}, bf16[1296,128]{1,0:T(8,128)(2,1)}, bf16[1296,128]{1,0:T(8,128)(2,1)}) conditional(s32[]{:T(128)} %convert_element_type.11, () %tuple.174, (bf16[768,768]{1,0:T(8,128)(2,1)S(1)}, s32[1]{0:T(128)}, ...), branch_computations={%region_20.21_spmd, %region_21.22_spmd} | conditional | flops 1024 | bytes 403686464 | solution.py:770
  388.6 33.6 %all_to_all.58 = bf16[8,96,768]{2,1,0:T(8,128)(2,1)} all-to-all(bf16[8,96,768]{2,1,0:T(8,128)(2,1)S(1)} %bitcast.40), channel_id=1, replica_groups=mesh['lat'=8,'lon'=4] {'lat'}, dimensions={0} | all-to-all | bytes 2359296 | tf_op jit(solution)/shard_map/cond/branch_1_fun/back_spectra_0/all_to_all | solution.py:759
  434.4 35.0 %conditional.25 = (bf16[1,128]{1,0:T(2,128)(2,1)S(1)}, bf16[1296,128]{1,0:T(8,128)(2,1)}, bf16[1296,128]{1,0:T(8,128)(2,1)}, bf16[1296,128]{1,0:T(8,128)(2,1)}, bf16[1296,128]{1,0:T(8,128)(2,1)}) conditional(s32[]{:T(128)} %convert_element_type.11, () %tuple.177, (bf16[768,768]{1,0:T(8,128)(2,1)}, s32[1]{0:T(128)}, ...), branch_computations={%region_22.23_spmd, %region_23.24_spmd} | conditional | flops 1024 | bytes 402359328 | solution.py:770
  434.4 27.8 %all_to_all.59 = bf16[8,96,768]{2,1,0:T(8,128)(2,1)} all-to-all(bf16[8,96,768]{2,1,0:T(8,128)(2,1)} %bitcast.19), channel_id=1, replica_groups=mesh['lat'=8,'lon'=4] {'lat'}, dimensions={0} | all-to-all | bytes 2359296 | tf_op jit(solution)/shard_map/cond/branch_1_fun/back_spectra_1/all_to_all | solution.py:759
  476.0 28.0 %conditional.26 = (bf16[1,128]{1,0:T(2,128)(2,1)S(1)}, bf16[1296,128]{1,0:T(8,128)(2,1)}, bf16[1296,128]{1,0:T(8,128)(2,1)}, bf16[1296,128]{1,0:T(8,128)(2,1)}, bf16[1296,128]{1,0:T(8,128)(2,1)}) conditional(s32[]{:T(128)} %convert_element_type.11, () %tuple.179, (bf16[768,768]{1,0:T(8,128)(2,1)}, s32[1]{0:T(128)}, ...), branch_computations={%region_25.26_spmd, %region_26.27_spmd} | conditional | flops 1024 | bytes 403686464 | solution.py:770
  476.0 21.2 %all_to_all.60 = bf16[8,96,768]{2,1,0:T(8,128)(2,1)} all-to-all(bf16[8,96,768]{2,1,0:T(8,128)(2,1)} %bitcast.21), channel_id=1, replica_groups=mesh['lat'=8,'lon'=4] {'lat'}, dimensions={0} | all-to-all | bytes 2359296 | tf_op jit(solution)/shard_map/cond/branch_1_fun/back_spectra_2/all_to_all | solution.py:759
  511.0 28.5 %conditional.27 = (bf16[1,128]{1,0:T(2,128)(2,1)S(1)}, bf16[1296,128]{1,0:T(8,128)(2,1)S(1)}, bf16[1296,128]{1,0:T(8,128)(2,1)}, bf16[1296,128]{1,0:T(8,128)(2,1...) conditional(s32[]{:T(128)} %convert_element_type.11, () %tuple.144, ...), branch_computations={%region_27.28_spmd, %region_28.29_spmd} | conditional | flops 4096 | bytes 1610911872 | solution.py:770
  547.1 13.9 %collective-permute-start.34 = (bf16[1296,128]{1,0:T(8,128)(2,1)}, bf16[1296,128]{1,0:T(8,128)(2,1)S(1)}, u32[]{:S(2)}, u32[]{:S(2)}) collective-permute-start(bf16[1296,128]{1,0:T(8,128)(2,1)} %get-tuple-element.1071), channel_id=1, source_target_pairs={{0,2},{1,3},{2,0},{3,1},{4,6},{5,7},{6,4},{7,5},{8,10},{9,11},{10,... | collective-permute-start | bytes 995336 | tf_op jit(solution)/shard_map/input_grad_3/ppermute | solution.py:751
  563.0 17.1 %conditional.28 = (bf16[1,128]{1,0:T(2,128)(2,1)S(1)}, f32[24,768]{1,0:T(8,128)S(1)}, f32[4,16,64,641]{3,2,1,0:T(8,128)}) conditional(s32[]{:T(128)} %convert_element_type.11, () %tuple.186, (f32[192,768]{1,0:T(8,128)}, s32[1]{0:T(128)}, bf16[1296,128]{1,0:T(8,128)(2,1)}, bf16[1296,128]{1,0:T(8,128)(2,1)}, bf16[1296,128]{1,0:T(8,128)(2,1)}, ...), branch_computations={%region_30.31_spmd, %region_31.33_spmd} | conditional | flops 132096 | bytes 1203760128 | solution.py:770
  592.6 17.6 %conditional.29 = (f32[192,768]{1,0:T(8,128)S(1)}) conditional(s32[]{:T(128)} %convert_element_type.11, () %tuple.185, (f32[24,768]{1,0:T(8,128)S(1)}, f32[24,768]{1,0:T(8,128)S(1)}) %tuple.189), branch_computations={%region_33.34_spmd, %region_34.35_spmd} | conditional | flops 18432 | bytes 2064392 | solution.py:770
  592.6 17.5 %all_to_all.61 = f32[8,24,768]{2,1,0:T(8,128)S(1)} all-to-all(f32[8,24,768]{2,1,0:T(8,128)S(1)} %broadcast_in_dim.2), channel_id=1, replica_groups=mesh['lat'=8,'lon'=4] {'lat'}, dimensions={0} | all-to-all | bytes 1179648 | tf_op jit(solution)/shard_map/cond/branch_1_fun/gather/all_to_all | solution.py:759
  631.0 8.0 %adafactor.3 = (f32[641,1282]{1,0:T(8,128)}, f32[641,1282]{1,0:T(8,128)}, f32[641,1]{1,0:T(8,128)}, f32[1,1282]{1,0:T(1,128)}) custom-call(bf16[1536,1408]{1,0:T(8,128)(2,1)} %all-gather.2.cloned.1.call-done.grad_ref, f32[641,1282]{1,0:T(8,128)} %bitcast.33, f32[641,1]{1,0:T(8,128)} %broadcast_in_dim.20.rows_ref, f32[1,1282]{1,0:T(1,128)} %broadcast_in_dim.18.columns_ref), custom_call_target="tpu_custom_call" | custom-call | flops 1024 | bytes 400000000 | tf_op jit(solution)/shard_map/adafactor/pallas_call | solution.py:668
  (265 shorter events, 272.9 us)
Async XLA Ops:
  7.2 465.4 %reduce-scatter.2.cloned.1.call-start = ((), (), s32[]{:S(2)}) async-start(), calls=%async_computation.15 | async-start | bytes 9732096 | tf_op jit(solution)/shard_map/weights_lat/reduce_scatter | solution.py:948
  38.6 36.2 %collective-permute-start.3 = (bf16[1296,128]{1,0:T(8,128)(2,1)}, bf16[1296,128]{1,0:T(8,128)(2,1)}, u32[]{:S(2)}, u32[]{:S(2)}) collective-permute-start(bf16[1296,128]{1,0:T(8,128)(2,1)} %get-tuple-element.914), channel_id=1, source_target_pairs={{0,1},{1,2},{2,3},{3,0},{4,5},{5,6},{6,7},{7,4},{8,9},{9,10},{10,1... | collective-permute-start | bytes 995336 | tf_op jit(solution)/shard_map/fields_1/ppermute | solution.py:751
  135.8 80.3 %collective-permute-start.12 = (bf16[2576,128]{1,0:T(8,128)(2,1)}, bf16[2576,128]{1,0:T(8,128)(2,1)}, u32[]{:S(2)}, u32[]{:S(2)}) collective-permute-start(bf16[2576,128]{1,0:T(8,128)(2,1)} %get-tuple-element.991), channel_id=1, source_target_pairs={{0,1},{1,2},{2,3},{3,0},{4,5},{5,6},{6,7},{7,4},{8,9},{9,10},{10,1... | collective-permute-start | bytes 1978376 | tf_op jit(solution)/shard_map/upstream_0/ppermute | solution.py:751
  138.0 79.8 %collective-permute-start.13 = (bf16[2576,128]{1,0:T(8,128)(2,1)}, bf16[2576,128]{1,0:T(8,128)(2,1)}, u32[]{:S(2)}, u32[]{:S(2)}) collective-permute-start(bf16[2576,128]{1,0:T(8,128)(2,1)} %get-tuple-element.992), channel_id=1, source_target_pairs={{0,2},{1,3},{2,0},{3,1},{4,6},{5,7},{6,4},{7,5},{8,10},{9,11},{10,... | collective-permute-start | bytes 1978376 | tf_op jit(solution)/shard_map/upstream_0/ppermute | solution.py:751
  140.3 77.5 %collective-permute-start.14 = (bf16[2576,128]{1,0:T(8,128)(2,1)}, bf16[2576,128]{1,0:T(8,128)(2,1)}, u32[]{:S(2)}, u32[]{:S(2)}) collective-permute-start(bf16[2576,128]{1,0:T(8,128)(2,1)} %get-tuple-element.993), channel_id=1, source_target_pairs={{0,3},{1,0},{2,1},{3,2},{4,7},{5,4},{6,5},{7,6},{8,11},{9,8},{10,9... | collective-permute-start | bytes 1978376 | tf_op jit(solution)/shard_map/upstream_0/ppermute | solution.py:751
  166.4 107.2 %collective-permute-start.15 = (bf16[2576,128]{1,0:T(8,128)(2,1)}, bf16[2576,128]{1,0:T(8,128)(2,1)}, u32[]{:S(2)}, u32[]{:S(2)}) collective-permute-start(bf16[2576,128]{1,0:T(8,128)(2,1)} %get-tuple-element.998), channel_id=1, source_target_pairs={{0,1},{1,2},{2,3},{3,0},{4,5},{5,6},{6,7},{7,4},{8,9},{9,10},{10,1... | collective-permute-start | bytes 1978376 | tf_op jit(solution)/shard_map/upstream_1/ppermute | solution.py:751
  168.4 105.2 %collective-permute-start.16 = (bf16[2576,128]{1,0:T(8,128)(2,1)}, bf16[2576,128]{1,0:T(8,128)(2,1)}, u32[]{:S(2)}, u32[]{:S(2)}) collective-permute-start(bf16[2576,128]{1,0:T(8,128)(2,1)} %get-tuple-element.999), channel_id=1, source_target_pairs={{0,2},{1,3},{2,0},{3,1},{4,6},{5,7},{6,4},{7,5},{8,10},{9,11},{10,... | collective-permute-start | bytes 1978376 | tf_op jit(solution)/shard_map/upstream_1/ppermute | solution.py:751
  216.1 57.5 %collective-permute-start.17 = (bf16[2576,128]{1,0:T(8,128)(2,1)}, bf16[2576,128]{1,0:T(8,128)(2,1)}, u32[]{:S(2)}, u32[]{:S(2)}) collective-permute-start(bf16[2576,128]{1,0:T(8,128)(2,1)} %get-tuple-element.1000), channel_id=1, source_target_pairs={{0,3},{1,0},{2,1},{3,2},{4,7},{5,4},{6,5},{7,6},{8,11},{9,8},{10,9... | collective-permute-start | bytes 1978376 | tf_op jit(solution)/shard_map/upstream_1/ppermute | solution.py:751
  217.8 46.2 %all-to-all-start.5 = ((bf16[8,192,768]{2,1,0:T(8,128)(2,1)}), bf16[8,192,768]{2,1,0:T(8,128)(2,1)}, u32[]{:S(2)}, u32[]{:S(2)}) async-start(bf16[8,192,768]{2,1,0:T(8,128)(2,1)} %bitcast.11), calls=%async_computation.5 | async-start | bytes 4718592 | tf_op jit(solution)/shard_map/cond/branch_1_fun/synthesis_1/all_to_all | solution.py:759
  264.0 59.7 %collective-permute-start.21 = (bf16[2576,128]{1,0:T(8,128)(2,1)}, bf16[2576,128]{1,0:T(8,128)(2,1)}, u32[]{:S(2)}, u32[]{:S(2)}) collective-permute-start(bf16[2576,128]{1,0:T(8,128)(2,1)} %get-tuple-element.1009), channel_id=1, source_target_pairs={{0,3},{1,0},{2,1},{3,2},{4,7},{5,4},{6,5},{7,6},{8,11},{9,8},{10,9... | collective-permute-start | bytes 1978376 | tf_op jit(solution)/shard_map/output_0_0/ppermute | solution.py:751
  266.1 65.9 %collective-permute-start.22 = (bf16[2576,128]{1,0:T(8,128)(2,1)}, bf16[2576,128]{1,0:T(8,128)(2,1)}, u32[]{:S(2)}, u32[]{:S(2)}) collective-permute-start(bf16[2576,128]{1,0:T(8,128)(2,1)} %get-tuple-element.1010), channel_id=1, source_target_pairs={{0,2},{1,3},{2,0},{3,1},{4,6},{5,7},{6,4},{7,5},{8,10},{9,11},{10,... | collective-permute-start | bytes 1978376 | tf_op jit(solution)/shard_map/output_0_0/ppermute | solution.py:751
  273.6 58.4 %collective-permute-start.23 = (bf16[2576,128]{1,0:T(8,128)(2,1)}, bf16[2576,128]{1,0:T(8,128)(2,1)}, u32[]{:S(2)}, u32[]{:S(2)}) collective-permute-start(bf16[2576,128]{1,0:T(8,128)(2,1)} %get-tuple-element.1011), channel_id=1, source_target_pairs={{0,1},{1,2},{2,3},{3,0},{4,5},{5,6},{6,7},{7,4},{8,9},{9,10},{10,1... | collective-permute-start | bytes 1978376 | tf_op jit(solution)/shard_map/output_0_0/ppermute | solution.py:751
  273.6 46.2 %all-to-all-start.6 = ((bf16[8,192,768]{2,1,0:T(8,128)(2,1)}), bf16[8,192,768]{2,1,0:T(8,128)(2,1)}, u32[]{:S(2)}, u32[]{:S(2)}) async-start(bf16[8,192,768]{2,1,0:T(8,128)(2,1)} %bitcast.13), calls=%async_computation.6 | async-start | bytes 4718592 | tf_op jit(solution)/shard_map/cond/branch_1_fun/back_synthesis_0/all_to_all | solution.py:759
  319.9 46.3 %collective-permute-start.18 = (bf16[1296,128]{1,0:T(8,128)(2,1)}, bf16[1296,128]{1,0:T(8,128)(2,1)S(1)}, u32[]{:S(2)}, u32[]{:S(2)}) collective-permute-start(bf16[1296,128]{1,0:T(8,128)(2,1)} %get-tuple-element.1005), channel_id=1, source_target_pairs={{0,3},{1,0},{2,1},{3,2},{4,7},{5,4},{6,5},{7,6},{8,11},{9,8},{10,9... | collective-permute-start | bytes 995336 | tf_op jit(solution)/shard_map/output_1_0/ppermute | solution.py:751
  323.7 42.4 %collective-permute-start.19 = (bf16[1296,128]{1,0:T(8,128)(2,1)}, bf16[1296,128]{1,0:T(8,128)(2,1)S(1)}, u32[]{:S(2)}, u32[]{:S(2)}) collective-permute-start(bf16[1296,128]{1,0:T(8,128)(2,1)} %get-tuple-element.1006), channel_id=1, source_target_pairs={{0,2},{1,3},{2,0},{3,1},{4,6},{5,7},{6,4},{7,5},{8,10},{9,11},{10,... | collective-permute-start | bytes 995336 | tf_op jit(solution)/shard_map/output_1_0/ppermute | solution.py:751
  323.7 42.5 %collective-permute-start.20 = (bf16[1296,128]{1,0:T(8,128)(2,1)}, bf16[1296,128]{1,0:T(8,128)(2,1)S(1)}, u32[]{:S(2)}, u32[]{:S(2)}) collective-permute-start(bf16[1296,128]{1,0:T(8,128)(2,1)} %get-tuple-element.1007), channel_id=1, source_target_pairs={{0,1},{1,2},{2,3},{3,0},{4,5},{5,6},{6,7},{7,4},{8,9},{9,10},{10,1... | collective-permute-start | bytes 995336 | tf_op jit(solution)/shard_map/output_1_0/ppermute | solution.py:751
  367.1 179.9 %all-reduce.7.cloned.1.call-start = ((), (), s32[]{:S(2)}) async-start(), calls=%async_computation.16 | async-start | bytes 1081344 | tf_op jit(solution)/shard_map/weights_lon/psum | solution.py:956
  367.1 65.2 %collective-permute-start.24 = (bf16[1296,128]{1,0:T(8,128)(2,1)}, bf16[1296,128]{1,0:T(8,128)(2,1)}, u32[]{:S(2)}, u32[]{:S(2)}) collective-permute-start(bf16[1296,128]{1,0:T(8,128)(2,1)} %get-tuple-element.1040), channel_id=1, source_target_pairs={{0,3},{1,0},{2,1},{3,2},{4,7},{5,4},{6,5},{7,6},{8,11},{9,8},{10,9... | collective-permute-start | bytes 995336 | tf_op jit(solution)/shard_map/output_1_1/ppermute | solution.py:751
  367.1 67.2 %collective-permute-start.25 = (bf16[1296,128]{1,0:T(8,128)(2,1)}, bf16[1296,128]{1,0:T(8,128)(2,1)}, u32[]{:S(2)}, u32[]{:S(2)}) collective-permute-start(bf16[1296,128]{1,0:T(8,128)(2,1)} %get-tuple-element.1041), channel_id=1, source_target_pairs={{0,2},{1,3},{2,0},{3,1},{4,6},{5,7},{6,4},{7,5},{8,10},{9,11},{10,... | collective-permute-start | bytes 995336 | tf_op jit(solution)/shard_map/output_1_1/ppermute | solution.py:751
  367.2 67.2 %collective-permute-start.26 = (bf16[1296,128]{1,0:T(8,128)(2,1)}, bf16[1296,128]{1,0:T(8,128)(2,1)}, u32[]{:S(2)}, u32[]{:S(2)}) collective-permute-start(bf16[1296,128]{1,0:T(8,128)(2,1)} %get-tuple-element.1042), channel_id=1, source_target_pairs={{0,1},{1,2},{2,3},{3,0},{4,5},{5,6},{6,7},{7,4},{8,9},{9,10},{10,1... | collective-permute-start | bytes 995336 | tf_op jit(solution)/shard_map/output_1_1/ppermute | solution.py:751
  429.4 45.5 %collective-permute-start.30 = (bf16[1296,128]{1,0:T(8,128)(2,1)}, bf16[1296,128]{1,0:T(8,128)(2,1)}, u32[]{:S(2)}, u32[]{:S(2)}) collective-permute-start(bf16[1296,128]{1,0:T(8,128)(2,1)} %get-tuple-element.1059), channel_id=1, source_target_pairs={{0,3},{1,0},{2,1},{3,2},{4,7},{5,4},{6,5},{7,6},{8,11},{9,8},{10,9... | collective-permute-start | bytes 995336 | tf_op jit(solution)/shard_map/input_grad_0/ppermute | solution.py:751
  431.4 44.6 %collective-permute-start.31 = (bf16[1296,128]{1,0:T(8,128)(2,1)}, bf16[1296,128]{1,0:T(8,128)(2,1)}, u32[]{:S(2)}, u32[]{:S(2)}) collective-permute-start(bf16[1296,128]{1,0:T(8,128)(2,1)} %get-tuple-element.1060), channel_id=1, source_target_pairs={{0,2},{1,3},{2,0},{3,1},{4,6},{5,7},{6,4},{7,5},{8,10},{9,11},{10,... | collective-permute-start | bytes 995336 | tf_op jit(solution)/shard_map/input_grad_0/ppermute | solution.py:751
  432.4 43.6 %collective-permute-start.32 = (bf16[1296,128]{1,0:T(8,128)(2,1)}, bf16[1296,128]{1,0:T(8,128)(2,1)}, u32[]{:S(2)}, u32[]{:S(2)}) collective-permute-start(bf16[1296,128]{1,0:T(8,128)(2,1)} %get-tuple-element.1061), channel_id=1, source_target_pairs={{0,1},{1,2},{2,3},{3,0},{4,5},{5,6},{6,7},{7,4},{8,9},{9,10},{10,1... | collective-permute-start | bytes 995336 | tf_op jit(solution)/shard_map/input_grad_0/ppermute | solution.py:751
  469.3 38.6 %collective-permute-start.27 = (bf16[1296,128]{1,0:T(8,128)(2,1)}, bf16[1296,128]{1,0:T(8,128)(2,1)}, u32[]{:S(2)}, u32[]{:S(2)}) collective-permute-start(bf16[1296,128]{1,0:T(8,128)(2,1)} %get-tuple-element.1054), channel_id=1, source_target_pairs={{0,3},{1,0},{2,1},{3,2},{4,7},{5,4},{6,5},{7,6},{8,11},{9,8},{10,9... | collective-permute-start | bytes 995336 | tf_op jit(solution)/shard_map/input_grad_1/ppermute | solution.py:751
  474.8 145.9 %all-gather.2.cloned.1.call-start = ((), (), s32[]{:S(2)}) async-start(), calls=%async_computation.17 | async-start | bytes 4866048 | tf_op jit(solution)/shard_map/weights_lat/all_gather | solution.py:1010
  474.8 36.2 %collective-permute-start.28 = (bf16[1296,128]{1,0:T(8,128)(2,1)}, bf16[1296,128]{1,0:T(8,128)(2,1)}, u32[]{:S(2)}, u32[]{:S(2)}) collective-permute-start(bf16[1296,128]{1,0:T(8,128)(2,1)} %get-tuple-element.1055), channel_id=1, source_target_pairs={{0,2},{1,3},{2,0},{3,1},{4,6},{5,7},{6,4},{7,5},{8,10},{9,11},{10,... | collective-permute-start | bytes 995336 | tf_op jit(solution)/shard_map/input_grad_1/ppermute | solution.py:751
  474.9 36.1 %collective-permute-start.29 = (bf16[1296,128]{1,0:T(8,128)(2,1)}, bf16[1296,128]{1,0:T(8,128)(2,1)}, u32[]{:S(2)}, u32[]{:S(2)}) collective-permute-start(bf16[1296,128]{1,0:T(8,128)(2,1)} %get-tuple-element.1056), channel_id=1, source_target_pairs={{0,1},{1,2},{2,3},{3,0},{4,5},{5,6},{6,7},{7,4},{8,9},{9,10},{10,1... | collective-permute-start | bytes 995336 | tf_op jit(solution)/shard_map/input_grad_1/ppermute | solution.py:751
  506.9 40.2 %collective-permute-start.37 = (bf16[1296,128]{1,0:T(8,128)(2,1)}, bf16[1296,128]{1,0:T(8,128)(2,1)}, u32[]{:S(2)}, u32[]{:S(2)}) collective-permute-start(bf16[1296,128]{1,0:T(8,128)(2,1)} %get-tuple-element.1085), channel_id=1, source_target_pairs={{0,2},{1,3},{2,0},{3,1},{4,6},{5,7},{6,4},{7,5},{8,10},{9,11},{10,... | collective-permute-start | bytes 995336 | tf_op jit(solution)/shard_map/input_grad_2/ppermute | solution.py:751
  507.9 39.1 %collective-permute-start.38 = (bf16[1296,128]{1,0:T(8,128)(2,1)}, bf16[1296,128]{1,0:T(8,128)(2,1)}, u32[]{:S(2)}, u32[]{:S(2)}) collective-permute-start(bf16[1296,128]{1,0:T(8,128)(2,1)} %get-tuple-element.1086), channel_id=1, source_target_pairs={{0,1},{1,2},{2,3},{3,0},{4,5},{5,6},{6,7},{7,4},{8,9},{9,10},{10,1... | collective-permute-start | bytes 995336 | tf_op jit(solution)/shard_map/input_grad_2/ppermute | solution.py:751
  547.1 63.0 %collective-permute-start.33 = (bf16[1296,128]{1,0:T(8,128)(2,1)}, bf16[1296,128]{1,0:T(8,128)(2,1)S(1)}, u32[]{:S(2)}, u32[]{:S(2)}) collective-permute-start(bf16[1296,128]{1,0:T(8,128)(2,1)} %get-tuple-element.1070), channel_id=1, source_target_pairs={{0,3},{1,0},{2,1},{3,2},{4,7},{5,4},{6,5},{7,6},{8,11},{9,8},{10,9... | collective-permute-start | bytes 995336 | tf_op jit(solution)/shard_map/input_grad_3/ppermute | solution.py:751
  547.1 63.0 %collective-permute-start.34 = (bf16[1296,128]{1,0:T(8,128)(2,1)}, bf16[1296,128]{1,0:T(8,128)(2,1)S(1)}, u32[]{:S(2)}, u32[]{:S(2)}) collective-permute-start(bf16[1296,128]{1,0:T(8,128)(2,1)} %get-tuple-element.1071), channel_id=1, source_target_pairs={{0,2},{1,3},{2,0},{3,1},{4,6},{5,7},{6,4},{7,5},{8,10},{9,11},{10,... | collective-permute-start | bytes 995336 | tf_op jit(solution)/shard_map/input_grad_3/ppermute | solution.py:751
  561.1 49.1 %collective-permute-start.35 = (bf16[1296,128]{1,0:T(8,128)(2,1)}, bf16[1296,128]{1,0:T(8,128)(2,1)S(1)}, u32[]{:S(2)}, u32[]{:S(2)}) collective-permute-start(bf16[1296,128]{1,0:T(8,128)(2,1)} %get-tuple-element.1072), channel_id=1, source_target_pairs={{0,1},{1,2},{2,3},{3,0},{4,5},{5,6},{6,7},{7,4},{8,9},{9,10},{10,1... | collective-permute-start | bytes 995336 | tf_op jit(solution)/shard_map/input_grad_3/ppermute | solution.py:751
  (70 other events, 1310.7 us)
Sparse Core Ops, SparseCore 0:
  366.4 94.8 reduce-scatter.1
  474.9 67.8 all-reduce.6
  547.2 53.2 all-gather.1

commit v4 on v3

--- a/solution.py
+++ b/solution.py
@@ -649,8 +649,11 @@
         columns_mean = jnp.sum(squares, axis=0, keepdims=True) * (1.0 / height)
         rows_new = decay_rate * rows_ref[...] + (1.0 - decay_rate) * rows_mean
         columns_new = decay_rate * columns_ref[...] + (1.0 - decay_rate) * columns_mean
-        rows_out[...] = rows_new
-        columns_out[...] = columns_new
+        across = lax.broadcasted_iota(jnp.int32, (height, height), 0)
+        along = lax.broadcasted_iota(jnp.int32, (height, height), 1)
+        turned = jnp.sum(jnp.where(across == along, rows_new, 0.0), axis=0, keepdims=True)
+        rows_out[...] = turned[0]
+        columns_out[...] = columns_new[0]
         mean = jnp.mean(rows_new) if by_rows else jnp.mean(columns_new)
         update = gradient * (lax.rsqrt(rows_new / mean) * lax.rsqrt(columns_new))
         weight = weight_ref[...]
@@ -659,11 +662,11 @@
         rate = STEP_RATE * jnp.maximum(SECOND_EPS, jnp.sqrt(jnp.sum(weight * weight) * size))
         new[...] = weight - update * (rate / clip)
 
-    whole = lambda a: pl.BlockSpec(a.shape, lambda i: (0, 0))
+    whole = lambda a: pl.BlockSpec(a.shape, lambda i: (0,) * len(a.shape))
     tall, wide = gradients.shape
     matrix = jax.ShapeDtypeStruct((height, width), F32)
     outs = [matrix, matrix]
-    outs += [jax.ShapeDtypeStruct((height, 1), F32), jax.ShapeDtypeStruct((1, width), F32)]
+    outs += [jax.ShapeDtypeStruct((height,), F32), jax.ShapeDtypeStruct((width,), F32)]
     arrays = [weight_now, rows_old[:, None], columns_old[None]]
     return pl.pallas_call(
         kernel,
@@ -938,10 +941,10 @@
         return values, spread(jnp.concatenate([filter_part, gain_part[None]], axis=0))
 
     early = mids - 1
-    outputs[:early], backs[-1] = tie(outputs[:early], backs[-1])
     backs[-1], weight_part = unit(to_weights, backs[-1], parts)
-    outputs[early:-1], backs[-1], weight_part = tie(outputs[early:-1], backs[-1], weight_part)
+    outputs[:early], order[0], weight_part = tie(outputs[:early], order[0], weight_part)
     values, small = unit(to_gradients, backs, coefs, gain_parts)
+    outputs[early:-1], order[0] = tie(outputs[early:-1], order[0])
 
     gradients = []
     with jax.named_scope("weights_lat"):
@@ -1000,27 +1003,31 @@
         while bit < lon:
             small = small + lax.ppermute(small, "lon", [(i, i ^ bit) for i in range(lon)])
             bit *= 2
-    small = unit(gathered, small)
+    with jax.named_scope("weights_lat"):
+        summed = lax.all_gather(part, "lat", axis=0, tiled=True)
+    decay_rate = 1.0 - STEP ** (-0.8)
+
+    def to_updates(small, summed, weight_in, weight_out):
+        inner = adafactor_call(
+            summed, 0, weight_in, in_row_stats, in_column_stats, True, decay_rate
+        )
+        outer = adafactor_call(
+            summed, 1, weight_out.T, out_column_stats, out_row_stats, False, decay_rate
+        )
+        return gathered(small), inner, outer
+
+    small, inner, outer = unit(to_updates, small, summed, weight_in, weight_out)
+    grad_weight_in, new_weight_in, new_in_rows, new_in_columns = inner
+    grad_weight_out, new_weight_out, new_out_columns, new_out_rows = outer
     gradients[-1], small = tie(gradients[-1], small)
     input_grad = unpack(
         me, gradients[-1], input_grad, chunks - 1, depth, fields_in.shape, F32
     )
 
-    with jax.named_scope("weights_lat"):
-        summed = lax.all_gather(part, "lat", axis=0, tiled=True)
     grad_filter = small[:L, :channels]
     grad_one = jnp.sum(spectral_filter * grad_filter, axis=0) / norm_gains[0]
     grad_gains = jnp.stack([grad_one, small[L, :channels]])
-    decay_rate = 1.0 - STEP ** (-0.8)
-    grad_weight_in, new_weight_in, new_in_rows, new_in_columns = adafactor_call(
-        summed, 0, weight_in, in_row_stats, in_column_stats, True, decay_rate
-    )
-    grad_weight_out, new_weight_out, new_out_columns, new_out_rows = adafactor_call(
-        summed, 1, weight_out.T, out_column_stats, out_row_stats, False, decay_rate
-    )
     grad_weight_out, new_weight_out = grad_weight_out.T, new_weight_out.T
-    new_in_rows, new_in_columns = new_in_rows[:, 0], new_in_columns[0]
-    new_out_rows, new_out_columns = new_out_rows[0], new_out_columns[:, 0]
     new_filter, new_filter_rows, new_filter_columns = adafactor_matrix(
         spectral_filter, grad_filter, filter_row_stats, filter_column_stats, decay_rate
     )

time: 658 us -> 645 us (0.980)
  blocking collectives: 142 us -> 116 us
  starting transfers between devices: 117 us -> 126 us
  waiting for transfers between devices: 87 us -> 93.6 us
    all_to_all x6 -> x5, blocking collectives: 142 us -> 116 us  [exchange_lat(): lax.all_to_all(blocks, 'lat', split_axis=0, concat_axis=0, tiled=True)]
    all_gather x1, waiting for transfers between devices: 0.01 us -> 8.18 us  [body(): summed = lax.all_gather(part, 'lat', axis=0, tiled=True)]
    all_to_all x8 -> x9, starting transfers between devices: 34.8 us -> 38.9 us  [exchange_lat(): lax.all_to_all(blocks, 'lat', split_axis=0, concat_axis=0, tiled=True)]
    all_to_all x8 -> x9, waiting for transfers between devices: 53.6 us -> 53.5 us  [exchange_lat(): lax.all_to_all(blocks, 'lat', split_axis=0, concat_axis=0, tiled=True)]
  transfers between devices with their start and end apart: 52 -> 53, of which waited for: 12 -> 13; matrix products, arithmetic and copies ran while one was open for 2% -> 2% of each run, Pallas kernels for 38% -> 41%
where the time goes in v4:
time: 645 us; the launch traced here: 635 us
  Pallas kernels  265 us (41%)
  starting transfers between devices  126 us (20%)
  blocking collectives  116 us (18%)
  waiting for transfers between devices  93.6 us (15%)
  between operations  16.6 us (3%)
  local copies, waits for them, and re-layouts  9.52 us (1%)
  other arithmetic  7.51 us (1%)
    all_to_all x5, blocking collectives, exchange_lat(): lax.all_to_all(blocks, 'lat', split_axis=0, concat_axis=0, tiled=True)  116 us
    ppermute x39, starting transfers between devices, exchange_lon(): lax.ppermute(slot, 'lon', [(i, (i + sign * s) % lon) for i in range(lon)])  84.6 us
    pallas_call x2, Pallas kernels, feed_forward(): pl.pallas_call(kernel, out_shape=outs, grid_spec=pltpu.PrefetchScalarGrid...  82.7 us
    all_to_all x9, waiting for transfers between devices, exchange_lat(): lax.all_to_all(blocks, 'lat', split_axis=0, concat_axis=0, tiled=True)  53.5 us
    all_to_all x9, starting transfers between devices, exchange_lat(): lax.all_to_all(blocks, 'lat', split_axis=0, concat_axis=0, tiled=True)  38.9 us
    pallas_call x2, Pallas kernels, filter_call(): pl.pallas_call(kernel, out_shape=outs, grid_spec=pltpu.PrefetchScalarGrid...  30 us
    pallas_call x1, Pallas kernels, weight_sums(): pl.pallas_call(kernel, out_shape=shape, grid=(count * steps,), in_specs=[...  29.2 us
    pallas_call x4, Pallas kernels, first_backward(): pl.pallas_call(kernel, out_shape=outs, grid_spec=pltpu.PrefetchScalarGrid...  28.4 us
  transfers between devices with their start and end apart: 53, of which 13 were waited for; matrix products, arithmetic and copies ran while one was open for 2% of the time, Pallas kernels for 41%

profile of v4, /device:TPU:0, one launch (start us, length us, event | category | flops | bytes accessed | tf_op | source)
XLA Modules:
  0.0 635.4 jit_solution(10914706537290289336)
XLA Ops:
  48.5 26.2 %conditional.15 = (bf16[1,128]{1,0:T(2,128)(2,1)S(1)}, bf16[768,768]{1,0:T(8,128)(2,1)}, bf16[2576,128]{1,0:T(8,128)(2,1)}, bf16[2576,128]{1,0:T(8,128)(2,1)}, b...) conditional(s32[]{:T(128)} %convert_element_type.11, () %tuple.151, (f32[2,641]{1,0:T(2,128)S(1)}, s32[1]{0:T(128)}, ...), branch_computations={%region_0.1_spmd, %region_1.2_spmd} | conditional | flops 2048 | bytes 803539520 | solution.py:773
  62.9 11.9 %all-to-all-done = bf16[8,96,768]{2,1,0:T(8,128)(2,1)} async-done(((bf16[8,96,768]{2,1,0:T(8,128)(2,1)}), bf16[8,96,768]{2,1,0:T(8,128)(2,1)}, u32[]{:S(2)}, u32[]{:S(2)}) %all-to-all-start) | async-done | bytes 1179680 | tf_op jit(solution)/shard_map/cond/branch_1_fun/spectra_0/all_to_all | solution.py:762
  78.7 26.2 %conditional.16 = (bf16[1,128]{1,0:T(2,128)(2,1)S(1)}, bf16[768,768]{1,0:T(8,128)(2,1)}, bf16[2576,128]{1,0:T(8,128)(2,1)}, bf16[2576,128]{1,0:T(8,128)(2,1)}, b...) conditional(s32[]{:T(128)} %convert_element_type.11, () %tuple.155, (s32[1]{0:T(128)}, ...), branch_computations={%region_2.3_spmd, %region_3.4_spmd} | conditional | flops 2048 | bytes 803539008 | solution.py:773
  93.0 11.9 %all-to-all-done.1 = bf16[8,96,768]{2,1,0:T(8,128)(2,1)} async-done(((bf16[8,96,768]{2,1,0:T(8,128)(2,1)}), bf16[8,96,768]{2,1,0:T(8,128)(2,1)}, u32[]{:S(2)}, u32[]{:S(2)}) %all-to-all-start.1) | async-done | bytes 1179680 | tf_op jit(solution)/shard_map/cond/branch_1_fun/spectra_1/all_to_all | solution.py:762
  110.3 25.5 %conditional.17 = (bf16[1,128]{1,0:T(2,128)(2,1)S(1)}, bf16[768,768]{1,0:T(8,128)(2,1)S(1)}) conditional(s32[]{:T(128)} %convert_element_type.11, () %tuple.159, (s32[1]{0:T(128)}, bf16[4,768,256]{2,1,0:T(8,128)(2,1)S(1)}, f32[1,768]{1,0:T(1,128)S(1)}, f32[1,768]{1,0:T(1,128)S(1)}, bf16[1296,128]{1,0:T(8,128)(2,1)}, ...), branch_computations={%region_4.5_spmd, %region_5.6_spmd} | conditional | flops 1024 | bytes 402359296 | solution.py:773
  115.3 20.5 %all_to_all.56 = bf16[8,96,768]{2,1,0:T(8,128)(2,1)S(1)} all-to-all(bf16[8,96,768]{2,1,0:T(8,128)(2,1)} %bitcast.38), channel_id=1, replica_groups=mesh['lat'=8,'lon'=4] {'lat'}, dimensions={0} | all-to-all | bytes 2359296 | tf_op jit(solution)/shard_map/cond/branch_1_fun/spectra_2/all_to_all | solution.py:762
  140.4 26.1 %conditional.18 = (bf16[1,128]{1,0:T(2,128)(2,1)S(1)}, bf16[768,768]{1,0:T(8,128)(2,1)}) conditional(s32[]{:T(128)} %convert_element_type.11, () %tuple.162, (s32[1]{0:T(128)}, bf16[4,768,256]{2,1,0:T(8,128)(2,1)S(1)}, f32[1,768]{1,0:T(1,128)S(1)}, f32[1,768]{1,0:T(1,128)S(1)}, bf16[1296,128]{1,0:T(8,128)(2,1)S(1)}, ...), branch_computations={%region_6.7_spmd, %region_7.8_spmd} | conditional | flops 1024 | bytes 402359296 | solution.py:773
  145.4 21.0 %all_to_all.57 = bf16[8,96,768]{2,1,0:T(8,128)(2,1)} all-to-all(bf16[8,96,768]{2,1,0:T(8,128)(2,1)} %bitcast.39), channel_id=1, replica_groups=mesh['lat'=8,'lon'=4] {'lat'}, dimensions={0} | all-to-all | bytes 2359296 | tf_op jit(solution)/shard_map/cond/branch_1_fun/spectra_3/all_to_all | solution.py:762
  169.0 47.0 %conditional.19 = (bf16[1,128]{1,0:T(2,128)(2,1)S(1)}, bf16[1536,768]{1,0:T(8,128)(2,1)}, bf16[1536,768]{1,0:T(8,128)(2,1)}, f32[6,512,768]{2,1,0:T(8,128)}, bf1...) conditional(s32[]{:T(128)} %convert_element_type.11, () %tuple.149, ...), branch_computations={%region_8.9_spmd, %region_9.10_spmd} | conditional | flops 1024 | bytes 407077984 | solution.py:773
  169.0 13.2 %filter_forward.1 = (bf16[1536,768]{1,0:T(8,128)(2,1)}, bf16[1536,768]{1,0:T(8,128)(2,1)}, f32[6,512,768]{2,1,0:T(8,128)}) custom-call(s32[1]{0:T(128)} %get-tuple-element.449.first_ref, bf16[96,128,128]{2,1,0:T(8,128)(2,1)} %constant.133.clone.1.to_ref, bf16[96,128,128]{2,1,0:T(8,128)(2,1)} %constant.134.clone.1.back_ref, ...), custom_call_target="tpu_custom_call" | custom-call | flops 1024 | bytes 400000000 | tf_op jit(solution)/shard_map/cond/branch_1_fun/filter_forward/pallas_call | solution.py:261
  193.7 22.4 %all-to-all-done.4 = bf16[8,192,768]{2,1,0:T(8,128)(2,1)} async-done(((bf16[8,192,768]{2,1,0:T(8,128)(2,1)}), bf16[8,192,768]{2,1,0:T(8,128)(2,1)}, u32[]{:S(2)}, u32[]{:S(2)}) %all-to-all-start.4) | async-done | bytes 2359328 | tf_op jit(solution)/shard_map/cond/branch_1_fun/synthesis_0/all_to_all | solution.py:762
  217.8 46.2 %conditional.20 = (bf16[1,128]{1,0:T(2,128)(2,1)S(1)}, bf16[2576,128]{1,0:T(8,128)(2,1)}, bf16[2576,128]{1,0:T(8,128)(2,1)}, bf16[2576,128]{1,0:T(8,128)(2,1)}, ...) conditional(s32[]{:T(128)} %convert_element_type.11, () %tuple.168, ...), branch_computations={%region_10.11_spmd, %region_11.12_spmd} | conditional | flops 1024 | bytes 408405152 | solution.py:773
  222.6 41.4 %feed_forward.2 = (bf16[2576,128]{1,0:T(8,128)(2,1)}, bf16[2576,128]{1,0:T(8,128)(2,1)}, bf16[2576,128]{1,0:T(8,128)(2,1)}, bf16[2576,128]{1,0:T(8,128)(2,1)}, f...) custom-call(s32[1]{0:T(128)} %get-tuple-element.469.me_ref, ...), custom_call_target="tpu_custom_call" | custom-call | flops 1024 | bytes 400000000 | tf_op jit(solution)/shard_map/cond/branch_1_fun/feed_forward/pallas_call | solution.py:506
  273.7 46.3 %conditional.21 = (bf16[1,128]{1,0:T(2,128)(2,1)S(1)}, bf16[1296,128]{1,0:T(8,128)(2,1)}, bf16[1296,128]{1,0:T(8,128)(2,1)}, bf16[1296,128]{1,0:T(8,128)(2,1)}, ...) conditional(s32[]{:T(128)} %convert_element_type.11, () %tuple.167, ...), branch_computations={%region_12.13_spmd, %region_13.14_spmd} | conditional | flops 1024 | bytes 408405184 | solution.py:773
  278.6 41.3 %feed_forward.3 = (bf16[1296,128]{1,0:T(8,128)(2,1)}, bf16[1296,128]{1,0:T(8,128)(2,1)}, bf16[1296,128]{1,0:T(8,128)(2,1)}, bf16[1296,128]{1,0:T(8,128)(2,1)}, b...) custom-call(s32[1]{0:T(128)} %get-tuple-element.504.me_ref, ...), custom_call_target="tpu_custom_call" | custom-call | flops 1024 | bytes 400000000 | tf_op jit(solution)/shard_map/cond/branch_1_fun/feed_forward/pallas_call | solution.py:506
  320.0 34.1 %conditional.22 = (bf16[1,128]{1,0:T(2,128)(2,1)S(1)}, bf16[1536,768]{1,0:T(8,128)(2,1)}, f32[1536,1408]{1,0:T(8,128)}) conditional(s32[]{:T(128)} %convert_element_type.11, () %tuple.171, (bf16[1536,768]{1,0:T(8,128)(2,1)}, bf16[2048,768]{1,0:T(8,128)(2,1)}, bf16[2048,1408]{1,0:T(8,128)(2,1)}, bf16[2048,1408]{1,0:T(8,128)(2,1)}, ...), branch_computations={%region_14.15_spmd, %region_15.16_spmd} | conditional | flops 1024 | bytes 407077952 | solution.py:773
  324.6 29.2 %weight_sums.1 = f32[1536,1408]{1,0:T(8,128)} custom-call(bf16[2048,768]{1,0:T(8,128)(2,1)} %get-tuple-element.544.refs_0_, bf16[2048,1408]{1,0:T(8,128)(2,1)} %get-tuple-element.545.refs_1_, bf16[2048,1408]{1,0:T(8,128)(2,1)} %get-tuple-element.546.refs_2_, bf16[2048,768]{1,0:T(8,128)(2,1)} %get-tuple-element.547.refs_3_, ...), custom_call_target="tpu_custom_call" | custom-call | flops 1024 | bytes 400000000 | tf_op jit(solution)/shard_map/cond/branch_1_fun/weight_sums/pallas_call | solution.py:562
  368.0 19.4 %conditional.23 = (bf16[1,128]{1,0:T(2,128)(2,1)S(1)}, bf16[768,768]{1,0:T(8,128)(2,1)S(1)}, bf16[768,768]{1,0:T(8,128)(2,1)}, bf16[768,768]{1,0:T(8,128)(2,1)},...) conditional(s32[]{:T(128)} %convert_element_type.11, () %tuple.147, (s32[1]{0:T(128)}, ...), branch_computations={%region_16.17_spmd, %region_17.20_spmd.clone} | conditional | flops 602368 | bytes 401058368 | solution.py:773
  368.0 16.8 %filter_backward.1 = (bf16[768,768]{1,0:T(8,128)(2,1)S(1)}, bf16[768,768]{1,0:T(8,128)(2,1)}, bf16[768,768]{1,0:T(8,128)(2,1)}, bf16[768,768]{1,0:T(8,128)(2,1)}, f32[128,768]{1,0:T(8,128)}) custom-call(s32[1]{0:T(128)} %get-tuple-element.1152.first_ref, bf16[96,128,128]{2,1,0:T(8,128)(2,1)} %constant.132.clone.2.to_ref, ...), custom_call_target="tpu_custom_call" | custom-call | flops 1024 | bytes 400000000 | tf_op jit(solution)/shard_map/cond/branch_1_fun/filter_backward/pallas_call | solution.py:261
  387.4 39.9 %conditional.24 = (bf16[1,128]{1,0:T(2,128)(2,1)S(1)}, bf16[1296,128]{1,0:T(8,128)(2,1)}, bf16[1296,128]{1,0:T(8,128)(2,1)}, bf16[1296,128]{1,0:T(8,128)(2,1)}, bf16[1296,128]{1,0:T(8,128)(2,1)}) conditional(s32[]{:T(128)} %convert_element_type.11, () %tuple.176, (bf16[768,768]{1,0:T(8,128)(2,1)S(1)}, s32[1]{0:T(128)}, ...), branch_computations={%region_20.21_spmd, %region_21.22_spmd} | conditional | flops 1024 | bytes 403686464 | solution.py:773
  387.4 32.7 %all_to_all.58 = bf16[8,96,768]{2,1,0:T(8,128)(2,1)} all-to-all(bf16[8,96,768]{2,1,0:T(8,128)(2,1)S(1)} %bitcast.40), channel_id=1, replica_groups=mesh['lat'=8,'lon'=4] {'lat'}, dimensions={0} | all-to-all | bytes 2359296 | tf_op jit(solution)/shard_map/cond/branch_1_fun/back_spectra_0/all_to_all | solution.py:762
  434.9 28.3 %conditional.25 = (bf16[1,128]{1,0:T(2,128)(2,1)S(1)}, bf16[1296,128]{1,0:T(8,128)(2,1)}, bf16[1296,128]{1,0:T(8,128)(2,1)}, bf16[1296,128]{1,0:T(8,128)(2,1)}, bf16[1296,128]{1,0:T(8,128)(2,1)}) conditional(s32[]{:T(128)} %convert_element_type.11, () %tuple.179, (bf16[768,768]{1,0:T(8,128)(2,1)}, s32[1]{0:T(128)}, ...), branch_computations={%region_22.23_spmd, %region_23.24_spmd} | conditional | flops 1024 | bytes 402359328 | solution.py:773
  434.9 21.2 %all_to_all.59 = bf16[8,96,768]{2,1,0:T(8,128)(2,1)} all-to-all(bf16[8,96,768]{2,1,0:T(8,128)(2,1)} %bitcast.19), channel_id=1, replica_groups=mesh['lat'=8,'lon'=4] {'lat'}, dimensions={0} | all-to-all | bytes 2359296 | tf_op jit(solution)/shard_map/cond/branch_1_fun/back_spectra_1/all_to_all | solution.py:762
  467.8 28.1 %conditional.26 = (bf16[1,128]{1,0:T(2,128)(2,1)S(1)}, bf16[1296,128]{1,0:T(8,128)(2,1)}, bf16[1296,128]{1,0:T(8,128)(2,1)}, bf16[1296,128]{1,0:T(8,128)(2,1)}, bf16[1296,128]{1,0:T(8,128)(2,1)}) conditional(s32[]{:T(128)} %convert_element_type.11, () %tuple.181, (bf16[768,768]{1,0:T(8,128)(2,1)}, s32[1]{0:T(128)}, ...), branch_computations={%region_25.26_spmd, %region_26.27_spmd} | conditional | flops 1024 | bytes 403686464 | solution.py:773
  467.9 21.2 %all_to_all.60 = bf16[8,96,768]{2,1,0:T(8,128)(2,1)} all-to-all(bf16[8,96,768]{2,1,0:T(8,128)(2,1)} %bitcast.21), channel_id=1, replica_groups=mesh['lat'=8,'lon'=4] {'lat'}, dimensions={0} | all-to-all | bytes 2359296 | tf_op jit(solution)/shard_map/cond/branch_1_fun/back_spectra_2/all_to_all | solution.py:762
  503.9 28.9 %conditional.27 = (bf16[1,128]{1,0:T(2,128)(2,1)S(1)}, bf16[1296,128]{1,0:T(8,128)(2,1)}, bf16[1296,128]{1,0:T(8,128)(2,1)}, bf16[1296,128]{1,0:T(8,128)(2,1)}, ...) conditional(s32[]{:T(128)} %convert_element_type.11, () %tuple.146, (bf16[768,768]{1,0:T(8,128)(2,1)}, ...), branch_computations={%region_27.28_spmd, %region_28.29_spmd} | conditional | flops 4096 | bytes 1609584768 | solution.py:773
  539.9 14.5 %collective-permute-start.34 = (bf16[1296,128]{1,0:T(8,128)(2,1)}, bf16[1296,128]{1,0:T(8,128)(2,1)}, u32[]{:S(2)}, u32[]{:S(2)}) collective-permute-start(bf16[1296,128]{1,0:T(8,128)(2,1)} %get-tuple-element.1094), channel_id=1, source_target_pairs={{0,2},{1,3},{2,0},{3,1},{4,6},{5,7},{6,4},{7,5},{8,10},{9,11},{10,... | collective-permute-start | bytes 995336 | tf_op jit(solution)/shard_map/input_grad_3/ppermute | solution.py:754
  556.4 17.1 %conditional.28 = (bf16[1,128]{1,0:T(2,128)(2,1)S(1)}, f32[24,768]{1,0:T(8,128)S(1)}, f32[4,16,64,641]{3,2,1,0:T(8,128)}) conditional(s32[]{:T(128)} %convert_element_type.11, () %tuple.188, (f32[192,768]{1,0:T(8,128)}, s32[1]{0:T(128)}, bf16[1296,128]{1,0:T(8,128)(2,1)}, bf16[1296,128]{1,0:T(8,128)(2,1)}, bf16[1296,128]{1,0:T(8,128)(2,1)}, ...), branch_computations={%region_30.31_spmd, %region_31.33_spmd} | conditional | flops 132096 | bytes 1202433024 | solution.py:773
  585.6 8.2 %all-gather.2.cloned.1.call-done = bf16[1536,1408]{1,0:T(8,128)(2,1)} async-done(((bf16[192,1408]{1,0:T(8,128)(2,1)}), bf16[1536,1408]{1,0:T(8,128)(2,1)}) %all-gather.2.cloned.1.call-update) | async-done | bytes 4325392 | tf_op jit(solution)/shard_map/weights_lat/all_gather | solution.py:1007
  593.9 23.3 %conditional.29 = (f32[192,768]{1,0:T(8,128)}, f32[641,1282]{1,0:T(8,128)}, f32[641,1282]{1,0:T(8,128)}, f32[641]{0:T(1024)}, f32[1282]{0:T(1024)}, /*index=5*/f...) conditional(s32[]{:T(128)} %convert_element_type.11, () %tuple.187, ...), branch_computations={%region_33.34_spmd, %region_34.35_spmd} | conditional | flops 20480 | bytes 815833280 | solution.py:773
  600.5 7.6 %adafactor.2 = (f32[641,1282]{1,0:T(8,128)}, f32[641,1282]{1,0:T(8,128)}, f32[641]{0:T(1024)}, f32[1282]{0:T(1024)}) custom-call(bf16[1536,1408]{1,0:T(8,128)(2,1)} %get-tuple-element.657.grad_ref, f32[641,1282]{1,0:T(8,128)} %get-tuple-element.658.weight_ref, f32[641,1]{1,0:T(8,128)} %broadcast_in_dim.11.rows_ref, f32[1,1282]{1,0:T(1,128)} %broadcast_in_dim.2.columns_ref), custom_call_target="tpu_custom_call" | custom-call | flops 1024 | bytes 400000000 | tf_op jit(solution)/shard_map/cond/branch_1_fun/adafactor/pallas_call | solution.py:671
  609.6 7.6 %adafactor.3 = (f32[641,1282]{1,0:T(8,128)}, f32[641,1282]{1,0:T(8,128)}, f32[641]{0:T(1024)}, f32[1282]{0:T(1024)}) custom-call(bf16[1536,1408]{1,0:T(8,128)(2,1)} %get-tuple-element.657.grad_ref, f32[641,1282]{1,0:T(8,128)S(1)} %bitcast.34, f32[641,1]{1,0:T(8,128)} %broadcast_in_dim.12.rows_ref, f32[1,1282]{1,0:T(1,128)} %broadcast_in_dim.10.columns_ref), custom_call_target="tpu_custom_call" | custom-call | flops 1024 | bytes 400000000 | tf_op jit(solution)/shard_map/cond/branch_1_fun/adafactor/pallas_call | solution.py:671
  (255 shorter events, 276.0 us)
Async XLA Ops:
  7.2 457.8 %reduce-scatter.2.cloned.1.call-start = ((), (), s32[]{:S(2)}) async-start(), calls=%async_computation.15 | async-start | bytes 9732096 | tf_op jit(solution)/shard_map/weights_lat/reduce_scatter | solution.py:951
  38.6 36.2 %collective-permute-start.3 = (bf16[1296,128]{1,0:T(8,128)(2,1)}, bf16[1296,128]{1,0:T(8,128)(2,1)}, u32[]{:S(2)}, u32[]{:S(2)}) collective-permute-start(bf16[1296,128]{1,0:T(8,128)(2,1)} %get-tuple-element.937), channel_id=1, source_target_pairs={{0,1},{1,2},{2,3},{3,0},{4,5},{5,6},{6,7},{7,4},{8,9},{9,10},{10,1... | collective-permute-start | bytes 995336 | tf_op jit(solution)/shard_map/fields_1/ppermute | solution.py:754
  135.8 80.3 %collective-permute-start.12 = (bf16[2576,128]{1,0:T(8,128)(2,1)}, bf16[2576,128]{1,0:T(8,128)(2,1)}, u32[]{:S(2)}, u32[]{:S(2)}) collective-permute-start(bf16[2576,128]{1,0:T(8,128)(2,1)} %get-tuple-element.1014), channel_id=1, source_target_pairs={{0,1},{1,2},{2,3},{3,0},{4,5},{5,6},{6,7},{7,4},{8,9},{9,10},{10,1... | collective-permute-start | bytes 1978376 | tf_op jit(solution)/shard_map/upstream_0/ppermute | solution.py:754
  138.0 79.8 %collective-permute-start.13 = (bf16[2576,128]{1,0:T(8,128)(2,1)}, bf16[2576,128]{1,0:T(8,128)(2,1)}, u32[]{:S(2)}, u32[]{:S(2)}) collective-permute-start(bf16[2576,128]{1,0:T(8,128)(2,1)} %get-tuple-element.1015), channel_id=1, source_target_pairs={{0,2},{1,3},{2,0},{3,1},{4,6},{5,7},{6,4},{7,5},{8,10},{9,11},{10,... | collective-permute-start | bytes 1978376 | tf_op jit(solution)/shard_map/upstream_0/ppermute | solution.py:754
  140.3 77.5 %collective-permute-start.14 = (bf16[2576,128]{1,0:T(8,128)(2,1)}, bf16[2576,128]{1,0:T(8,128)(2,1)}, u32[]{:S(2)}, u32[]{:S(2)}) collective-permute-start(bf16[2576,128]{1,0:T(8,128)(2,1)} %get-tuple-element.1016), channel_id=1, source_target_pairs={{0,3},{1,0},{2,1},{3,2},{4,7},{5,4},{6,5},{7,6},{8,11},{9,8},{10,9... | collective-permute-start | bytes 1978376 | tf_op jit(solution)/shard_map/upstream_0/ppermute | solution.py:754
  166.5 107.2 %collective-permute-start.15 = (bf16[2576,128]{1,0:T(8,128)(2,1)}, bf16[2576,128]{1,0:T(8,128)(2,1)}, u32[]{:S(2)}, u32[]{:S(2)}) collective-permute-start(bf16[2576,128]{1,0:T(8,128)(2,1)} %get-tuple-element.1021), channel_id=1, source_target_pairs={{0,1},{1,2},{2,3},{3,0},{4,5},{5,6},{6,7},{7,4},{8,9},{9,10},{10,1... | collective-permute-start | bytes 1978376 | tf_op jit(solution)/shard_map/upstream_1/ppermute | solution.py:754
  168.4 105.2 %collective-permute-start.16 = (bf16[2576,128]{1,0:T(8,128)(2,1)}, bf16[2576,128]{1,0:T(8,128)(2,1)}, u32[]{:S(2)}, u32[]{:S(2)}) collective-permute-start(bf16[2576,128]{1,0:T(8,128)(2,1)} %get-tuple-element.1022), channel_id=1, source_target_pairs={{0,2},{1,3},{2,0},{3,1},{4,6},{5,7},{6,4},{7,5},{8,10},{9,11},{10,... | collective-permute-start | bytes 1978376 | tf_op jit(solution)/shard_map/upstream_1/ppermute | solution.py:754
  182.2 33.9 %all-to-all-start.4 = ((bf16[8,192,768]{2,1,0:T(8,128)(2,1)}), bf16[8,192,768]{2,1,0:T(8,128)(2,1)}, u32[]{:S(2)}, u32[]{:S(2)}) async-start(bf16[8,192,768]{2,1,0:T(8,128)(2,1)} %bitcast.45), calls=%async_computation.4 | async-start | bytes 4718592 | tf_op jit(solution)/shard_map/cond/branch_1_fun/synthesis_0/all_to_all | solution.py:762
  216.1 57.6 %collective-permute-start.17 = (bf16[2576,128]{1,0:T(8,128)(2,1)}, bf16[2576,128]{1,0:T(8,128)(2,1)}, u32[]{:S(2)}, u32[]{:S(2)}) collective-permute-start(bf16[2576,128]{1,0:T(8,128)(2,1)} %get-tuple-element.1023), channel_id=1, source_target_pairs={{0,3},{1,0},{2,1},{3,2},{4,7},{5,4},{6,5},{7,6},{8,11},{9,8},{10,9... | collective-permute-start | bytes 1978376 | tf_op jit(solution)/shard_map/upstream_1/ppermute | solution.py:754
  217.9 46.2 %all-to-all-start.5 = ((bf16[8,192,768]{2,1,0:T(8,128)(2,1)}), bf16[8,192,768]{2,1,0:T(8,128)(2,1)}, u32[]{:S(2)}, u32[]{:S(2)}) async-start(bf16[8,192,768]{2,1,0:T(8,128)(2,1)} %bitcast.11), calls=%async_computation.5 | async-start | bytes 4718592 | tf_op jit(solution)/shard_map/cond/branch_1_fun/synthesis_1/all_to_all | solution.py:762
  264.0 90.0 %collective-permute-start.18 = (bf16[2576,128]{1,0:T(8,128)(2,1)}, bf16[2576,128]{1,0:T(8,128)(2,1)}, u32[]{:S(2)}, u32[]{:S(2)}) collective-permute-start(bf16[2576,128]{1,0:T(8,128)(2,1)} %get-tuple-element.1041), channel_id=1, source_target_pairs={{0,3},{1,0},{2,1},{3,2},{4,7},{5,4},{6,5},{7,6},{8,11},{9,8},{10,9... | collective-permute-start | bytes 1978376 | tf_op jit(solution)/shard_map/output_0_0/ppermute | solution.py:754
  266.1 87.9 %collective-permute-start.19 = (bf16[2576,128]{1,0:T(8,128)(2,1)}, bf16[2576,128]{1,0:T(8,128)(2,1)}, u32[]{:S(2)}, u32[]{:S(2)}) collective-permute-start(bf16[2576,128]{1,0:T(8,128)(2,1)} %get-tuple-element.1042), channel_id=1, source_target_pairs={{0,2},{1,3},{2,0},{3,1},{4,6},{5,7},{6,4},{7,5},{8,10},{9,11},{10,... | collective-permute-start | bytes 1978376 | tf_op jit(solution)/shard_map/output_0_0/ppermute | solution.py:754
  273.7 80.4 %collective-permute-start.20 = (bf16[2576,128]{1,0:T(8,128)(2,1)}, bf16[2576,128]{1,0:T(8,128)(2,1)}, u32[]{:S(2)}, u32[]{:S(2)}) collective-permute-start(bf16[2576,128]{1,0:T(8,128)(2,1)} %get-tuple-element.1043), channel_id=1, source_target_pairs={{0,1},{1,2},{2,3},{3,0},{4,5},{5,6},{6,7},{7,4},{8,9},{9,10},{10,1... | collective-permute-start | bytes 1978376 | tf_op jit(solution)/shard_map/output_0_0/ppermute | solution.py:754
  273.7 46.3 %all-to-all-start.6 = ((bf16[8,192,768]{2,1,0:T(8,128)(2,1)}), bf16[8,192,768]{2,1,0:T(8,128)(2,1)}, u32[]{:S(2)}, u32[]{:S(2)}) async-start(bf16[8,192,768]{2,1,0:T(8,128)(2,1)} %bitcast.13), calls=%async_computation.6 | async-start | bytes 4718592 | tf_op jit(solution)/shard_map/cond/branch_1_fun/back_synthesis_0/all_to_all | solution.py:762
  320.0 34.1 %all-to-all-start.7 = ((bf16[8,192,768]{2,1,0:T(8,128)(2,1)}), bf16[8,192,768]{2,1,0:T(8,128)(2,1)}, u32[]{:S(2)}, u32[]{:S(2)}) async-start(bf16[8,192,768]{2,1,0:T(8,128)(2,1)} %bitcast.15), calls=%async_computation.7 | async-start | bytes 4718592 | tf_op jit(solution)/shard_map/cond/branch_1_fun/back_synthesis_1/all_to_all | solution.py:762
  354.1 185.7 %all-reduce.7.cloned.1.call-start = ((), (), s32[]{:S(2)}) async-start(), calls=%async_computation.16 | async-start | bytes 1081344 | tf_op jit(solution)/shard_map/weights_lon/psum | solution.py:959
  358.6 74.2 %collective-permute-start.24 = (bf16[1296,128]{1,0:T(8,128)(2,1)}, bf16[1296,128]{1,0:T(8,128)(2,1)}, u32[]{:S(2)}, u32[]{:S(2)}) collective-permute-start(bf16[1296,128]{1,0:T(8,128)(2,1)} %get-tuple-element.1063), channel_id=1, source_target_pairs={{0,3},{1,0},{2,1},{3,2},{4,7},{5,4},{6,5},{7,6},{8,11},{9,8},{10,9... | collective-permute-start | bytes 995336 | tf_op jit(solution)/shard_map/output_1_1/ppermute | solution.py:754
  361.8 73.0 %collective-permute-start.25 = (bf16[1296,128]{1,0:T(8,128)(2,1)}, bf16[1296,128]{1,0:T(8,128)(2,1)}, u32[]{:S(2)}, u32[]{:S(2)}) collective-permute-start(bf16[1296,128]{1,0:T(8,128)(2,1)} %get-tuple-element.1064), channel_id=1, source_target_pairs={{0,2},{1,3},{2,0},{3,1},{4,6},{5,7},{6,4},{7,5},{8,10},{9,11},{10,... | collective-permute-start | bytes 995336 | tf_op jit(solution)/shard_map/output_1_1/ppermute | solution.py:754
  367.2 67.6 %collective-permute-start.26 = (bf16[1296,128]{1,0:T(8,128)(2,1)}, bf16[1296,128]{1,0:T(8,128)(2,1)}, u32[]{:S(2)}, u32[]{:S(2)}) collective-permute-start(bf16[1296,128]{1,0:T(8,128)(2,1)} %get-tuple-element.1065), channel_id=1, source_target_pairs={{0,1},{1,2},{2,3},{3,0},{4,5},{5,6},{6,7},{7,4},{8,9},{9,10},{10,1... | collective-permute-start | bytes 995336 | tf_op jit(solution)/shard_map/output_1_1/ppermute | solution.py:754
  427.3 40.0 %collective-permute-start.30 = (bf16[1296,128]{1,0:T(8,128)(2,1)}, bf16[1296,128]{1,0:T(8,128)(2,1)}, u32[]{:S(2)}, u32[]{:S(2)}) collective-permute-start(bf16[1296,128]{1,0:T(8,128)(2,1)} %get-tuple-element.1082), channel_id=1, source_target_pairs={{0,3},{1,0},{2,1},{3,2},{4,7},{5,4},{6,5},{7,6},{8,11},{9,8},{10,9... | collective-permute-start | bytes 995336 | tf_op jit(solution)/shard_map/input_grad_0/ppermute | solution.py:754
  430.6 37.2 %collective-permute-start.31 = (bf16[1296,128]{1,0:T(8,128)(2,1)}, bf16[1296,128]{1,0:T(8,128)(2,1)}, u32[]{:S(2)}, u32[]{:S(2)}) collective-permute-start(bf16[1296,128]{1,0:T(8,128)(2,1)} %get-tuple-element.1083), channel_id=1, source_target_pairs={{0,2},{1,3},{2,0},{3,1},{4,6},{5,7},{6,4},{7,5},{8,10},{9,11},{10,... | collective-permute-start | bytes 995336 | tf_op jit(solution)/shard_map/input_grad_0/ppermute | solution.py:754
  432.8 35.0 %collective-permute-start.32 = (bf16[1296,128]{1,0:T(8,128)(2,1)}, bf16[1296,128]{1,0:T(8,128)(2,1)}, u32[]{:S(2)}, u32[]{:S(2)}) collective-permute-start(bf16[1296,128]{1,0:T(8,128)(2,1)} %get-tuple-element.1084), channel_id=1, source_target_pairs={{0,1},{1,2},{2,3},{3,0},{4,5},{5,6},{6,7},{7,4},{8,9},{9,10},{10,1... | collective-permute-start | bytes 995336 | tf_op jit(solution)/shard_map/input_grad_0/ppermute | solution.py:754
  463.2 37.1 %collective-permute-start.27 = (bf16[1296,128]{1,0:T(8,128)(2,1)}, bf16[1296,128]{1,0:T(8,128)(2,1)}, u32[]{:S(2)}, u32[]{:S(2)}) collective-permute-start(bf16[1296,128]{1,0:T(8,128)(2,1)} %get-tuple-element.1077), channel_id=1, source_target_pairs={{0,3},{1,0},{2,1},{3,2},{4,7},{5,4},{6,5},{7,6},{8,11},{9,8},{10,9... | collective-permute-start | bytes 995336 | tf_op jit(solution)/shard_map/input_grad_1/ppermute | solution.py:754
  467.1 126.7 %all-gather.2.cloned.1.call-start = ((), (), s32[]{:S(2)}) async-start(), calls=%async_computation.17 | async-start | bytes 4866048 | tf_op jit(solution)/shard_map/weights_lat/all_gather | solution.py:1007
  467.2 36.8 %collective-permute-start.28 = (bf16[1296,128]{1,0:T(8,128)(2,1)}, bf16[1296,128]{1,0:T(8,128)(2,1)}, u32[]{:S(2)}, u32[]{:S(2)}) collective-permute-start(bf16[1296,128]{1,0:T(8,128)(2,1)} %get-tuple-element.1078), channel_id=1, source_target_pairs={{0,2},{1,3},{2,0},{3,1},{4,6},{5,7},{6,4},{7,5},{8,10},{9,11},{10,... | collective-permute-start | bytes 995336 | tf_op jit(solution)/shard_map/input_grad_1/ppermute | solution.py:754
  467.3 36.7 %collective-permute-start.29 = (bf16[1296,128]{1,0:T(8,128)(2,1)}, bf16[1296,128]{1,0:T(8,128)(2,1)}, u32[]{:S(2)}, u32[]{:S(2)}) collective-permute-start(bf16[1296,128]{1,0:T(8,128)(2,1)} %get-tuple-element.1079), channel_id=1, source_target_pairs={{0,1},{1,2},{2,3},{3,0},{4,5},{5,6},{6,7},{7,4},{8,9},{9,10},{10,1... | collective-permute-start | bytes 995336 | tf_op jit(solution)/shard_map/input_grad_1/ppermute | solution.py:754
  495.9 36.9 %collective-permute-start.36 = (bf16[1296,128]{1,0:T(8,128)(2,1)}, bf16[1296,128]{1,0:T(8,128)(2,1)}, u32[]{:S(2)}, u32[]{:S(2)}) collective-permute-start(bf16[1296,128]{1,0:T(8,128)(2,1)} %get-tuple-element.1107), channel_id=1, source_target_pairs={{0,3},{1,0},{2,1},{3,2},{4,7},{5,4},{6,5},{7,6},{8,11},{9,8},{10,9... | collective-permute-start | bytes 995336 | tf_op jit(solution)/shard_map/input_grad_2/ppermute | solution.py:754
  499.2 40.5 %collective-permute-start.37 = (bf16[1296,128]{1,0:T(8,128)(2,1)}, bf16[1296,128]{1,0:T(8,128)(2,1)}, u32[]{:S(2)}, u32[]{:S(2)}) collective-permute-start(bf16[1296,128]{1,0:T(8,128)(2,1)} %get-tuple-element.1108), channel_id=1, source_target_pairs={{0,2},{1,3},{2,0},{3,1},{4,6},{5,7},{6,4},{7,5},{8,10},{9,11},{10,... | collective-permute-start | bytes 995336 | tf_op jit(solution)/shard_map/input_grad_2/ppermute | solution.py:754
  500.3 39.5 %collective-permute-start.38 = (bf16[1296,128]{1,0:T(8,128)(2,1)}, bf16[1296,128]{1,0:T(8,128)(2,1)}, u32[]{:S(2)}, u32[]{:S(2)}) collective-permute-start(bf16[1296,128]{1,0:T(8,128)(2,1)} %get-tuple-element.1109), channel_id=1, source_target_pairs={{0,1},{1,2},{2,3},{3,0},{4,5},{5,6},{6,7},{7,4},{8,9},{9,10},{10,1... | collective-permute-start | bytes 995336 | tf_op jit(solution)/shard_map/input_grad_2/ppermute | solution.py:754
  539.8 77.4 %collective-permute-start.33 = (bf16[1296,128]{1,0:T(8,128)(2,1)}, bf16[1296,128]{1,0:T(8,128)(2,1)}, u32[]{:S(2)}, u32[]{:S(2)}) collective-permute-start(bf16[1296,128]{1,0:T(8,128)(2,1)} %get-tuple-element.1093), channel_id=1, source_target_pairs={{0,3},{1,0},{2,1},{3,2},{4,7},{5,4},{6,5},{7,6},{8,11},{9,8},{10,9... | collective-permute-start | bytes 995336 | tf_op jit(solution)/shard_map/input_grad_3/ppermute | solution.py:754
  539.9 77.3 %collective-permute-start.34 = (bf16[1296,128]{1,0:T(8,128)(2,1)}, bf16[1296,128]{1,0:T(8,128)(2,1)}, u32[]{:S(2)}, u32[]{:S(2)}) collective-permute-start(bf16[1296,128]{1,0:T(8,128)(2,1)} %get-tuple-element.1094), channel_id=1, source_target_pairs={{0,2},{1,3},{2,0},{3,1},{4,6},{5,7},{6,4},{7,5},{8,10},{9,11},{10,... | collective-permute-start | bytes 995336 | tf_op jit(solution)/shard_map/input_grad_3/ppermute | solution.py:754
  554.4 62.8 %collective-permute-start.35 = (bf16[1296,128]{1,0:T(8,128)(2,1)}, bf16[1296,128]{1,0:T(8,128)(2,1)}, u32[]{:S(2)}, u32[]{:S(2)}) collective-permute-start(bf16[1296,128]{1,0:T(8,128)(2,1)} %get-tuple-element.1095), channel_id=1, source_target_pairs={{0,1},{1,2},{2,3},{3,0},{4,5},{5,6},{6,7},{7,4},{8,9},{9,10},{10,1... | collective-permute-start | bytes 995336 | tf_op jit(solution)/shard_map/input_grad_3/ppermute | solution.py:754
  (67 other events, 1449.0 us)
Sparse Core Ops, SparseCore 0:
  354.2 86.7 reduce-scatter.1
  467.2 68.0 all-reduce.6
  539.9 53.8 all-gather.1

commit v5 on v4

--- a/solution.py
+++ b/solution.py
@@ -524,7 +524,7 @@
     )(me, *arrays)
 
 
-def weight_sums(parts, block=512):
+def weight_sums(parts, kept, block=512):
     count = len(parts)
     height, width = parts[0][0].shape
     hidden_width = parts[0][1].shape[1]
@@ -540,9 +540,10 @@
             out[...] = jnp.zeros_like(out)
 
         def add(row, left, right):
-            out[row : row + width, :] += lax.dot_general(
+            result = lax.dot_general(
                 left[...], right[...], (((0,), (0,)), ((), ())), preferred_element_type=F32
             )
+            out[row : row + kept, :] += result[:kept]
 
         for m in range(count):
 
@@ -550,7 +551,7 @@
             def _():
                 second, active, pre, cot = ins[4 * m : 4 * m + 4]
                 add(0, second, pre)
-                add(width, cot, active)
+                add(kept, cot, active)
 
     def spec(array, m):
         return pl.BlockSpec(
@@ -558,7 +559,7 @@
             lambda k: (jnp.clip(k - m * steps, 0, steps - 1), 0),
         )
 
-    shape = jax.ShapeDtypeStruct((2 * width, hidden_width), F32)
+    shape = jax.ShapeDtypeStruct((2 * kept, hidden_width), F32)
     return pl.pallas_call(
         kernel,
         out_shape=shape,
@@ -742,6 +743,7 @@
     pair = 2 if chunks % 2 == 0 else 1
     mids = chunks // pair
     n = depth * points
+    kept = -(-channels // (4 * lat)) * (4 * lat)
 
     def wider(array, *sizes):
         return jnp.pad(array, [(0, s - d) for s, d in zip(sizes, array.shape)])
@@ -921,7 +923,7 @@
         backs.append(back)
 
     def to_weights(late, parts):
-        return exchange_lat(f"back_synthesis_{mids - 1}", late), weight_sums(parts)
+        return exchange_lat(f"back_synthesis_{mids - 1}", late), weight_sums(parts, kept)
 
     def to_gradients(backs, coefs, gain_parts):
         *values, filter_part = filter_backward(

time: 645 us -> 640 us (level)
  transfers between devices with their start and end apart: 53 -> 53, of which waited for: 13 -> 14; matrix products, arithmetic and copies ran while one was open for 2% -> 2% of each run, Pallas kernels for 41% -> 41%
where the time goes in v5:
time: 640 us; the launch traced here: 631 us
  Pallas kernels  264 us (41%)
  starting transfers between devices  128 us (20%)
  blocking collectives  113 us (18%)
  waiting for transfers between devices  91 us (14%)
  between operations  16.6 us (3%)
  local copies, waits for them, and re-layouts  9.5 us (1%)
  other arithmetic  8.46 us (1%)
    all_to_all x5, blocking collectives, exchange_lat(): lax.all_to_all(blocks, 'lat', split_axis=0, concat_axis=0, tiled=True)  113 us
    ppermute x39, starting transfers between devices, exchange_lon(): lax.ppermute(slot, 'lon', [(i, (i + sign * s) % lon) for i in range(lon)])  86.6 us
    pallas_call x2, Pallas kernels, feed_forward(): pl.pallas_call(kernel, out_shape=outs, grid_spec=pltpu.PrefetchScalarGrid...  82.6 us
    all_to_all x9, waiting for transfers between devices, exchange_lat(): lax.all_to_all(blocks, 'lat', split_axis=0, concat_axis=0, tiled=True)  53.3 us
    all_to_all x9, starting transfers between devices, exchange_lat(): lax.all_to_all(blocks, 'lat', split_axis=0, concat_axis=0, tiled=True)  38.9 us
    pallas_call x2, Pallas kernels, filter_call(): pl.pallas_call(kernel, out_shape=outs, grid_spec=pltpu.PrefetchScalarGrid...  29.9 us
    pallas_call x1, Pallas kernels, weight_sums(): pl.pallas_call(kernel, out_shape=shape, grid=(count * steps,), in_specs=[...  28.7 us
    pallas_call x4, Pallas kernels, first_backward(): pl.pallas_call(kernel, out_shape=outs, grid_spec=pltpu.PrefetchScalarGrid...  28.5 us
  transfers between devices with their start and end apart: 53, of which 14 were waited for; matrix products, arithmetic and copies ran while one was open for 2% of the time, Pallas kernels for 41%

profile of v5, /device:TPU:0, one launch (start us, length us, event | category | flops | bytes accessed | tf_op | source)
XLA Modules:
  0.0 630.6 jit_solution(15301860967255032281)
XLA Ops:
  38.6 7.6 %collective-permute-start.3 = (bf16[1296,128]{1,0:T(8,128)(2,1)}, bf16[1296,128]{1,0:T(8,128)(2,1)}, u32[]{:S(2)}, u32[]{:S(2)}) collective-permute-start(bf16[1296,128]{1,0:T(8,128)(2,1)} %get-tuple-element.937), channel_id=1, source_target_pairs={{0,1},{1,2},{2,3},{3,0},{4,5},{5,6},{6,7},{7,4},{8,9},{9,10},{10,1... | collective-permute-start | bytes 995336 | tf_op jit(solution)/shard_map/fields_1/ppermute | solution.py:756
  48.5 26.2 %conditional.15 = (bf16[1,128]{1,0:T(2,128)(2,1)S(1)}, bf16[768,768]{1,0:T(8,128)(2,1)}, bf16[2576,128]{1,0:T(8,128)(2,1)}, bf16[2576,128]{1,0:T(8,128)(2,1)}, b...) conditional(s32[]{:T(128)} %convert_element_type.11, () %tuple.151, (f32[2,641]{1,0:T(2,128)S(1)}, s32[1]{0:T(128)}, ...), branch_computations={%region_0.1_spmd, %region_1.2_spmd} | conditional | flops 2048 | bytes 803539520 | solution.py:775
  62.9 11.9 %all-to-all-done = bf16[8,96,768]{2,1,0:T(8,128)(2,1)} async-done(((bf16[8,96,768]{2,1,0:T(8,128)(2,1)}), bf16[8,96,768]{2,1,0:T(8,128)(2,1)}, u32[]{:S(2)}, u32[]{:S(2)}) %all-to-all-start) | async-done | bytes 1179680 | tf_op jit(solution)/shard_map/cond/branch_1_fun/spectra_0/all_to_all | solution.py:764
  78.7 26.2 %conditional.16 = (bf16[1,128]{1,0:T(2,128)(2,1)S(1)}, bf16[768,768]{1,0:T(8,128)(2,1)}, bf16[2576,128]{1,0:T(8,128)(2,1)}, bf16[2576,128]{1,0:T(8,128)(2,1)}, b...) conditional(s32[]{:T(128)} %convert_element_type.11, () %tuple.155, (s32[1]{0:T(128)}, ...), branch_computations={%region_2.3_spmd, %region_3.4_spmd} | conditional | flops 2048 | bytes 803539008 | solution.py:775
  93.0 11.9 %all-to-all-done.1 = bf16[8,96,768]{2,1,0:T(8,128)(2,1)} async-done(((bf16[8,96,768]{2,1,0:T(8,128)(2,1)}), bf16[8,96,768]{2,1,0:T(8,128)(2,1)}, u32[]{:S(2)}, u32[]{:S(2)}) %all-to-all-start.1) | async-done | bytes 1179680 | tf_op jit(solution)/shard_map/cond/branch_1_fun/spectra_1/all_to_all | solution.py:764
  110.3 25.5 %conditional.17 = (bf16[1,128]{1,0:T(2,128)(2,1)S(1)}, bf16[768,768]{1,0:T(8,128)(2,1)S(1)}) conditional(s32[]{:T(128)} %convert_element_type.11, () %tuple.159, (s32[1]{0:T(128)}, bf16[4,768,256]{2,1,0:T(8,128)(2,1)S(1)}, f32[1,768]{1,0:T(1,128)S(1)}, f32[1,768]{1,0:T(1,128)S(1)}, bf16[1296,128]{1,0:T(8,128)(2,1)}, ...), branch_computations={%region_4.5_spmd, %region_5.6_spmd} | conditional | flops 1024 | bytes 402359296 | solution.py:775
  115.3 20.5 %all_to_all.56 = bf16[8,96,768]{2,1,0:T(8,128)(2,1)S(1)} all-to-all(bf16[8,96,768]{2,1,0:T(8,128)(2,1)} %bitcast.39), channel_id=1, replica_groups=mesh['lat'=8,'lon'=4] {'lat'}, dimensions={0} | all-to-all | bytes 2359296 | tf_op jit(solution)/shard_map/cond/branch_1_fun/spectra_2/all_to_all | solution.py:764
  140.4 26.1 %conditional.18 = (bf16[1,128]{1,0:T(2,128)(2,1)S(1)}, bf16[768,768]{1,0:T(8,128)(2,1)}) conditional(s32[]{:T(128)} %convert_element_type.11, () %tuple.162, (s32[1]{0:T(128)}, bf16[4,768,256]{2,1,0:T(8,128)(2,1)S(1)}, f32[1,768]{1,0:T(1,128)S(1)}, f32[1,768]{1,0:T(1,128)S(1)}, bf16[1296,128]{1,0:T(8,128)(2,1)S(1)}, ...), branch_computations={%region_6.7_spmd, %region_7.8_spmd} | conditional | flops 1024 | bytes 402359296 | solution.py:775
  145.4 21.0 %all_to_all.57 = bf16[8,96,768]{2,1,0:T(8,128)(2,1)} all-to-all(bf16[8,96,768]{2,1,0:T(8,128)(2,1)} %bitcast.40), channel_id=1, replica_groups=mesh['lat'=8,'lon'=4] {'lat'}, dimensions={0} | all-to-all | bytes 2359296 | tf_op jit(solution)/shard_map/cond/branch_1_fun/spectra_3/all_to_all | solution.py:764
  169.0 47.0 %conditional.19 = (bf16[1,128]{1,0:T(2,128)(2,1)S(1)}, bf16[1536,768]{1,0:T(8,128)(2,1)}, bf16[1536,768]{1,0:T(8,128)(2,1)}, f32[6,512,768]{2,1,0:T(8,128)}, bf1...) conditional(s32[]{:T(128)} %convert_element_type.11, () %tuple.149, ...), branch_computations={%region_8.9_spmd, %region_9.10_spmd} | conditional | flops 1024 | bytes 407077984 | solution.py:775
  169.0 13.2 %filter_forward.1 = (bf16[1536,768]{1,0:T(8,128)(2,1)}, bf16[1536,768]{1,0:T(8,128)(2,1)}, f32[6,512,768]{2,1,0:T(8,128)}) custom-call(s32[1]{0:T(128)} %get-tuple-element.449.first_ref, bf16[96,128,128]{2,1,0:T(8,128)(2,1)} %constant.133.clone.1.to_ref, bf16[96,128,128]{2,1,0:T(8,128)(2,1)} %constant.134.clone.1.back_ref, ...), custom_call_target="tpu_custom_call" | custom-call | flops 1024 | bytes 400000000 | tf_op jit(solution)/shard_map/cond/branch_1_fun/filter_forward/pallas_call | solution.py:261
  193.6 22.5 %all-to-all-done.4 = bf16[8,192,768]{2,1,0:T(8,128)(2,1)} async-done(((bf16[8,192,768]{2,1,0:T(8,128)(2,1)}), bf16[8,192,768]{2,1,0:T(8,128)(2,1)}, u32[]{:S(2)}, u32[]{:S(2)}) %all-to-all-start.4) | async-done | bytes 2359328 | tf_op jit(solution)/shard_map/cond/branch_1_fun/synthesis_0/all_to_all | solution.py:764
  217.8 46.2 %conditional.20 = (bf16[1,128]{1,0:T(2,128)(2,1)S(1)}, bf16[2576,128]{1,0:T(8,128)(2,1)}, bf16[2576,128]{1,0:T(8,128)(2,1)}, bf16[2576,128]{1,0:T(8,128)(2,1)}, ...) conditional(s32[]{:T(128)} %convert_element_type.11, () %tuple.168, ...), branch_computations={%region_10.11_spmd, %region_11.12_spmd} | conditional | flops 1024 | bytes 408405152 | solution.py:775
  222.6 41.4 %feed_forward.2 = (bf16[2576,128]{1,0:T(8,128)(2,1)}, bf16[2576,128]{1,0:T(8,128)(2,1)}, bf16[2576,128]{1,0:T(8,128)(2,1)}, bf16[2576,128]{1,0:T(8,128)(2,1)}, f...) custom-call(s32[1]{0:T(128)} %get-tuple-element.469.me_ref, ...), custom_call_target="tpu_custom_call" | custom-call | flops 1024 | bytes 400000000 | tf_op jit(solution)/shard_map/cond/branch_1_fun/feed_forward/pallas_call | solution.py:506
  273.6 46.2 %conditional.21 = (bf16[1,128]{1,0:T(2,128)(2,1)S(1)}, bf16[1296,128]{1,0:T(8,128)(2,1)}, bf16[1296,128]{1,0:T(8,128)(2,1)}, bf16[1296,128]{1,0:T(8,128)(2,1)}, ...) conditional(s32[]{:T(128)} %convert_element_type.11, () %tuple.167, ...), branch_computations={%region_12.13_spmd, %region_13.14_spmd} | conditional | flops 1024 | bytes 408405184 | solution.py:775
  278.6 41.2 %feed_forward.3 = (bf16[1296,128]{1,0:T(8,128)(2,1)}, bf16[1296,128]{1,0:T(8,128)(2,1)}, bf16[1296,128]{1,0:T(8,128)(2,1)}, bf16[1296,128]{1,0:T(8,128)(2,1)}, b...) custom-call(s32[1]{0:T(128)} %get-tuple-element.504.me_ref, ...), custom_call_target="tpu_custom_call" | custom-call | flops 1024 | bytes 400000000 | tf_op jit(solution)/shard_map/cond/branch_1_fun/feed_forward/pallas_call | solution.py:506
  319.8 34.1 %conditional.22 = (bf16[1,128]{1,0:T(2,128)(2,1)S(1)}, bf16[1536,768]{1,0:T(8,128)(2,1)}, f32[1344,1408]{1,0:T(8,128)}) conditional(s32[]{:T(128)} %convert_element_type.11, () %tuple.171, (bf16[1536,768]{1,0:T(8,128)(2,1)}, bf16[2048,768]{1,0:T(8,128)(2,1)}, bf16[2048,1408]{1,0:T(8,128)(2,1)}, bf16[2048,1408]{1,0:T(8,128)(2,1)}, ...), branch_computations={%region_14.15_spmd, %region_15.16_spmd} | conditional | flops 1024 | bytes 407077952 | solution.py:775
  324.4 28.7 %weight_sums.1 = f32[1344,1408]{1,0:T(8,128)} custom-call(bf16[2048,768]{1,0:T(8,128)(2,1)} %get-tuple-element.544.refs_0_, bf16[2048,1408]{1,0:T(8,128)(2,1)} %get-tuple-element.545.refs_1_, bf16[2048,1408]{1,0:T(8,128)(2,1)} %get-tuple-element.546.refs_2_, bf16[2048,768]{1,0:T(8,128)(2,1)} %get-tuple-element.547.refs_3_, ...), custom_call_target="tpu_custom_call" | custom-call | flops 1024 | bytes 400000000 | tf_op jit(solution)/shard_map/cond/branch_1_fun/weight_sums/pallas_call | solution.py:563
  367.8 19.3 %conditional.23 = (bf16[1,128]{1,0:T(2,128)(2,1)S(1)}, bf16[768,768]{1,0:T(8,128)(2,1)S(1)}, bf16[768,768]{1,0:T(8,128)(2,1)}, bf16[768,768]{1,0:T(8,128)(2,1)},...) conditional(s32[]{:T(128)} %convert_element_type.11, () %tuple.147, (s32[1]{0:T(128)}, ...), branch_computations={%region_16.17_spmd, %region_17.20_spmd.clone} | conditional | flops 602368 | bytes 401058368 | solution.py:775
  367.8 16.7 %filter_backward.1 = (bf16[768,768]{1,0:T(8,128)(2,1)S(1)}, bf16[768,768]{1,0:T(8,128)(2,1)}, bf16[768,768]{1,0:T(8,128)(2,1)}, bf16[768,768]{1,0:T(8,128)(2,1)}, f32[128,768]{1,0:T(8,128)}) custom-call(s32[1]{0:T(128)} %get-tuple-element.1152.first_ref, bf16[96,128,128]{2,1,0:T(8,128)(2,1)} %constant.132.clone.2.to_ref, ...), custom_call_target="tpu_custom_call" | custom-call | flops 1024 | bytes 400000000 | tf_op jit(solution)/shard_map/cond/branch_1_fun/filter_backward/pallas_call | solution.py:261
  387.1 36.3 %conditional.24 = (bf16[1,128]{1,0:T(2,128)(2,1)S(1)}, bf16[1296,128]{1,0:T(8,128)(2,1)}, bf16[1296,128]{1,0:T(8,128)(2,1)}, bf16[1296,128]{1,0:T(8,128)(2,1)}, bf16[1296,128]{1,0:T(8,128)(2,1)}) conditional(s32[]{:T(128)} %convert_element_type.11, () %tuple.176, (bf16[768,768]{1,0:T(8,128)(2,1)S(1)}, s32[1]{0:T(128)}, ...), branch_computations={%region_20.21_spmd, %region_21.22_spmd} | conditional | flops 1024 | bytes 403686464 | solution.py:775
  387.1 28.9 %all_to_all.58 = bf16[8,96,768]{2,1,0:T(8,128)(2,1)} all-to-all(bf16[8,96,768]{2,1,0:T(8,128)(2,1)S(1)} %bitcast.41), channel_id=1, replica_groups=mesh['lat'=8,'lon'=4] {'lat'}, dimensions={0} | all-to-all | bytes 2359296 | tf_op jit(solution)/shard_map/cond/branch_1_fun/back_spectra_0/all_to_all | solution.py:764
  434.1 28.3 %conditional.25 = (bf16[1,128]{1,0:T(2,128)(2,1)S(1)}, bf16[1296,128]{1,0:T(8,128)(2,1)}, bf16[1296,128]{1,0:T(8,128)(2,1)}, bf16[1296,128]{1,0:T(8,128)(2,1)}, bf16[1296,128]{1,0:T(8,128)(2,1)}) conditional(s32[]{:T(128)} %convert_element_type.11, () %tuple.179, (bf16[768,768]{1,0:T(8,128)(2,1)}, s32[1]{0:T(128)}, ...), branch_computations={%region_22.23_spmd, %region_23.24_spmd} | conditional | flops 1024 | bytes 402359328 | solution.py:775
  434.1 21.1 %all_to_all.59 = bf16[8,96,768]{2,1,0:T(8,128)(2,1)} all-to-all(bf16[8,96,768]{2,1,0:T(8,128)(2,1)} %bitcast.19), channel_id=1, replica_groups=mesh['lat'=8,'lon'=4] {'lat'}, dimensions={0} | all-to-all | bytes 2359296 | tf_op jit(solution)/shard_map/cond/branch_1_fun/back_spectra_1/all_to_all | solution.py:764
  466.9 28.0 %conditional.26 = (bf16[1,128]{1,0:T(2,128)(2,1)S(1)}, bf16[1296,128]{1,0:T(8,128)(2,1)}, bf16[1296,128]{1,0:T(8,128)(2,1)}, bf16[1296,128]{1,0:T(8,128)(2,1)}, bf16[1296,128]{1,0:T(8,128)(2,1)}) conditional(s32[]{:T(128)} %convert_element_type.11, () %tuple.181, (bf16[768,768]{1,0:T(8,128)(2,1)}, s32[1]{0:T(128)}, ...), branch_computations={%region_25.26_spmd, %region_26.27_spmd} | conditional | flops 1024 | bytes 403686464 | solution.py:775
  467.0 21.2 %all_to_all.60 = bf16[8,96,768]{2,1,0:T(8,128)(2,1)} all-to-all(bf16[8,96,768]{2,1,0:T(8,128)(2,1)} %bitcast.21), channel_id=1, replica_groups=mesh['lat'=8,'lon'=4] {'lat'}, dimensions={0} | all-to-all | bytes 2359296 | tf_op jit(solution)/shard_map/cond/branch_1_fun/back_spectra_2/all_to_all | solution.py:764
  501.3 28.8 %conditional.27 = (bf16[1,128]{1,0:T(2,128)(2,1)S(1)}, bf16[1296,128]{1,0:T(8,128)(2,1)}, bf16[1296,128]{1,0:T(8,128)(2,1)}, bf16[1296,128]{1,0:T(8,128)(2,1)}, ...) conditional(s32[]{:T(128)} %convert_element_type.11, () %tuple.146, (bf16[768,768]{1,0:T(8,128)(2,1)}, ...), branch_computations={%region_27.28_spmd, %region_28.29_spmd} | conditional | flops 4096 | bytes 1609584768 | solution.py:775
  537.5 13.6 %collective-permute-start.34 = (bf16[1296,128]{1,0:T(8,128)(2,1)}, bf16[1296,128]{1,0:T(8,128)(2,1)}, u32[]{:S(2)}, u32[]{:S(2)}) collective-permute-start(bf16[1296,128]{1,0:T(8,128)(2,1)} %get-tuple-element.1094), channel_id=1, source_target_pairs={{0,2},{1,3},{2,0},{3,1},{4,6},{5,7},{6,4},{7,5},{8,10},{9,11},{10,... | collective-permute-start | bytes 995336 | tf_op jit(solution)/shard_map/input_grad_3/ppermute | solution.py:756
  553.1 16.3 %conditional.28 = (bf16[1,128]{1,0:T(2,128)(2,1)S(1)}, f32[24,768]{1,0:T(8,128)S(1)}, f32[4,16,64,641]{3,2,1,0:T(8,128)}) conditional(s32[]{:T(128)} %convert_element_type.11, () %tuple.188, (f32[192,768]{1,0:T(8,128)}, s32[1]{0:T(128)}, bf16[1296,128]{1,0:T(8,128)(2,1)}, bf16[1296,128]{1,0:T(8,128)(2,1)}, bf16[1296,128]{1,0:T(8,128)(2,1)}, ...), branch_computations={%region_30.31_spmd, %region_31.33_spmd} | conditional | flops 132096 | bytes 1202433024 | solution.py:775
  588.3 23.0 %conditional.29 = (f32[192,768]{1,0:T(8,128)}, f32[641,1282]{1,0:T(8,128)}, f32[641,1282]{1,0:T(8,128)}, f32[641]{0:T(1024)}, f32[1282]{0:T(1024)}, /*index=5*/f...) conditional(s32[]{:T(128)} %convert_element_type.11, () %tuple.187, ...), branch_computations={%region_33.34_spmd, %region_34.35_spmd} | conditional | flops 20480 | bytes 817823936 | solution.py:775
  594.8 7.5 %adafactor.2 = (f32[641,1282]{1,0:T(8,128)}, f32[641,1282]{1,0:T(8,128)}, f32[641]{0:T(1024)}, f32[1282]{0:T(1024)}) custom-call(bf16[1344,1408]{1,0:T(8,128)(2,1)} %get-tuple-element.657.grad_ref, f32[641,1282]{1,0:T(8,128)} %get-tuple-element.658.weight_ref, f32[641,1]{1,0:T(8,128)} %broadcast_in_dim.11.rows_ref, f32[1,1282]{1,0:T(1,128)} %broadcast_in_dim.2.columns_ref), custom_call_target="tpu_custom_call" | custom-call | flops 1024 | bytes 400000000 | tf_op jit(solution)/shard_map/cond/branch_1_fun/adafactor/pallas_call | solution.py:672
  603.8 7.4 %adafactor.3 = (f32[641,1282]{1,0:T(8,128)}, f32[641,1282]{1,0:T(8,128)}, f32[641]{0:T(1024)}, f32[1282]{0:T(1024)}) custom-call(bf16[1344,1408]{1,0:T(8,128)(2,1)S(1)} %copy-done.4, f32[641,1282]{1,0:T(8,128)} %bitcast.35, f32[641,1]{1,0:T(8,128)} %broadcast_in_dim.12.rows_ref, f32[1,1282]{1,0:T(1,128)} %broadcast_in_dim.10.columns_ref), custom_call_target="tpu_custom_call" | custom-call | flops 1024 | bytes 400000000 | tf_op jit(solution)/shard_map/cond/branch_1_fun/adafactor/pallas_call | solution.py:672
  (255 shorter events, 277.4 us)
Async XLA Ops:
  7.2 457.0 %reduce-scatter.4.cloned.1.call-start = ((), (), s32[]{:S(2)}) async-start(), calls=%async_computation.17 | async-start | bytes 8515584
  38.6 36.2 %collective-permute-start.3 = (bf16[1296,128]{1,0:T(8,128)(2,1)}, bf16[1296,128]{1,0:T(8,128)(2,1)}, u32[]{:S(2)}, u32[]{:S(2)}) collective-permute-start(bf16[1296,128]{1,0:T(8,128)(2,1)} %get-tuple-element.937), channel_id=1, source_target_pairs={{0,1},{1,2},{2,3},{3,0},{4,5},{5,6},{6,7},{7,4},{8,9},{9,10},{10,1... | collective-permute-start | bytes 995336 | tf_op jit(solution)/shard_map/fields_1/ppermute | solution.py:756
  135.8 80.3 %collective-permute-start.12 = (bf16[2576,128]{1,0:T(8,128)(2,1)}, bf16[2576,128]{1,0:T(8,128)(2,1)}, u32[]{:S(2)}, u32[]{:S(2)}) collective-permute-start(bf16[2576,128]{1,0:T(8,128)(2,1)} %get-tuple-element.1014), channel_id=1, source_target_pairs={{0,1},{1,2},{2,3},{3,0},{4,5},{5,6},{6,7},{7,4},{8,9},{9,10},{10,1... | collective-permute-start | bytes 1978376 | tf_op jit(solution)/shard_map/upstream_0/ppermute | solution.py:756
  138.0 79.8 %collective-permute-start.13 = (bf16[2576,128]{1,0:T(8,128)(2,1)}, bf16[2576,128]{1,0:T(8,128)(2,1)}, u32[]{:S(2)}, u32[]{:S(2)}) collective-permute-start(bf16[2576,128]{1,0:T(8,128)(2,1)} %get-tuple-element.1015), channel_id=1, source_target_pairs={{0,2},{1,3},{2,0},{3,1},{4,6},{5,7},{6,4},{7,5},{8,10},{9,11},{10,... | collective-permute-start | bytes 1978376 | tf_op jit(solution)/shard_map/upstream_0/ppermute | solution.py:756
  140.3 77.5 %collective-permute-start.14 = (bf16[2576,128]{1,0:T(8,128)(2,1)}, bf16[2576,128]{1,0:T(8,128)(2,1)}, u32[]{:S(2)}, u32[]{:S(2)}) collective-permute-start(bf16[2576,128]{1,0:T(8,128)(2,1)} %get-tuple-element.1016), channel_id=1, source_target_pairs={{0,3},{1,0},{2,1},{3,2},{4,7},{5,4},{6,5},{7,6},{8,11},{9,8},{10,9... | collective-permute-start | bytes 1978376 | tf_op jit(solution)/shard_map/upstream_0/ppermute | solution.py:756
  166.5 107.1 %collective-permute-start.15 = (bf16[2576,128]{1,0:T(8,128)(2,1)}, bf16[2576,128]{1,0:T(8,128)(2,1)}, u32[]{:S(2)}, u32[]{:S(2)}) collective-permute-start(bf16[2576,128]{1,0:T(8,128)(2,1)} %get-tuple-element.1021), channel_id=1, source_target_pairs={{0,1},{1,2},{2,3},{3,0},{4,5},{5,6},{6,7},{7,4},{8,9},{9,10},{10,1... | collective-permute-start | bytes 1978376 | tf_op jit(solution)/shard_map/upstream_1/ppermute | solution.py:756
  168.4 105.2 %collective-permute-start.16 = (bf16[2576,128]{1,0:T(8,128)(2,1)}, bf16[2576,128]{1,0:T(8,128)(2,1)}, u32[]{:S(2)}, u32[]{:S(2)}) collective-permute-start(bf16[2576,128]{1,0:T(8,128)(2,1)} %get-tuple-element.1022), channel_id=1, source_target_pairs={{0,2},{1,3},{2,0},{3,1},{4,6},{5,7},{6,4},{7,5},{8,10},{9,11},{10,... | collective-permute-start | bytes 1978376 | tf_op jit(solution)/shard_map/upstream_1/ppermute | solution.py:756
  182.2 33.9 %all-to-all-start.4 = ((bf16[8,192,768]{2,1,0:T(8,128)(2,1)}), bf16[8,192,768]{2,1,0:T(8,128)(2,1)}, u32[]{:S(2)}, u32[]{:S(2)}) async-start(bf16[8,192,768]{2,1,0:T(8,128)(2,1)} %bitcast.46), calls=%async_computation.4 | async-start | bytes 4718592 | tf_op jit(solution)/shard_map/cond/branch_1_fun/synthesis_0/all_to_all | solution.py:764
  216.1 57.5 %collective-permute-start.17 = (bf16[2576,128]{1,0:T(8,128)(2,1)}, bf16[2576,128]{1,0:T(8,128)(2,1)}, u32[]{:S(2)}, u32[]{:S(2)}) collective-permute-start(bf16[2576,128]{1,0:T(8,128)(2,1)} %get-tuple-element.1023), channel_id=1, source_target_pairs={{0,3},{1,0},{2,1},{3,2},{4,7},{5,4},{6,5},{7,6},{8,11},{9,8},{10,9... | collective-permute-start | bytes 1978376 | tf_op jit(solution)/shard_map/upstream_1/ppermute | solution.py:756
  217.9 46.2 %all-to-all-start.5 = ((bf16[8,192,768]{2,1,0:T(8,128)(2,1)}), bf16[8,192,768]{2,1,0:T(8,128)(2,1)}, u32[]{:S(2)}, u32[]{:S(2)}) async-start(bf16[8,192,768]{2,1,0:T(8,128)(2,1)} %bitcast.11), calls=%async_computation.5 | async-start | bytes 4718592 | tf_op jit(solution)/shard_map/cond/branch_1_fun/synthesis_1/all_to_all | solution.py:764
  264.0 89.8 %collective-permute-start.18 = (bf16[2576,128]{1,0:T(8,128)(2,1)}, bf16[2576,128]{1,0:T(8,128)(2,1)}, u32[]{:S(2)}, u32[]{:S(2)}) collective-permute-start(bf16[2576,128]{1,0:T(8,128)(2,1)} %get-tuple-element.1041), channel_id=1, source_target_pairs={{0,3},{1,0},{2,1},{3,2},{4,7},{5,4},{6,5},{7,6},{8,11},{9,8},{10,9... | collective-permute-start | bytes 1978376 | tf_op jit(solution)/shard_map/output_0_0/ppermute | solution.py:756
  266.1 87.7 %collective-permute-start.19 = (bf16[2576,128]{1,0:T(8,128)(2,1)}, bf16[2576,128]{1,0:T(8,128)(2,1)}, u32[]{:S(2)}, u32[]{:S(2)}) collective-permute-start(bf16[2576,128]{1,0:T(8,128)(2,1)} %get-tuple-element.1042), channel_id=1, source_target_pairs={{0,2},{1,3},{2,0},{3,1},{4,6},{5,7},{6,4},{7,5},{8,10},{9,11},{10,... | collective-permute-start | bytes 1978376 | tf_op jit(solution)/shard_map/output_0_0/ppermute | solution.py:756
  273.6 80.3 %collective-permute-start.20 = (bf16[2576,128]{1,0:T(8,128)(2,1)}, bf16[2576,128]{1,0:T(8,128)(2,1)}, u32[]{:S(2)}, u32[]{:S(2)}) collective-permute-start(bf16[2576,128]{1,0:T(8,128)(2,1)} %get-tuple-element.1043), channel_id=1, source_target_pairs={{0,1},{1,2},{2,3},{3,0},{4,5},{5,6},{6,7},{7,4},{8,9},{9,10},{10,1... | collective-permute-start | bytes 1978376 | tf_op jit(solution)/shard_map/output_0_0/ppermute | solution.py:756
  273.6 46.2 %all-to-all-start.6 = ((bf16[8,192,768]{2,1,0:T(8,128)(2,1)}), bf16[8,192,768]{2,1,0:T(8,128)(2,1)}, u32[]{:S(2)}, u32[]{:S(2)}) async-start(bf16[8,192,768]{2,1,0:T(8,128)(2,1)} %bitcast.13), calls=%async_computation.6 | async-start | bytes 4718592 | tf_op jit(solution)/shard_map/cond/branch_1_fun/back_synthesis_0/all_to_all | solution.py:764
  319.8 34.1 %all-to-all-start.7 = ((bf16[8,192,768]{2,1,0:T(8,128)(2,1)}), bf16[8,192,768]{2,1,0:T(8,128)(2,1)}, u32[]{:S(2)}, u32[]{:S(2)}) async-start(bf16[8,192,768]{2,1,0:T(8,128)(2,1)} %bitcast.15), calls=%async_computation.7 | async-start | bytes 4718592 | tf_op jit(solution)/shard_map/cond/branch_1_fun/back_synthesis_1/all_to_all | solution.py:764
  353.9 183.5 %all-reduce.8.cloned.1.call-start = ((), (), s32[]{:S(2)}) async-start(), calls=%async_computation.15 | async-start | bytes 946176 | tf_op jit(solution)/shard_map/weights_lon/psum | solution.py:961
  358.4 73.6 %collective-permute-start.24 = (bf16[1296,128]{1,0:T(8,128)(2,1)}, bf16[1296,128]{1,0:T(8,128)(2,1)}, u32[]{:S(2)}, u32[]{:S(2)}) collective-permute-start(bf16[1296,128]{1,0:T(8,128)(2,1)} %get-tuple-element.1063), channel_id=1, source_target_pairs={{0,3},{1,0},{2,1},{3,2},{4,7},{5,4},{6,5},{7,6},{8,11},{9,8},{10,9... | collective-permute-start | bytes 995336 | tf_op jit(solution)/shard_map/output_1_1/ppermute | solution.py:756
  361.6 72.4 %collective-permute-start.25 = (bf16[1296,128]{1,0:T(8,128)(2,1)}, bf16[1296,128]{1,0:T(8,128)(2,1)}, u32[]{:S(2)}, u32[]{:S(2)}) collective-permute-start(bf16[1296,128]{1,0:T(8,128)(2,1)} %get-tuple-element.1064), channel_id=1, source_target_pairs={{0,2},{1,3},{2,0},{3,1},{4,6},{5,7},{6,4},{7,5},{8,10},{9,11},{10,... | collective-permute-start | bytes 995336 | tf_op jit(solution)/shard_map/output_1_1/ppermute | solution.py:756
  367.1 66.9 %collective-permute-start.26 = (bf16[1296,128]{1,0:T(8,128)(2,1)}, bf16[1296,128]{1,0:T(8,128)(2,1)}, u32[]{:S(2)}, u32[]{:S(2)}) collective-permute-start(bf16[1296,128]{1,0:T(8,128)(2,1)} %get-tuple-element.1065), channel_id=1, source_target_pairs={{0,1},{1,2},{2,3},{3,0},{4,5},{5,6},{6,7},{7,4},{8,9},{9,10},{10,1... | collective-permute-start | bytes 995336 | tf_op jit(solution)/shard_map/output_1_1/ppermute | solution.py:756
  423.4 42.9 %collective-permute-start.30 = (bf16[1296,128]{1,0:T(8,128)(2,1)}, bf16[1296,128]{1,0:T(8,128)(2,1)}, u32[]{:S(2)}, u32[]{:S(2)}) collective-permute-start(bf16[1296,128]{1,0:T(8,128)(2,1)} %get-tuple-element.1082), channel_id=1, source_target_pairs={{0,3},{1,0},{2,1},{3,2},{4,7},{5,4},{6,5},{7,6},{8,11},{9,8},{10,9... | collective-permute-start | bytes 995336 | tf_op jit(solution)/shard_map/input_grad_0/ppermute | solution.py:756
  426.8 40.1 %collective-permute-start.31 = (bf16[1296,128]{1,0:T(8,128)(2,1)}, bf16[1296,128]{1,0:T(8,128)(2,1)}, u32[]{:S(2)}, u32[]{:S(2)}) collective-permute-start(bf16[1296,128]{1,0:T(8,128)(2,1)} %get-tuple-element.1083), channel_id=1, source_target_pairs={{0,2},{1,3},{2,0},{3,1},{4,6},{5,7},{6,4},{7,5},{8,10},{9,11},{10,... | collective-permute-start | bytes 995336 | tf_op jit(solution)/shard_map/input_grad_0/ppermute | solution.py:756
  432.0 34.9 %collective-permute-start.32 = (bf16[1296,128]{1,0:T(8,128)(2,1)}, bf16[1296,128]{1,0:T(8,128)(2,1)}, u32[]{:S(2)}, u32[]{:S(2)}) collective-permute-start(bf16[1296,128]{1,0:T(8,128)(2,1)} %get-tuple-element.1084), channel_id=1, source_target_pairs={{0,1},{1,2},{2,3},{3,0},{4,5},{5,6},{6,7},{7,4},{8,9},{9,10},{10,1... | collective-permute-start | bytes 995336 | tf_op jit(solution)/shard_map/input_grad_0/ppermute | solution.py:756
  462.3 37.0 %collective-permute-start.27 = (bf16[1296,128]{1,0:T(8,128)(2,1)}, bf16[1296,128]{1,0:T(8,128)(2,1)}, u32[]{:S(2)}, u32[]{:S(2)}) collective-permute-start(bf16[1296,128]{1,0:T(8,128)(2,1)} %get-tuple-element.1077), channel_id=1, source_target_pairs={{0,3},{1,0},{2,1},{3,2},{4,7},{5,4},{6,5},{7,6},{8,11},{9,8},{10,9... | collective-permute-start | bytes 995336 | tf_op jit(solution)/shard_map/input_grad_1/ppermute | solution.py:756
  466.2 122.0 %all-gather.2.cloned.1.call-start = ((), (), s32[]{:S(2)}) async-start(), calls=%async_computation.16 | async-start | bytes 4257792 | tf_op jit(solution)/shard_map/weights_lat/all_gather | solution.py:1009
  466.3 35.1 %collective-permute-start.28 = (bf16[1296,128]{1,0:T(8,128)(2,1)}, bf16[1296,128]{1,0:T(8,128)(2,1)}, u32[]{:S(2)}, u32[]{:S(2)}) collective-permute-start(bf16[1296,128]{1,0:T(8,128)(2,1)} %get-tuple-element.1078), channel_id=1, source_target_pairs={{0,2},{1,3},{2,0},{3,1},{4,6},{5,7},{6,4},{7,5},{8,10},{9,11},{10,... | collective-permute-start | bytes 995336 | tf_op jit(solution)/shard_map/input_grad_1/ppermute | solution.py:756
  466.3 35.0 %collective-permute-start.29 = (bf16[1296,128]{1,0:T(8,128)(2,1)}, bf16[1296,128]{1,0:T(8,128)(2,1)}, u32[]{:S(2)}, u32[]{:S(2)}) collective-permute-start(bf16[1296,128]{1,0:T(8,128)(2,1)} %get-tuple-element.1079), channel_id=1, source_target_pairs={{0,1},{1,2},{2,3},{3,0},{4,5},{5,6},{6,7},{7,4},{8,9},{9,10},{10,1... | collective-permute-start | bytes 995336 | tf_op jit(solution)/shard_map/input_grad_1/ppermute | solution.py:756
  495.0 35.2 %collective-permute-start.36 = (bf16[1296,128]{1,0:T(8,128)(2,1)}, bf16[1296,128]{1,0:T(8,128)(2,1)}, u32[]{:S(2)}, u32[]{:S(2)}) collective-permute-start(bf16[1296,128]{1,0:T(8,128)(2,1)} %get-tuple-element.1107), channel_id=1, source_target_pairs={{0,3},{1,0},{2,1},{3,2},{4,7},{5,4},{6,5},{7,6},{8,11},{9,8},{10,9... | collective-permute-start | bytes 995336 | tf_op jit(solution)/shard_map/input_grad_2/ppermute | solution.py:756
  498.3 38.6 %collective-permute-start.37 = (bf16[1296,128]{1,0:T(8,128)(2,1)}, bf16[1296,128]{1,0:T(8,128)(2,1)}, u32[]{:S(2)}, u32[]{:S(2)}) collective-permute-start(bf16[1296,128]{1,0:T(8,128)(2,1)} %get-tuple-element.1108), channel_id=1, source_target_pairs={{0,2},{1,3},{2,0},{3,1},{4,6},{5,7},{6,4},{7,5},{8,10},{9,11},{10,... | collective-permute-start | bytes 995336 | tf_op jit(solution)/shard_map/input_grad_2/ppermute | solution.py:756
  499.3 37.5 %collective-permute-start.38 = (bf16[1296,128]{1,0:T(8,128)(2,1)}, bf16[1296,128]{1,0:T(8,128)(2,1)}, u32[]{:S(2)}, u32[]{:S(2)}) collective-permute-start(bf16[1296,128]{1,0:T(8,128)(2,1)} %get-tuple-element.1109), channel_id=1, source_target_pairs={{0,1},{1,2},{2,3},{3,0},{4,5},{5,6},{6,7},{7,4},{8,9},{9,10},{10,1... | collective-permute-start | bytes 995336 | tf_op jit(solution)/shard_map/input_grad_2/ppermute | solution.py:756
  537.5 73.9 %collective-permute-start.33 = (bf16[1296,128]{1,0:T(8,128)(2,1)}, bf16[1296,128]{1,0:T(8,128)(2,1)}, u32[]{:S(2)}, u32[]{:S(2)}) collective-permute-start(bf16[1296,128]{1,0:T(8,128)(2,1)} %get-tuple-element.1093), channel_id=1, source_target_pairs={{0,3},{1,0},{2,1},{3,2},{4,7},{5,4},{6,5},{7,6},{8,11},{9,8},{10,9... | collective-permute-start | bytes 995336 | tf_op jit(solution)/shard_map/input_grad_3/ppermute | solution.py:756
  537.5 73.8 %collective-permute-start.34 = (bf16[1296,128]{1,0:T(8,128)(2,1)}, bf16[1296,128]{1,0:T(8,128)(2,1)}, u32[]{:S(2)}, u32[]{:S(2)}) collective-permute-start(bf16[1296,128]{1,0:T(8,128)(2,1)} %get-tuple-element.1094), channel_id=1, source_target_pairs={{0,2},{1,3},{2,0},{3,1},{4,6},{5,7},{6,4},{7,5},{8,10},{9,11},{10,... | collective-permute-start | bytes 995336 | tf_op jit(solution)/shard_map/input_grad_3/ppermute | solution.py:756
  551.1 60.2 %collective-permute-start.35 = (bf16[1296,128]{1,0:T(8,128)(2,1)}, bf16[1296,128]{1,0:T(8,128)(2,1)}, u32[]{:S(2)}, u32[]{:S(2)}) collective-permute-start(bf16[1296,128]{1,0:T(8,128)(2,1)} %get-tuple-element.1095), channel_id=1, source_target_pairs={{0,1},{1,2},{2,3},{3,0},{4,5},{5,6},{6,7},{7,4},{8,9},{9,10},{10,1... | collective-permute-start | bytes 995336 | tf_op jit(solution)/shard_map/input_grad_3/ppermute | solution.py:756
  (67 other events, 1416.9 us)
Sparse Core Ops, SparseCore 0:
  354.0 79.5 reduce-scatter.3
  466.3 71.0 all-reduce.7
  539.3 48.8 all-gather.1

commit v6 on v5

--- a/solution.py
+++ b/solution.py
@@ -1018,13 +1018,14 @@
         )
         return gathered(small), inner, outer
 
-    small, inner, outer = unit(to_updates, small, summed, weight_in, weight_out)
-    grad_weight_in, new_weight_in, new_in_rows, new_in_columns = inner
-    grad_weight_out, new_weight_out, new_out_columns, new_out_rows = outer
     gradients[-1], small = tie(gradients[-1], small)
     input_grad = unpack(
         me, gradients[-1], input_grad, chunks - 1, depth, fields_in.shape, F32
     )
+    input_grad, order[0] = tie(input_grad, order[0])
+    small, inner, outer = unit(to_updates, small, summed, weight_in, weight_out)
+    grad_weight_in, new_weight_in, new_in_rows, new_in_columns = inner
+    grad_weight_out, new_weight_out, new_out_columns, new_out_rows = outer
 
     grad_filter = small[:L, :channels]
     grad_one = jnp.sum(spectral_filter * grad_filter, axis=0) / norm_gains[0]

time: 640 us -> 639 us (level)
  transfers between devices with their start and end apart: 53 -> 53, of which waited for: 14 -> 14; matrix products, arithmetic and copies ran while one was open for 2% -> 1% of each run, Pallas kernels for 41% -> 41%
where the time goes in v6:
time: 639 us; the launch traced here: 629 us
  Pallas kernels  264 us (41%)
  starting transfers between devices  130 us (20%)
  blocking collectives  113 us (18%)
  waiting for transfers between devices  86.4 us (14%)
  between operations  16.6 us (3%)
  local copies, waits for them, and re-layouts  10.4 us (2%)
  other arithmetic  8.46 us (1%)
    all_to_all x5, blocking collectives, exchange_lat(): lax.all_to_all(blocks, 'lat', split_axis=0, concat_axis=0, tiled=True)  113 us
    ppermute x39, starting transfers between devices, exchange_lon(): lax.ppermute(slot, 'lon', [(i, (i + sign * s) % lon) for i in range(lon)])  86.3 us
    pallas_call x2, Pallas kernels, feed_forward(): pl.pallas_call(kernel, out_shape=outs, grid_spec=pltpu.PrefetchScalarGrid...  82.6 us
    all_to_all x9, waiting for transfers between devices, exchange_lat(): lax.all_to_all(blocks, 'lat', split_axis=0, concat_axis=0, tiled=True)  53.3 us
    all_to_all x9, starting transfers between devices, exchange_lat(): lax.all_to_all(blocks, 'lat', split_axis=0, concat_axis=0, tiled=True)  41.3 us
    pallas_call x2, Pallas kernels, filter_call(): pl.pallas_call(kernel, out_shape=outs, grid_spec=pltpu.PrefetchScalarGrid...  29.9 us
    pallas_call x1, Pallas kernels, weight_sums(): pl.pallas_call(kernel, out_shape=shape, grid=(count * steps,), in_specs=[...  28.7 us
    pallas_call x4, Pallas kernels, first_backward(): pl.pallas_call(kernel, out_shape=outs, grid_spec=pltpu.PrefetchScalarGrid...  28.4 us
  transfers between devices with their start and end apart: 53, of which 14 were waited for; matrix products, arithmetic and copies ran while one was open for 1% of the time, Pallas kernels for 41%

profile of v6, /device:TPU:0, one launch (start us, length us, event | category | flops | bytes accessed | tf_op | source)
XLA Modules:
  0.0 629.1 jit_solution(1865028406936096348)
XLA Ops:
  38.6 7.6 %collective-permute-start.3 = (bf16[1296,128]{1,0:T(8,128)(2,1)}, bf16[1296,128]{1,0:T(8,128)(2,1)}, u32[]{:S(2)}, u32[]{:S(2)}) collective-permute-start(bf16[1296,128]{1,0:T(8,128)(2,1)} %get-tuple-element.939), channel_id=1, source_target_pairs={{0,1},{1,2},{2,3},{3,0},{4,5},{5,6},{6,7},{7,4},{8,9},{9,10},{10,1... | collective-permute-start | bytes 995336 | tf_op jit(solution)/shard_map/fields_1/ppermute | solution.py:756
  48.5 26.2 %conditional.15 = (bf16[1,128]{1,0:T(2,128)(2,1)S(1)}, bf16[768,768]{1,0:T(8,128)(2,1)}, bf16[2576,128]{1,0:T(8,128)(2,1)}, bf16[2576,128]{1,0:T(8,128)(2,1)}, b...) conditional(s32[]{:T(128)} %convert_element_type.11, () %tuple.152, (f32[2,641]{1,0:T(2,128)S(1)}, s32[1]{0:T(128)}, ...), branch_computations={%region_0.1_spmd, %region_1.2_spmd} | conditional | flops 2048 | bytes 803539520 | solution.py:775
  62.9 11.9 %all-to-all-done = bf16[8,96,768]{2,1,0:T(8,128)(2,1)} async-done(((bf16[8,96,768]{2,1,0:T(8,128)(2,1)}), bf16[8,96,768]{2,1,0:T(8,128)(2,1)}, u32[]{:S(2)}, u32[]{:S(2)}) %all-to-all-start) | async-done | bytes 1179680 | tf_op jit(solution)/shard_map/cond/branch_1_fun/spectra_0/all_to_all | solution.py:764
  78.7 26.2 %conditional.16 = (bf16[1,128]{1,0:T(2,128)(2,1)S(1)}, bf16[768,768]{1,0:T(8,128)(2,1)}, bf16[2576,128]{1,0:T(8,128)(2,1)}, bf16[2576,128]{1,0:T(8,128)(2,1)}, b...) conditional(s32[]{:T(128)} %convert_element_type.11, () %tuple.156, (s32[1]{0:T(128)}, ...), branch_computations={%region_2.3_spmd, %region_3.4_spmd} | conditional | flops 2048 | bytes 803539008 | solution.py:775
  93.1 11.8 %all-to-all-done.1 = bf16[8,96,768]{2,1,0:T(8,128)(2,1)} async-done(((bf16[8,96,768]{2,1,0:T(8,128)(2,1)}), bf16[8,96,768]{2,1,0:T(8,128)(2,1)}, u32[]{:S(2)}, u32[]{:S(2)}) %all-to-all-start.1) | async-done | bytes 1179680 | tf_op jit(solution)/shard_map/cond/branch_1_fun/spectra_1/all_to_all | solution.py:764
  110.3 25.5 %conditional.17 = (bf16[1,128]{1,0:T(2,128)(2,1)S(1)}, bf16[768,768]{1,0:T(8,128)(2,1)S(1)}) conditional(s32[]{:T(128)} %convert_element_type.11, () %tuple.160, (s32[1]{0:T(128)}, bf16[4,768,256]{2,1,0:T(8,128)(2,1)S(1)}, f32[1,768]{1,0:T(1,128)S(1)}, f32[1,768]{1,0:T(1,128)S(1)}, bf16[1296,128]{1,0:T(8,128)(2,1)}, ...), branch_computations={%region_4.5_spmd, %region_5.6_spmd} | conditional | flops 1024 | bytes 402359296 | solution.py:775
  115.3 20.5 %all_to_all.56 = bf16[8,96,768]{2,1,0:T(8,128)(2,1)S(1)} all-to-all(bf16[8,96,768]{2,1,0:T(8,128)(2,1)} %bitcast.39), channel_id=1, replica_groups=mesh['lat'=8,'lon'=4] {'lat'}, dimensions={0} | all-to-all | bytes 2359296 | tf_op jit(solution)/shard_map/cond/branch_1_fun/spectra_2/all_to_all | solution.py:764
  140.4 26.1 %conditional.18 = (bf16[1,128]{1,0:T(2,128)(2,1)S(1)}, bf16[768,768]{1,0:T(8,128)(2,1)}) conditional(s32[]{:T(128)} %convert_element_type.11, () %tuple.163, (s32[1]{0:T(128)}, bf16[4,768,256]{2,1,0:T(8,128)(2,1)S(1)}, f32[1,768]{1,0:T(1,128)S(1)}, f32[1,768]{1,0:T(1,128)S(1)}, bf16[1296,128]{1,0:T(8,128)(2,1)S(1)}, ...), branch_computations={%region_6.7_spmd, %region_7.8_spmd} | conditional | flops 1024 | bytes 402359296 | solution.py:775
  145.4 21.0 %all_to_all.57 = bf16[8,96,768]{2,1,0:T(8,128)(2,1)} all-to-all(bf16[8,96,768]{2,1,0:T(8,128)(2,1)} %bitcast.40), channel_id=1, replica_groups=mesh['lat'=8,'lon'=4] {'lat'}, dimensions={0} | all-to-all | bytes 2359296 | tf_op jit(solution)/shard_map/cond/branch_1_fun/spectra_3/all_to_all | solution.py:764
  169.0 47.0 %conditional.19 = (bf16[1,128]{1,0:T(2,128)(2,1)S(1)}, bf16[1536,768]{1,0:T(8,128)(2,1)}, bf16[1536,768]{1,0:T(8,128)(2,1)}, f32[6,512,768]{2,1,0:T(8,128)}, bf1...) conditional(s32[]{:T(128)} %convert_element_type.11, () %tuple.150, ...), branch_computations={%region_8.9_spmd, %region_9.10_spmd} | conditional | flops 1024 | bytes 407077984 | solution.py:775
  169.0 13.2 %filter_forward.1 = (bf16[1536,768]{1,0:T(8,128)(2,1)}, bf16[1536,768]{1,0:T(8,128)(2,1)}, f32[6,512,768]{2,1,0:T(8,128)}) custom-call(s32[1]{0:T(128)} %get-tuple-element.449.first_ref, bf16[96,128,128]{2,1,0:T(8,128)(2,1)} %constant.133.clone.1.to_ref, bf16[96,128,128]{2,1,0:T(8,128)(2,1)} %constant.134.clone.1.back_ref, ...), custom_call_target="tpu_custom_call" | custom-call | flops 1024 | bytes 400000000 | tf_op jit(solution)/shard_map/cond/branch_1_fun/filter_forward/pallas_call | solution.py:261
  193.6 22.5 %all-to-all-done.4 = bf16[8,192,768]{2,1,0:T(8,128)(2,1)} async-done(((bf16[8,192,768]{2,1,0:T(8,128)(2,1)}), bf16[8,192,768]{2,1,0:T(8,128)(2,1)}, u32[]{:S(2)}, u32[]{:S(2)}) %all-to-all-start.4) | async-done | bytes 2359328 | tf_op jit(solution)/shard_map/cond/branch_1_fun/synthesis_0/all_to_all | solution.py:764
  217.8 46.2 %conditional.20 = (bf16[1,128]{1,0:T(2,128)(2,1)S(1)}, bf16[2576,128]{1,0:T(8,128)(2,1)}, bf16[2576,128]{1,0:T(8,128)(2,1)}, bf16[2576,128]{1,0:T(8,128)(2,1)}, ...) conditional(s32[]{:T(128)} %convert_element_type.11, () %tuple.169, ...), branch_computations={%region_10.11_spmd, %region_11.12_spmd} | conditional | flops 1024 | bytes 408405152 | solution.py:775
  222.6 41.4 %feed_forward.2 = (bf16[2576,128]{1,0:T(8,128)(2,1)}, bf16[2576,128]{1,0:T(8,128)(2,1)}, bf16[2576,128]{1,0:T(8,128)(2,1)}, bf16[2576,128]{1,0:T(8,128)(2,1)}, f...) custom-call(s32[1]{0:T(128)} %get-tuple-element.469.me_ref, ...), custom_call_target="tpu_custom_call" | custom-call | flops 1024 | bytes 400000000 | tf_op jit(solution)/shard_map/cond/branch_1_fun/feed_forward/pallas_call | solution.py:506
  273.6 46.2 %conditional.21 = (bf16[1,128]{1,0:T(2,128)(2,1)S(1)}, bf16[1296,128]{1,0:T(8,128)(2,1)}, bf16[1296,128]{1,0:T(8,128)(2,1)}, bf16[1296,128]{1,0:T(8,128)(2,1)}, ...) conditional(s32[]{:T(128)} %convert_element_type.11, () %tuple.168, ...), branch_computations={%region_12.13_spmd, %region_13.14_spmd} | conditional | flops 1024 | bytes 408405184 | solution.py:775
  278.6 41.2 %feed_forward.3 = (bf16[1296,128]{1,0:T(8,128)(2,1)}, bf16[1296,128]{1,0:T(8,128)(2,1)}, bf16[1296,128]{1,0:T(8,128)(2,1)}, bf16[1296,128]{1,0:T(8,128)(2,1)}, b...) custom-call(s32[1]{0:T(128)} %get-tuple-element.504.me_ref, ...), custom_call_target="tpu_custom_call" | custom-call | flops 1024 | bytes 400000000 | tf_op jit(solution)/shard_map/cond/branch_1_fun/feed_forward/pallas_call | solution.py:506
  319.8 34.0 %conditional.22 = (bf16[1,128]{1,0:T(2,128)(2,1)S(1)}, bf16[1536,768]{1,0:T(8,128)(2,1)}, f32[1344,1408]{1,0:T(8,128)}) conditional(s32[]{:T(128)} %convert_element_type.11, () %tuple.172, (bf16[1536,768]{1,0:T(8,128)(2,1)}, bf16[2048,768]{1,0:T(8,128)(2,1)}, bf16[2048,1408]{1,0:T(8,128)(2,1)}, bf16[2048,1408]{1,0:T(8,128)(2,1)}, ...), branch_computations={%region_14.15_spmd, %region_15.16_spmd} | conditional | flops 1024 | bytes 407077952 | solution.py:775
  324.4 28.7 %weight_sums.1 = f32[1344,1408]{1,0:T(8,128)} custom-call(bf16[2048,768]{1,0:T(8,128)(2,1)} %get-tuple-element.544.refs_0_, bf16[2048,1408]{1,0:T(8,128)(2,1)} %get-tuple-element.545.refs_1_, bf16[2048,1408]{1,0:T(8,128)(2,1)} %get-tuple-element.546.refs_2_, bf16[2048,768]{1,0:T(8,128)(2,1)} %get-tuple-element.547.refs_3_, ...), custom_call_target="tpu_custom_call" | custom-call | flops 1024 | bytes 400000000 | tf_op jit(solution)/shard_map/cond/branch_1_fun/weight_sums/pallas_call | solution.py:563
  367.8 19.3 %conditional.23 = (bf16[1,128]{1,0:T(2,128)(2,1)S(1)}, bf16[768,768]{1,0:T(8,128)(2,1)S(1)}, bf16[768,768]{1,0:T(8,128)(2,1)}, bf16[768,768]{1,0:T(8,128)(2,1)},...) conditional(s32[]{:T(128)} %convert_element_type.11, () %tuple.148, (s32[1]{0:T(128)}, ...), branch_computations={%region_16.17_spmd, %region_17.20_spmd.clone} | conditional | flops 602368 | bytes 401058368 | solution.py:775
  367.8 16.8 %filter_backward.1 = (bf16[768,768]{1,0:T(8,128)(2,1)S(1)}, bf16[768,768]{1,0:T(8,128)(2,1)}, bf16[768,768]{1,0:T(8,128)(2,1)}, bf16[768,768]{1,0:T(8,128)(2,1)}, f32[128,768]{1,0:T(8,128)}) custom-call(s32[1]{0:T(128)} %get-tuple-element.1154.first_ref, bf16[96,128,128]{2,1,0:T(8,128)(2,1)} %constant.132.clone.2.to_ref, ...), custom_call_target="tpu_custom_call" | custom-call | flops 1024 | bytes 400000000 | tf_op jit(solution)/shard_map/cond/branch_1_fun/filter_backward/pallas_call | solution.py:261
  387.2 36.2 %conditional.24 = (bf16[1,128]{1,0:T(2,128)(2,1)S(1)}, bf16[1296,128]{1,0:T(8,128)(2,1)}, bf16[1296,128]{1,0:T(8,128)(2,1)}, bf16[1296,128]{1,0:T(8,128)(2,1)}, bf16[1296,128]{1,0:T(8,128)(2,1)}) conditional(s32[]{:T(128)} %convert_element_type.11, () %tuple.177, (bf16[768,768]{1,0:T(8,128)(2,1)S(1)}, s32[1]{0:T(128)}, ...), branch_computations={%region_20.21_spmd, %region_21.22_spmd} | conditional | flops 1024 | bytes 403686464 | solution.py:775
  387.2 28.8 %all_to_all.58 = bf16[8,96,768]{2,1,0:T(8,128)(2,1)} all-to-all(bf16[8,96,768]{2,1,0:T(8,128)(2,1)S(1)} %bitcast.41), channel_id=1, replica_groups=mesh['lat'=8,'lon'=4] {'lat'}, dimensions={0} | all-to-all | bytes 2359296 | tf_op jit(solution)/shard_map/cond/branch_1_fun/back_spectra_0/all_to_all | solution.py:764
  434.1 28.3 %conditional.25 = (bf16[1,128]{1,0:T(2,128)(2,1)S(1)}, bf16[1296,128]{1,0:T(8,128)(2,1)}, bf16[1296,128]{1,0:T(8,128)(2,1)}, bf16[1296,128]{1,0:T(8,128)(2,1)}, bf16[1296,128]{1,0:T(8,128)(2,1)}) conditional(s32[]{:T(128)} %convert_element_type.11, () %tuple.180, (bf16[768,768]{1,0:T(8,128)(2,1)}, s32[1]{0:T(128)}, ...), branch_computations={%region_22.23_spmd, %region_23.24_spmd} | conditional | flops 1024 | bytes 402359328 | solution.py:775
  434.1 21.2 %all_to_all.59 = bf16[8,96,768]{2,1,0:T(8,128)(2,1)} all-to-all(bf16[8,96,768]{2,1,0:T(8,128)(2,1)} %bitcast.19), channel_id=1, replica_groups=mesh['lat'=8,'lon'=4] {'lat'}, dimensions={0} | all-to-all | bytes 2359296 | tf_op jit(solution)/shard_map/cond/branch_1_fun/back_spectra_1/all_to_all | solution.py:764
  467.0 28.0 %conditional.26 = (bf16[1,128]{1,0:T(2,128)(2,1)S(1)}, bf16[1296,128]{1,0:T(8,128)(2,1)}, bf16[1296,128]{1,0:T(8,128)(2,1)}, bf16[1296,128]{1,0:T(8,128)(2,1)}, bf16[1296,128]{1,0:T(8,128)(2,1)}) conditional(s32[]{:T(128)} %convert_element_type.11, () %tuple.182, (bf16[768,768]{1,0:T(8,128)(2,1)}, s32[1]{0:T(128)}, ...), branch_computations={%region_25.26_spmd, %region_26.27_spmd} | conditional | flops 1024 | bytes 403686464 | solution.py:775
  467.0 21.2 %all_to_all.60 = bf16[8,96,768]{2,1,0:T(8,128)(2,1)} all-to-all(bf16[8,96,768]{2,1,0:T(8,128)(2,1)} %bitcast.21), channel_id=1, replica_groups=mesh['lat'=8,'lon'=4] {'lat'}, dimensions={0} | all-to-all | bytes 2359296 | tf_op jit(solution)/shard_map/cond/branch_1_fun/back_spectra_2/all_to_all | solution.py:764
  501.3 28.6 %conditional.27 = (bf16[1,128]{1,0:T(2,128)(2,1)S(1)}, bf16[1296,128]{1,0:T(8,128)(2,1)S(1)}, bf16[1296,128]{1,0:T(8,128)(2,1)}, bf16[1296,128]{1,0:T(8,128)(2,1...) conditional(s32[]{:T(128)} %convert_element_type.11, () %tuple.147, ...), branch_computations={%region_27.28_spmd, %region_28.29_spmd} | conditional | flops 4096 | bytes 1609584768 | solution.py:775
  537.5 13.3 %collective-permute-start.34 = (bf16[1296,128]{1,0:T(8,128)(2,1)}, bf16[1296,128]{1,0:T(8,128)(2,1)S(1)}, u32[]{:S(2)}, u32[]{:S(2)}) collective-permute-start(bf16[1296,128]{1,0:T(8,128)(2,1)} %get-tuple-element.1096), channel_id=1, source_target_pairs={{0,2},{1,3},{2,0},{3,1},{4,6},{5,7},{6,4},{7,5},{8,10},{9,11},{10,... | collective-permute-start | bytes 995336 | tf_op jit(solution)/shard_map/input_grad_3/ppermute | solution.py:756
  552.8 16.4 %conditional.28 = (bf16[1,128]{1,0:T(2,128)(2,1)S(1)}, f32[24,768]{1,0:T(8,128)S(1)}, f32[4,16,64,641]{3,2,1,0:T(8,128)}) conditional(s32[]{:T(128)} %convert_element_type.11, () %tuple.188, (f32[192,768]{1,0:T(8,128)}, s32[1]{0:T(128)}, bf16[1296,128]{1,0:T(8,128)(2,1)}, bf16[1296,128]{1,0:T(8,128)(2,1)}, bf16[1296,128]{1,0:T(8,128)(2,1)}, ...), branch_computations={%region_30.31_spmd, %region_31.33_spmd} | conditional | flops 132096 | bytes 1203760128 | solution.py:775
  588.0 25.5 %conditional.29 = (f32[192,768]{1,0:T(8,128)}, f32[641,1282]{1,0:T(8,128)}, f32[641,1282]{1,0:T(8,128)}, f32[641]{0:T(1024)}, f32[1282]{0:T(1024)}, /*index=5*/f...) conditional(s32[]{:T(128)} %convert_element_type.11, () %tuple.193, ...), branch_computations={%region_33.34_spmd, %region_34.35_spmd} | conditional | flops 2048 | bytes 817602752 | solution.py:775
  597.1 7.5 %adafactor.2 = (f32[641,1282]{1,0:T(8,128)}, f32[641,1282]{1,0:T(8,128)}, f32[641]{0:T(1024)}, f32[1282]{0:T(1024)}) custom-call(bf16[1344,1408]{1,0:T(8,128)(2,1)} %get-tuple-element.657.grad_ref, f32[641,1282]{1,0:T(8,128)} %get-tuple-element.658.weight_ref, f32[641,1]{1,0:T(8,128)} %broadcast_in_dim.11.rows_ref, f32[1,1282]{1,0:T(1,128)} %broadcast_in_dim.2.columns_ref), custom_call_target="tpu_custom_call" | custom-call | flops 1024 | bytes 400000000 | tf_op jit(solution)/shard_map/cond/branch_1_fun/adafactor/pallas_call | solution.py:672
  606.1 7.4 %adafactor.3 = (f32[641,1282]{1,0:T(8,128)}, f32[641,1282]{1,0:T(8,128)}, f32[641]{0:T(1024)}, f32[1282]{0:T(1024)}) custom-call(bf16[1344,1408]{1,0:T(8,128)(2,1)S(1)} %copy-done.4, f32[641,1282]{1,0:T(8,128)} %bitcast.35, f32[641,1]{1,0:T(8,128)} %broadcast_in_dim.12.rows_ref, f32[1,1282]{1,0:T(1,128)} %broadcast_in_dim.10.columns_ref), custom_call_target="tpu_custom_call" | custom-call | flops 1024 | bytes 400000000 | tf_op jit(solution)/shard_map/cond/branch_1_fun/adafactor/pallas_call | solution.py:672
  (259 shorter events, 276.1 us)
Async XLA Ops:
  7.2 457.0 %reduce-scatter.4.cloned.1.call-start = ((), (), s32[]{:S(2)}) async-start(), calls=%async_computation.17 | async-start | bytes 8515584
  38.6 36.2 %collective-permute-start.3 = (bf16[1296,128]{1,0:T(8,128)(2,1)}, bf16[1296,128]{1,0:T(8,128)(2,1)}, u32[]{:S(2)}, u32[]{:S(2)}) collective-permute-start(bf16[1296,128]{1,0:T(8,128)(2,1)} %get-tuple-element.939), channel_id=1, source_target_pairs={{0,1},{1,2},{2,3},{3,0},{4,5},{5,6},{6,7},{7,4},{8,9},{9,10},{10,1... | collective-permute-start | bytes 995336 | tf_op jit(solution)/shard_map/fields_1/ppermute | solution.py:756
  105.0 30.8 %collective-permute-start.9 = (bf16[1296,128]{1,0:T(8,128)(2,1)}, bf16[1296,128]{1,0:T(8,128)(2,1)}, u32[]{:S(2)}, u32[]{:S(2)}) collective-permute-start(bf16[1296,128]{1,0:T(8,128)(2,1)} %get-tuple-element.978), channel_id=1, source_target_pairs={{0,1},{1,2},{2,3},{3,0},{4,5},{5,6},{6,7},{7,4},{8,9},{9,10},{10,1... | collective-permute-start | bytes 995336 | tf_op jit(solution)/shard_map/fields_3/ppermute | solution.py:756
  135.8 80.3 %collective-permute-start.12 = (bf16[2576,128]{1,0:T(8,128)(2,1)}, bf16[2576,128]{1,0:T(8,128)(2,1)}, u32[]{:S(2)}, u32[]{:S(2)}) collective-permute-start(bf16[2576,128]{1,0:T(8,128)(2,1)} %get-tuple-element.1016), channel_id=1, source_target_pairs={{0,1},{1,2},{2,3},{3,0},{4,5},{5,6},{6,7},{7,4},{8,9},{9,10},{10,1... | collective-permute-start | bytes 1978376 | tf_op jit(solution)/shard_map/upstream_0/ppermute | solution.py:756
  138.0 79.8 %collective-permute-start.13 = (bf16[2576,128]{1,0:T(8,128)(2,1)}, bf16[2576,128]{1,0:T(8,128)(2,1)}, u32[]{:S(2)}, u32[]{:S(2)}) collective-permute-start(bf16[2576,128]{1,0:T(8,128)(2,1)} %get-tuple-element.1017), channel_id=1, source_target_pairs={{0,2},{1,3},{2,0},{3,1},{4,6},{5,7},{6,4},{7,5},{8,10},{9,11},{10,... | collective-permute-start | bytes 1978376 | tf_op jit(solution)/shard_map/upstream_0/ppermute | solution.py:756
  140.3 77.5 %collective-permute-start.14 = (bf16[2576,128]{1,0:T(8,128)(2,1)}, bf16[2576,128]{1,0:T(8,128)(2,1)}, u32[]{:S(2)}, u32[]{:S(2)}) collective-permute-start(bf16[2576,128]{1,0:T(8,128)(2,1)} %get-tuple-element.1018), channel_id=1, source_target_pairs={{0,3},{1,0},{2,1},{3,2},{4,7},{5,4},{6,5},{7,6},{8,11},{9,8},{10,9... | collective-permute-start | bytes 1978376 | tf_op jit(solution)/shard_map/upstream_0/ppermute | solution.py:756
  166.5 107.1 %collective-permute-start.15 = (bf16[2576,128]{1,0:T(8,128)(2,1)}, bf16[2576,128]{1,0:T(8,128)(2,1)}, u32[]{:S(2)}, u32[]{:S(2)}) collective-permute-start(bf16[2576,128]{1,0:T(8,128)(2,1)} %get-tuple-element.1023), channel_id=1, source_target_pairs={{0,1},{1,2},{2,3},{3,0},{4,5},{5,6},{6,7},{7,4},{8,9},{9,10},{10,1... | collective-permute-start | bytes 1978376 | tf_op jit(solution)/shard_map/upstream_1/ppermute | solution.py:756
  168.4 105.2 %collective-permute-start.16 = (bf16[2576,128]{1,0:T(8,128)(2,1)}, bf16[2576,128]{1,0:T(8,128)(2,1)}, u32[]{:S(2)}, u32[]{:S(2)}) collective-permute-start(bf16[2576,128]{1,0:T(8,128)(2,1)} %get-tuple-element.1024), channel_id=1, source_target_pairs={{0,2},{1,3},{2,0},{3,1},{4,6},{5,7},{6,4},{7,5},{8,10},{9,11},{10,... | collective-permute-start | bytes 1978376 | tf_op jit(solution)/shard_map/upstream_1/ppermute | solution.py:756
  182.2 33.9 %all-to-all-start.4 = ((bf16[8,192,768]{2,1,0:T(8,128)(2,1)}), bf16[8,192,768]{2,1,0:T(8,128)(2,1)}, u32[]{:S(2)}, u32[]{:S(2)}) async-start(bf16[8,192,768]{2,1,0:T(8,128)(2,1)} %bitcast.46), calls=%async_computation.4 | async-start | bytes 4718592 | tf_op jit(solution)/shard_map/cond/branch_1_fun/synthesis_0/all_to_all | solution.py:764
  216.1 57.5 %collective-permute-start.17 = (bf16[2576,128]{1,0:T(8,128)(2,1)}, bf16[2576,128]{1,0:T(8,128)(2,1)}, u32[]{:S(2)}, u32[]{:S(2)}) collective-permute-start(bf16[2576,128]{1,0:T(8,128)(2,1)} %get-tuple-element.1025), channel_id=1, source_target_pairs={{0,3},{1,0},{2,1},{3,2},{4,7},{5,4},{6,5},{7,6},{8,11},{9,8},{10,9... | collective-permute-start | bytes 1978376 | tf_op jit(solution)/shard_map/upstream_1/ppermute | solution.py:756
  217.9 46.2 %all-to-all-start.5 = ((bf16[8,192,768]{2,1,0:T(8,128)(2,1)}), bf16[8,192,768]{2,1,0:T(8,128)(2,1)}, u32[]{:S(2)}, u32[]{:S(2)}) async-start(bf16[8,192,768]{2,1,0:T(8,128)(2,1)} %bitcast.11), calls=%async_computation.5 | async-start | bytes 4718592 | tf_op jit(solution)/shard_map/cond/branch_1_fun/synthesis_1/all_to_all | solution.py:764
  264.1 89.8 %collective-permute-start.18 = (bf16[2576,128]{1,0:T(8,128)(2,1)}, bf16[2576,128]{1,0:T(8,128)(2,1)}, u32[]{:S(2)}, u32[]{:S(2)}) collective-permute-start(bf16[2576,128]{1,0:T(8,128)(2,1)} %get-tuple-element.1043), channel_id=1, source_target_pairs={{0,3},{1,0},{2,1},{3,2},{4,7},{5,4},{6,5},{7,6},{8,11},{9,8},{10,9... | collective-permute-start | bytes 1978376 | tf_op jit(solution)/shard_map/output_0_0/ppermute | solution.py:756
  266.2 87.7 %collective-permute-start.19 = (bf16[2576,128]{1,0:T(8,128)(2,1)}, bf16[2576,128]{1,0:T(8,128)(2,1)}, u32[]{:S(2)}, u32[]{:S(2)}) collective-permute-start(bf16[2576,128]{1,0:T(8,128)(2,1)} %get-tuple-element.1044), channel_id=1, source_target_pairs={{0,2},{1,3},{2,0},{3,1},{4,6},{5,7},{6,4},{7,5},{8,10},{9,11},{10,... | collective-permute-start | bytes 1978376 | tf_op jit(solution)/shard_map/output_0_0/ppermute | solution.py:756
  273.6 80.3 %collective-permute-start.20 = (bf16[2576,128]{1,0:T(8,128)(2,1)}, bf16[2576,128]{1,0:T(8,128)(2,1)}, u32[]{:S(2)}, u32[]{:S(2)}) collective-permute-start(bf16[2576,128]{1,0:T(8,128)(2,1)} %get-tuple-element.1045), channel_id=1, source_target_pairs={{0,1},{1,2},{2,3},{3,0},{4,5},{5,6},{6,7},{7,4},{8,9},{9,10},{10,1... | collective-permute-start | bytes 1978376 | tf_op jit(solution)/shard_map/output_0_0/ppermute | solution.py:756
  273.6 46.2 %all-to-all-start.6 = ((bf16[8,192,768]{2,1,0:T(8,128)(2,1)}), bf16[8,192,768]{2,1,0:T(8,128)(2,1)}, u32[]{:S(2)}, u32[]{:S(2)}) async-start(bf16[8,192,768]{2,1,0:T(8,128)(2,1)} %bitcast.13), calls=%async_computation.6 | async-start | bytes 4718592 | tf_op jit(solution)/shard_map/cond/branch_1_fun/back_synthesis_0/all_to_all | solution.py:764
  319.8 34.0 %all-to-all-start.7 = ((bf16[8,192,768]{2,1,0:T(8,128)(2,1)}), bf16[8,192,768]{2,1,0:T(8,128)(2,1)}, u32[]{:S(2)}, u32[]{:S(2)}) async-start(bf16[8,192,768]{2,1,0:T(8,128)(2,1)} %bitcast.15), calls=%async_computation.7 | async-start | bytes 4718592 | tf_op jit(solution)/shard_map/cond/branch_1_fun/back_synthesis_1/all_to_all | solution.py:764
  353.9 183.5 %all-reduce.8.cloned.1.call-start = ((), (), s32[]{:S(2)}) async-start(), calls=%async_computation.15 | async-start | bytes 946176 | tf_op jit(solution)/shard_map/weights_lon/psum | solution.py:961
  358.5 73.6 %collective-permute-start.24 = (bf16[1296,128]{1,0:T(8,128)(2,1)}, bf16[1296,128]{1,0:T(8,128)(2,1)}, u32[]{:S(2)}, u32[]{:S(2)}) collective-permute-start(bf16[1296,128]{1,0:T(8,128)(2,1)} %get-tuple-element.1065), channel_id=1, source_target_pairs={{0,3},{1,0},{2,1},{3,2},{4,7},{5,4},{6,5},{7,6},{8,11},{9,8},{10,9... | collective-permute-start | bytes 995336 | tf_op jit(solution)/shard_map/output_1_1/ppermute | solution.py:756
  361.6 72.4 %collective-permute-start.25 = (bf16[1296,128]{1,0:T(8,128)(2,1)}, bf16[1296,128]{1,0:T(8,128)(2,1)}, u32[]{:S(2)}, u32[]{:S(2)}) collective-permute-start(bf16[1296,128]{1,0:T(8,128)(2,1)} %get-tuple-element.1066), channel_id=1, source_target_pairs={{0,2},{1,3},{2,0},{3,1},{4,6},{5,7},{6,4},{7,5},{8,10},{9,11},{10,... | collective-permute-start | bytes 995336 | tf_op jit(solution)/shard_map/output_1_1/ppermute | solution.py:756
  367.1 66.9 %collective-permute-start.26 = (bf16[1296,128]{1,0:T(8,128)(2,1)}, bf16[1296,128]{1,0:T(8,128)(2,1)}, u32[]{:S(2)}, u32[]{:S(2)}) collective-permute-start(bf16[1296,128]{1,0:T(8,128)(2,1)} %get-tuple-element.1067), channel_id=1, source_target_pairs={{0,1},{1,2},{2,3},{3,0},{4,5},{5,6},{6,7},{7,4},{8,9},{9,10},{10,1... | collective-permute-start | bytes 995336 | tf_op jit(solution)/shard_map/output_1_1/ppermute | solution.py:756
  423.4 43.0 %collective-permute-start.30 = (bf16[1296,128]{1,0:T(8,128)(2,1)}, bf16[1296,128]{1,0:T(8,128)(2,1)}, u32[]{:S(2)}, u32[]{:S(2)}) collective-permute-start(bf16[1296,128]{1,0:T(8,128)(2,1)} %get-tuple-element.1084), channel_id=1, source_target_pairs={{0,3},{1,0},{2,1},{3,2},{4,7},{5,4},{6,5},{7,6},{8,11},{9,8},{10,9... | collective-permute-start | bytes 995336 | tf_op jit(solution)/shard_map/input_grad_0/ppermute | solution.py:756
  426.8 40.2 %collective-permute-start.31 = (bf16[1296,128]{1,0:T(8,128)(2,1)}, bf16[1296,128]{1,0:T(8,128)(2,1)}, u32[]{:S(2)}, u32[]{:S(2)}) collective-permute-start(bf16[1296,128]{1,0:T(8,128)(2,1)} %get-tuple-element.1085), channel_id=1, source_target_pairs={{0,2},{1,3},{2,0},{3,1},{4,6},{5,7},{6,4},{7,5},{8,10},{9,11},{10,... | collective-permute-start | bytes 995336 | tf_op jit(solution)/shard_map/input_grad_0/ppermute | solution.py:756
  432.0 34.9 %collective-permute-start.32 = (bf16[1296,128]{1,0:T(8,128)(2,1)}, bf16[1296,128]{1,0:T(8,128)(2,1)}, u32[]{:S(2)}, u32[]{:S(2)}) collective-permute-start(bf16[1296,128]{1,0:T(8,128)(2,1)} %get-tuple-element.1086), channel_id=1, source_target_pairs={{0,1},{1,2},{2,3},{3,0},{4,5},{5,6},{6,7},{7,4},{8,9},{9,10},{10,1... | collective-permute-start | bytes 995336 | tf_op jit(solution)/shard_map/input_grad_0/ppermute | solution.py:756
  462.4 37.0 %collective-permute-start.27 = (bf16[1296,128]{1,0:T(8,128)(2,1)}, bf16[1296,128]{1,0:T(8,128)(2,1)}, u32[]{:S(2)}, u32[]{:S(2)}) collective-permute-start(bf16[1296,128]{1,0:T(8,128)(2,1)} %get-tuple-element.1079), channel_id=1, source_target_pairs={{0,3},{1,0},{2,1},{3,2},{4,7},{5,4},{6,5},{7,6},{8,11},{9,8},{10,9... | collective-permute-start | bytes 995336 | tf_op jit(solution)/shard_map/input_grad_1/ppermute | solution.py:756
  466.2 121.8 %all-gather.2.cloned.1.call-start = ((), (), s32[]{:S(2)}) async-start(), calls=%async_computation.16 | async-start | bytes 4257792 | tf_op jit(solution)/shard_map/weights_lat/all_gather | solution.py:1009
  466.3 35.0 %collective-permute-start.28 = (bf16[1296,128]{1,0:T(8,128)(2,1)}, bf16[1296,128]{1,0:T(8,128)(2,1)}, u32[]{:S(2)}, u32[]{:S(2)}) collective-permute-start(bf16[1296,128]{1,0:T(8,128)(2,1)} %get-tuple-element.1080), channel_id=1, source_target_pairs={{0,2},{1,3},{2,0},{3,1},{4,6},{5,7},{6,4},{7,5},{8,10},{9,11},{10,... | collective-permute-start | bytes 995336 | tf_op jit(solution)/shard_map/input_grad_1/ppermute | solution.py:756
  466.4 34.9 %collective-permute-start.29 = (bf16[1296,128]{1,0:T(8,128)(2,1)}, bf16[1296,128]{1,0:T(8,128)(2,1)}, u32[]{:S(2)}, u32[]{:S(2)}) collective-permute-start(bf16[1296,128]{1,0:T(8,128)(2,1)} %get-tuple-element.1081), channel_id=1, source_target_pairs={{0,1},{1,2},{2,3},{3,0},{4,5},{5,6},{6,7},{7,4},{8,9},{9,10},{10,1... | collective-permute-start | bytes 995336 | tf_op jit(solution)/shard_map/input_grad_1/ppermute | solution.py:756
  495.0 34.9 %collective-permute-start.36 = (bf16[1296,128]{1,0:T(8,128)(2,1)}, bf16[1296,128]{1,0:T(8,128)(2,1)}, u32[]{:S(2)}, u32[]{:S(2)}) collective-permute-start(bf16[1296,128]{1,0:T(8,128)(2,1)} %get-tuple-element.1109), channel_id=1, source_target_pairs={{0,3},{1,0},{2,1},{3,2},{4,7},{5,4},{6,5},{7,6},{8,11},{9,8},{10,9... | collective-permute-start | bytes 995336 | tf_op jit(solution)/shard_map/input_grad_2/ppermute | solution.py:756
  498.3 38.6 %collective-permute-start.37 = (bf16[1296,128]{1,0:T(8,128)(2,1)}, bf16[1296,128]{1,0:T(8,128)(2,1)}, u32[]{:S(2)}, u32[]{:S(2)}) collective-permute-start(bf16[1296,128]{1,0:T(8,128)(2,1)} %get-tuple-element.1110), channel_id=1, source_target_pairs={{0,2},{1,3},{2,0},{3,1},{4,6},{5,7},{6,4},{7,5},{8,10},{9,11},{10,... | collective-permute-start | bytes 995336 | tf_op jit(solution)/shard_map/input_grad_2/ppermute | solution.py:756
  499.4 37.5 %collective-permute-start.38 = (bf16[1296,128]{1,0:T(8,128)(2,1)}, bf16[1296,128]{1,0:T(8,128)(2,1)}, u32[]{:S(2)}, u32[]{:S(2)}) collective-permute-start(bf16[1296,128]{1,0:T(8,128)(2,1)} %get-tuple-element.1111), channel_id=1, source_target_pairs={{0,1},{1,2},{2,3},{3,0},{4,5},{5,6},{6,7},{7,4},{8,9},{9,10},{10,1... | collective-permute-start | bytes 995336 | tf_op jit(solution)/shard_map/input_grad_2/ppermute | solution.py:756
  537.5 43.7 %collective-permute-start.33 = (bf16[1296,128]{1,0:T(8,128)(2,1)}, bf16[1296,128]{1,0:T(8,128)(2,1)S(1)}, u32[]{:S(2)}, u32[]{:S(2)}) collective-permute-start(bf16[1296,128]{1,0:T(8,128)(2,1)} %get-tuple-element.1095), channel_id=1, source_target_pairs={{0,3},{1,0},{2,1},{3,2},{4,7},{5,4},{6,5},{7,6},{8,11},{9,8},{10,9... | collective-permute-start | bytes 995336 | tf_op jit(solution)/shard_map/input_grad_3/ppermute | solution.py:756
  537.5 43.6 %collective-permute-start.34 = (bf16[1296,128]{1,0:T(8,128)(2,1)}, bf16[1296,128]{1,0:T(8,128)(2,1)S(1)}, u32[]{:S(2)}, u32[]{:S(2)}) collective-permute-start(bf16[1296,128]{1,0:T(8,128)(2,1)} %get-tuple-element.1096), channel_id=1, source_target_pairs={{0,2},{1,3},{2,0},{3,1},{4,6},{5,7},{6,4},{7,5},{8,10},{9,11},{10,... | collective-permute-start | bytes 995336 | tf_op jit(solution)/shard_map/input_grad_3/ppermute | solution.py:756
  (69 other events, 1239.0 us)
Sparse Core Ops, SparseCore 0:
  354.0 79.6 reduce-scatter.3
  466.4 71.0 all-reduce.7
  539.4 48.5 all-gather.1
